TPU v7x, 512 devices: a whole 4x8x8 slice. The times are simulated.
512 devices in a mesh: row: 16 (over x, y_lo), col: 16 (over z, y_hi), layer: 2 (over core).
Axes of the slice: x: 4, y: 8 (y_hi: 2, y_lo: 4; y = y_hi * 4 + y_lo), z: 8, core: 2. Of those that a mesh axis runs over, the one named last changes fastest.
Arguments:
- ham_blocks: bfloat16 [1472, 11776], P('row', 'col'), may hold values from -0.15625 to 0.15625
- ham_index: int32 [2, 16, 128], P(None, 'row', 'col'), may hold values from 0 to 3
- ham_count: int32 [16, 16], P('row', 'col'), may hold values from 1 to 8, as said below
- dens_blocks: bfloat16 [1472, 11776], P('row', 'col'), may hold values from -6 to 6
- dens_index: int32 [2, 16, 128], P(None, 'row', 'col'), may hold values from 0 to 3
- dens_count: int32 [16, 16], P('row', 'col'), may hold values from 1 to 8, as said below
- first_index: int32 [2, 16, 128], P(None, 'row', 'col'), may hold values from 0 to 3
- first_count: int32 [16, 16], P('row', 'col'), may hold values from 1 to 8, as said below
- second_index: int32 [2, 16, 128], P(None, 'row', 'col'), may hold values from 0 to 3
- second_count: int32 [16, 16], P('row', 'col'), may hold values from 1 to 8, as said below
- third_index: int32 [2, 16, 128], P(None, 'row', 'col'), may hold values from 0 to 3
- third_count: int32 [16, 16], P('row', 'col'), may hold values from 1 to 8, as said below
Outputs:
- real_part: float32 [5888, 5888], P('row', 'col')
- imag_part: float32 [5888, 5888], P('row', 'col')
Inputs may be any that keep to these rules, and one draw needn't show every extreme that they name: `ham_count`: in each tile the used slots name distinct blocks; in every draw some tile uses all 8 slots. `dens_count`: in each tile the used slots name distinct blocks; in every draw some tile uses all 8 slots. `first_count`: in each tile the used slots name distinct blocks; in every draw some tile uses all 8 slots. `second_count`: in each tile the used slots name distinct blocks; in every draw some tile uses all 8 slots. `third_count`: in each tile the used slots name distinct blocks; in every draw some tile uses all 8 slots.
All inputs are finite; a program needn't handle non-finite values.
Results may differ from a plain program's by a relative error of at most 0.0003.
Values may be sent and summed in bfloat16 or wider, within the bound.
No kernel may reach another device: no remote copies, remote signals or barrier semaphores. Data moves between devices by JAX's collectives and lax.ppermute only.
A program may use at most 64 MiB of HBM per device.

v0:
```python
import jax
import jax.numpy as jnp
from jax import lax
from jax.sharding import PartitionSpec as P

BT = 4


def shifted(block, axis, distance):
    devices = range(lax.axis_size(axis))
    route = [((i - distance) % len(devices), i) for i in devices]
    return lax.ppermute(block, axis, route)


def selector(indices, counts):
    capacity = indices.shape[2]
    in_use = jnp.arange(capacity) < counts[0, 0]
    positions = jnp.arange(BT)
    row_pick = (indices[0, 0][None, :] == positions[:, None]) & in_use[None, :]
    col_pick = (indices[1, 0][None, :] == positions[:, None]) & in_use[None, :]
    return (row_pick[:, None, :] & col_pick[None, :, :]).astype(jnp.bfloat16)


def densify(stacked, indices, counts):
    block_size = stacked.shape[0]
    capacity = indices.shape[2]
    chosen = selector(indices, counts)
    blocks = stacked.reshape(block_size, capacity, block_size)
    tile = jnp.einsum("ijs,asb->iajb", chosen, blocks, preferred_element_type=jnp.float32)
    return tile.reshape(BT * block_size, BT * block_size).astype(jnp.bfloat16)


def tile_mask(indices, counts, block_size):
    coarse = selector(indices, counts).astype(jnp.float32).sum(axis=2)
    return jnp.repeat(jnp.repeat(coarse, block_size, axis=0), block_size, axis=1)


def finish_term(total_sum, indices, counts):
    block_size = total_sum.shape[0] // BT
    return tile_mask(indices, counts, block_size) * lax.psum(total_sum, "layer")


def per_device(
    ham_blocks,
    ham_index,
    ham_count,
    dens_blocks,
    dens_index,
    dens_count,
    first_index,
    first_count,
    second_index,
    second_count,
    third_index,
    third_count,
):
    block_size = ham_blocks.shape[0]
    capacity = ham_index.shape[2]
    row_total = lax.axis_size("row")
    row_here = lax.axis_index("row")
    layer_here = lax.axis_index("layer")
    panel, panel_index, panel_count = (
        lax.all_gather(ham_blocks, "col", axis=1, tiled=True),
        lax.all_gather(ham_index, "col", axis=2, tiled=True),
        lax.all_gather(ham_count, "col", axis=1, tiled=True),
    )

    def ham_tile(which):
        stacked = lax.dynamic_slice_in_dim(
            panel, which * capacity * block_size, capacity * block_size, 1
        )
        indices = lax.dynamic_slice_in_dim(panel_index, which * capacity, capacity, 2)
        counts = lax.dynamic_slice_in_dim(panel_count, which, 1, 1)
        return densify(stacked, indices, counts)

    def source_row(step):
        return jnp.mod(row_here - layer_here - 2 * step, row_total)

    turns = row_total // 2
    side = BT * block_size

    def product_dense(right):
        moved = shifted(right, "row", 1)
        carried = jnp.where(layer_here == 1, moved, right)

        def advance(step, state):
            total_sum, current = state
            total_sum = total_sum + jnp.dot(
                ham_tile(source_row(step)), current, preferred_element_type=jnp.float32
            )
            current = shifted(current, "row", 2)
            return (total_sum, current)

        start_sum = jnp.zeros((side, side), jnp.float32)
        total_sum, current = lax.fori_loop(0, turns - 1, advance, (start_sum, carried))
        return total_sum + jnp.dot(
            ham_tile(source_row(turns - 1)), current, preferred_element_type=jnp.float32
        )

    dens_tile = densify(dens_blocks, dens_index, dens_count)
    first_term = finish_term(product_dense(dens_tile), first_index, first_count)
    first_round = first_term.astype(jnp.bfloat16)
    second_term = finish_term(product_dense(first_round), second_index, second_count)
    second_round = second_term.astype(jnp.bfloat16)
    third_term = finish_term(product_dense(second_round), third_index, third_count)
    real_part = dens_tile.astype(jnp.float32) - 0.5 * second_term
    imag_part = third_term / 6.0 - first_term
    return (real_part, imag_part)


def solution(mesh):
    in_specs = (
        P("row", "col"),
        P(None, "row", "col"),
        P("row", "col"),
        P("row", "col"),
        P(None, "row", "col"),
        P("row", "col"),
        P(None, "row", "col"),
        P("row", "col"),
        P(None, "row", "col"),
        P("row", "col"),
        P(None, "row", "col"),
        P("row", "col"),
    )
    out_specs = (P("row", "col"), P("row", "col"))
    return jax.shard_map(
        per_device, mesh=mesh, in_specs=in_specs, out_specs=out_specs, check_vma=False
    )
```

profile of v0, /device:TPU:1, one launch (start us, length us, event | category | flops | bytes accessed | tf_op | source)
XLA Modules:
  0.0 626.6 jit_solution(10951874973060506571)
XLA Ops:
  11.0 4.0 collective-permute-start.3
  18.3 23.4 %all-reduce = s32[16]{0:T(128)S(1)} all-reduce(s32[16]{0:T(128)S(1)} %bitcast_dynamic-update-slice_fusion), channel_id=1, replica_groups=mesh['row'=16,'col'=16,'layer'=2] {'col'}, use_global_device_ids=true, to_apply=%add | all-reduce | flops 16 | bytes 128
  43.7 43.8 %all_gather.10 = s32[2,1,128]{0,1,2:T(1,128)S(1)} all-gather(s32[2,1,8]{0,1,2:T(1,128)S(1)} %copy.52), channel_id=1, replica_groups=mesh['row'=16,'col'=16,'layer'=2] {'col'}, dimensions={2}, use_global_device_ids=true | all-gather | bytes 1088 | tf_op jit(solution)/shard_map/all_gather | solution.py:64
  88.1 35.1 %all-gather.3.cloned.1.call-done = bf16[16,736,92]{1,2,0:T(8,128)(2,1)} async-done(((bf16[1,736,92]{1,2,0:T(8,128)(2,1)}), bf16[16,736,92]{1,2,0:T(8,128)(2,1)}) %all-gather.3.cloned.1.call-update) | async-done | bytes 2166800 | tf_op jit(solution)/shard_map/all_gather | solution.py:63
  123.2 2.9 copy.51
  126.1 5.3 reshape.753
  133.4 119.0 %while.54 = (s32[]{:T(128)}, f32[368,368]{1,0:T(8,128)S(1)}, bf16[368,368]{1,0:T(8,128)(2,1)S(1)}, s32[]{:T(128)}, bf16[92,11776]{1,0:T(8,128)(2,1)}, /*index=5*...) while((s32[]{:T(128)}, f32[368,368]{1,0:T(8,128)S(1)}, ...), condition=%wide.region_3.4_spmd.clone, body=%wide.region_2.3_spmd.clone.sunk | while | flops 102245408 | bytes 5282378 | solution.py:95
  133.4 2.2 collective-permute-start
  139.5 12.1 %collective-permute-done = bf16[368,368]{1,0:T(8,128)(2,1)S(1)} collective-permute-done((bf16[368,368]{1,0:T(8,128)(2,1)S(1)}, bf16[368,368]{1,0:T(8,128)(2,1)S(1)}, u32[]{:S(2)}, u32[]{:S(2)}) %collective-permute-start) | collective-permute-done | bytes 270880 | tf_op jit(solution)/shard_map/while/body/eval_jaxpr/ppermute | solution.py:12
  157.4 9.9 %collective-permute-done = bf16[368,368]{1,0:T(8,128)(2,1)S(1)} collective-permute-done((bf16[368,368]{1,0:T(8,128)(2,1)S(1)}, bf16[368,368]{1,0:T(8,128)(2,1)S(1)}, u32[]{:S(2)}, u32[]{:S(2)}) %collective-permute-start) | collective-permute-done | bytes 270880 | tf_op jit(solution)/shard_map/while/body/eval_jaxpr/ppermute | solution.py:12
  167.3 1.9 collective-permute-start
  173.1 11.3 %collective-permute-done = bf16[368,368]{1,0:T(8,128)(2,1)S(1)} collective-permute-done((bf16[368,368]{1,0:T(8,128)(2,1)S(1)}, bf16[368,368]{1,0:T(8,128)(2,1)S(1)}, u32[]{:S(2)}, u32[]{:S(2)}) %collective-permute-start) | collective-permute-done | bytes 270880 | tf_op jit(solution)/shard_map/while/body/eval_jaxpr/ppermute | solution.py:12
  184.4 1.9 collective-permute-start
  190.1 11.3 %collective-permute-done = bf16[368,368]{1,0:T(8,128)(2,1)S(1)} collective-permute-done((bf16[368,368]{1,0:T(8,128)(2,1)S(1)}, bf16[368,368]{1,0:T(8,128)(2,1)S(1)}, u32[]{:S(2)}, u32[]{:S(2)}) %collective-permute-start) | collective-permute-done | bytes 270880 | tf_op jit(solution)/shard_map/while/body/eval_jaxpr/ppermute | solution.py:12
  207.3 11.3 %collective-permute-done = bf16[368,368]{1,0:T(8,128)(2,1)S(1)} collective-permute-done((bf16[368,368]{1,0:T(8,128)(2,1)S(1)}, bf16[368,368]{1,0:T(8,128)(2,1)S(1)}, u32[]{:S(2)}, u32[]{:S(2)}) %collective-permute-start) | collective-permute-done | bytes 270880 | tf_op jit(solution)/shard_map/while/body/eval_jaxpr/ppermute | solution.py:12
  224.3 11.0 %collective-permute-done = bf16[368,368]{1,0:T(8,128)(2,1)S(1)} collective-permute-done((bf16[368,368]{1,0:T(8,128)(2,1)S(1)}, bf16[368,368]{1,0:T(8,128)(2,1)S(1)}, u32[]{:S(2)}, u32[]{:S(2)}) %collective-permute-start) | collective-permute-done | bytes 270880 | tf_op jit(solution)/shard_map/while/body/eval_jaxpr/ppermute | solution.py:12
  235.3 1.9 collective-permute-start
  241.1 11.3 %collective-permute-done = bf16[368,368]{1,0:T(8,128)(2,1)S(1)} collective-permute-done((bf16[368,368]{1,0:T(8,128)(2,1)S(1)}, bf16[368,368]{1,0:T(8,128)(2,1)S(1)}, u32[]{:S(2)}, u32[]{:S(2)}) %collective-permute-start) | collective-permute-done | bytes 270880 | tf_op jit(solution)/shard_map/while/body/eval_jaxpr/ppermute | solution.py:12
  254.4 29.2 %all-reduce.5.cloned.1.call-done = f32[368,368]{1,0:T(8,128)} async-done(((f32[368,368]{1,0:T(8,128)}), f32[368,368]{1,0:T(8,128)}) %all-reduce.5.cloned.1.call-update) | async-done | bytes 541712 | tf_op jit(solution)/shard_map/psum | solution.py:40
  283.6 1.9 fusion.51
  285.5 2.1 collective-permute-start.4
  288.3 11.1 %collective-permute-done.4 = bf16[368,368]{1,0:T(8,128)(2,1)S(1)} collective-permute-done((bf16[368,368]{1,0:T(8,128)(2,1)S(1)}, bf16[368,368]{1,0:T(8,128)(2,1)S(1)}, u32[]{:S(2)}, u32[]{:S(2)}) %collective-permute-start.4) | collective-permute-done | bytes 270880 | tf_op jit(solution)/shard_map/ppermute | solution.py:12
  299.5 117.4 %while.55 = (s32[]{:T(128)}, f32[368,368]{1,0:T(8,128)S(1)}, bf16[368,368]{1,0:T(8,128)(2,1)S(1)}, s32[]{:T(128)}, bf16[92,11776]{1,0:T(8,128)(2,1)}, /*index=5*...) while((s32[]{:T(128)}, f32[368,368]{1,0:T(8,128)S(1)}, ...), condition=%wide.region_6.7_spmd.clone, body=%wide.region_5.6_spmd.clone.sunk | while | flops 102245408 | bytes 5282378 | solution.py:95
  299.5 1.9 collective-permute-start.1
  305.3 9.9 %collective-permute-done.1 = bf16[368,368]{1,0:T(8,128)(2,1)S(1)} collective-permute-done((bf16[368,368]{1,0:T(8,128)(2,1)S(1)}, bf16[368,368]{1,0:T(8,128)(2,1)S(1)}, u32[]{:S(2)}, u32[]{:S(2)}) %collective-permute-start.1) | collective-permute-done | bytes 270880 | tf_op jit(solution)/shard_map/while/body/eval_jaxpr/ppermute | solution.py:12
  315.2 1.9 collective-permute-start.1
  321.0 10.9 %collective-permute-done.1 = bf16[368,368]{1,0:T(8,128)(2,1)S(1)} collective-permute-done((bf16[368,368]{1,0:T(8,128)(2,1)S(1)}, bf16[368,368]{1,0:T(8,128)(2,1)S(1)}, u32[]{:S(2)}, u32[]{:S(2)}) %collective-permute-start.1) | collective-permute-done | bytes 270880 | tf_op jit(solution)/shard_map/while/body/eval_jaxpr/ppermute | solution.py:12
  337.7 11.4 %collective-permute-done.1 = bf16[368,368]{1,0:T(8,128)(2,1)S(1)} collective-permute-done((bf16[368,368]{1,0:T(8,128)(2,1)S(1)}, bf16[368,368]{1,0:T(8,128)(2,1)S(1)}, u32[]{:S(2)}, u32[]{:S(2)}) %collective-permute-start.1) | collective-permute-done | bytes 270880 | tf_op jit(solution)/shard_map/while/body/eval_jaxpr/ppermute | solution.py:12
  354.9 11.0 %collective-permute-done.1 = bf16[368,368]{1,0:T(8,128)(2,1)S(1)} collective-permute-done((bf16[368,368]{1,0:T(8,128)(2,1)S(1)}, bf16[368,368]{1,0:T(8,128)(2,1)S(1)}, u32[]{:S(2)}, u32[]{:S(2)}) %collective-permute-start.1) | collective-permute-done | bytes 270880 | tf_op jit(solution)/shard_map/while/body/eval_jaxpr/ppermute | solution.py:12
  365.9 1.9 collective-permute-start.1
  371.6 11.4 %collective-permute-done.1 = bf16[368,368]{1,0:T(8,128)(2,1)S(1)} collective-permute-done((bf16[368,368]{1,0:T(8,128)(2,1)S(1)}, bf16[368,368]{1,0:T(8,128)(2,1)S(1)}, u32[]{:S(2)}, u32[]{:S(2)}) %collective-permute-start.1) | collective-permute-done | bytes 270880 | tf_op jit(solution)/shard_map/while/body/eval_jaxpr/ppermute | solution.py:12
  388.8 10.9 %collective-permute-done.1 = bf16[368,368]{1,0:T(8,128)(2,1)S(1)} collective-permute-done((bf16[368,368]{1,0:T(8,128)(2,1)S(1)}, bf16[368,368]{1,0:T(8,128)(2,1)S(1)}, u32[]{:S(2)}, u32[]{:S(2)}) %collective-permute-start.1) | collective-permute-done | bytes 270880 | tf_op jit(solution)/shard_map/while/body/eval_jaxpr/ppermute | solution.py:12
  405.5 11.4 %collective-permute-done.1 = bf16[368,368]{1,0:T(8,128)(2,1)S(1)} collective-permute-done((bf16[368,368]{1,0:T(8,128)(2,1)S(1)}, bf16[368,368]{1,0:T(8,128)(2,1)S(1)}, u32[]{:S(2)}, u32[]{:S(2)}) %collective-permute-start.1) | collective-permute-done | bytes 270880 | tf_op jit(solution)/shard_map/while/body/eval_jaxpr/ppermute | solution.py:12
  419.1 31.8 %all-reduce.7.cloned.1.call-done = f32[368,368]{1,0:T(8,128)} async-done(((f32[368,368]{1,0:T(8,128)}), f32[368,368]{1,0:T(8,128)}) %all-reduce.7.cloned.1.call-update) | async-done | bytes 541712 | tf_op jit(solution)/shard_map/psum | solution.py:40
  450.8 2.0 multiply_convert_fusion
  452.8 2.1 collective-permute-start.5
  455.6 11.1 %collective-permute-done.5 = bf16[368,368]{1,0:T(8,128)(2,1)S(1)} collective-permute-done((bf16[368,368]{1,0:T(8,128)(2,1)S(1)}, bf16[368,368]{1,0:T(8,128)(2,1)S(1)}, u32[]{:S(2)}, u32[]{:S(2)}) %collective-permute-start.5) | collective-permute-done | bytes 270880 | tf_op jit(solution)/shard_map/ppermute | solution.py:12
  466.8 117.4 %while.56 = (s32[]{:T(128)}, f32[368,368]{1,0:T(8,128)S(1)}, bf16[368,368]{1,0:T(8,128)(2,1)S(1)}, s32[]{:T(128)}, bf16[92,11776]{1,0:T(8,128)(2,1)}, /*index=5*...) while((s32[]{:T(128)}, f32[368,368]{1,0:T(8,128)S(1)}, ...), condition=%wide.region_10.11_spmd.clone, body=%wide.region_9.10_spmd.clone.sunk | while | flops 102245408 | bytes 5282378 | solution.py:95
  466.8 1.9 collective-permute-start.2
  472.6 9.9 %collective-permute-done.2 = bf16[368,368]{1,0:T(8,128)(2,1)S(1)} collective-permute-done((bf16[368,368]{1,0:T(8,128)(2,1)S(1)}, bf16[368,368]{1,0:T(8,128)(2,1)S(1)}, u32[]{:S(2)}, u32[]{:S(2)}) %collective-permute-start.2) | collective-permute-done | bytes 270880 | tf_op jit(solution)/shard_map/while/body/eval_jaxpr/ppermute | solution.py:12
  488.2 10.9 %collective-permute-done.2 = bf16[368,368]{1,0:T(8,128)(2,1)S(1)} collective-permute-done((bf16[368,368]{1,0:T(8,128)(2,1)S(1)}, bf16[368,368]{1,0:T(8,128)(2,1)S(1)}, u32[]{:S(2)}, u32[]{:S(2)}) %collective-permute-start.2) | collective-permute-done | bytes 270880 | tf_op jit(solution)/shard_map/while/body/eval_jaxpr/ppermute | solution.py:12
  505.0 11.4 %collective-permute-done.2 = bf16[368,368]{1,0:T(8,128)(2,1)S(1)} collective-permute-done((bf16[368,368]{1,0:T(8,128)(2,1)S(1)}, bf16[368,368]{1,0:T(8,128)(2,1)S(1)}, u32[]{:S(2)}, u32[]{:S(2)}) %collective-permute-start.2) | collective-permute-done | bytes 270880 | tf_op jit(solution)/shard_map/while/body/eval_jaxpr/ppermute | solution.py:12
  522.1 11.0 %collective-permute-done.2 = bf16[368,368]{1,0:T(8,128)(2,1)S(1)} collective-permute-done((bf16[368,368]{1,0:T(8,128)(2,1)S(1)}, bf16[368,368]{1,0:T(8,128)(2,1)S(1)}, u32[]{:S(2)}, u32[]{:S(2)}) %collective-permute-start.2) | collective-permute-done | bytes 270880 | tf_op jit(solution)/shard_map/while/body/eval_jaxpr/ppermute | solution.py:12
  538.9 11.4 %collective-permute-done.2 = bf16[368,368]{1,0:T(8,128)(2,1)S(1)} collective-permute-done((bf16[368,368]{1,0:T(8,128)(2,1)S(1)}, bf16[368,368]{1,0:T(8,128)(2,1)S(1)}, u32[]{:S(2)}, u32[]{:S(2)}) %collective-permute-start.2) | collective-permute-done | bytes 270880 | tf_op jit(solution)/shard_map/while/body/eval_jaxpr/ppermute | solution.py:12
  556.1 10.9 %collective-permute-done.2 = bf16[368,368]{1,0:T(8,128)(2,1)S(1)} collective-permute-done((bf16[368,368]{1,0:T(8,128)(2,1)S(1)}, bf16[368,368]{1,0:T(8,128)(2,1)S(1)}, u32[]{:S(2)}, u32[]{:S(2)}) %collective-permute-start.2) | collective-permute-done | bytes 270880 | tf_op jit(solution)/shard_map/while/body/eval_jaxpr/ppermute | solution.py:12
  572.7 11.4 %collective-permute-done.2 = bf16[368,368]{1,0:T(8,128)(2,1)S(1)} collective-permute-done((bf16[368,368]{1,0:T(8,128)(2,1)S(1)}, bf16[368,368]{1,0:T(8,128)(2,1)S(1)}, u32[]{:S(2)}, u32[]{:S(2)}) %collective-permute-start.2) | collective-permute-done | bytes 270880 | tf_op jit(solution)/shard_map/while/body/eval_jaxpr/ppermute | solution.py:12
  586.1 32.0 %all-reduce.9.cloned.1.call-done = f32[368,368]{1,0:T(8,128)} async-done(((f32[368,368]{1,0:T(8,128)}), f32[368,368]{1,0:T(8,128)}) %all-reduce.9.cloned.1.call-update) | async-done | bytes 541712 | tf_op jit(solution)/shard_map/psum | solution.py:40
  618.2 1.9 multiply_subtract_fusion
  (323 shorter events, 119.3 us)
Async XLA Ops:
  7.2 116.0 %all-gather.3.cloned.1.call-start = ((), (), s32[]{:S(2)}) async-start(), calls=%async_computation.3 | async-start | bytes 2506752 | tf_op jit(solution)/shard_map/all_gather | solution.py:63
  7.9 275.7 %all-reduce.5.cloned.1.call-start = ((), (), s32[]{:S(2)}) async-start(), calls=%async_computation | async-start | bytes 1130496 | tf_op jit(solution)/shard_map/psum | solution.py:40
  11.0 77.0 %collective-permute-start.3 = (bf16[368,368]{1,0:T(8,128)(2,1)S(1)}, bf16[368,368]{1,0:T(8,128)(2,1)S(1)}, u32[]{:S(2)}, u32[]{:S(2)}) collective-permute-start(bf16[368,368]{1,0:T(8,128)(2,1)S(1)} %convert_element_type.110), channel_id=1, source_target_pairs={{480,0},{0,32},{32,64},{64,96},{96,128},{128,160},{160,192},{192,2... | collective-permute-start | bytes 812552 | tf_op jit(solution)/shard_map/ppermute | solution.py:12
  133.4 18.2 %collective-permute-start = (bf16[368,368]{1,0:T(8,128)(2,1)S(1)}, bf16[368,368]{1,0:T(8,128)(2,1)S(1)}, u32[]{:S(2)}, u32[]{:S(2)}) collective-permute-start(bf16[368,368]{1,0:T(8,128)(2,1)S(1)} %copy.78), channel_id=1, source_target_pairs={{448,0},{480,32},{0,64},{32,96},{64,128},{96,160},{128,192},{160,2... | collective-permute-start | bytes 812552 | tf_op jit(solution)/shard_map/while/body/eval_jaxpr/ppermute | solution.py:12
  151.6 15.6 %collective-permute-start = (bf16[368,368]{1,0:T(8,128)(2,1)S(1)}, bf16[368,368]{1,0:T(8,128)(2,1)S(1)}, u32[]{:S(2)}, u32[]{:S(2)}) collective-permute-start(bf16[368,368]{1,0:T(8,128)(2,1)S(1)} %copy.78), channel_id=1, source_target_pairs={{448,0},{480,32},{0,64},{32,96},{64,128},{96,160},{128,192},{160,2... | collective-permute-start | bytes 812552 | tf_op jit(solution)/shard_map/while/body/eval_jaxpr/ppermute | solution.py:12
  167.3 17.1 %collective-permute-start = (bf16[368,368]{1,0:T(8,128)(2,1)S(1)}, bf16[368,368]{1,0:T(8,128)(2,1)S(1)}, u32[]{:S(2)}, u32[]{:S(2)}) collective-permute-start(bf16[368,368]{1,0:T(8,128)(2,1)S(1)} %copy.78), channel_id=1, source_target_pairs={{448,0},{480,32},{0,64},{32,96},{64,128},{96,160},{128,192},{160,2... | collective-permute-start | bytes 812552 | tf_op jit(solution)/shard_map/while/body/eval_jaxpr/ppermute | solution.py:12
  184.4 17.1 %collective-permute-start = (bf16[368,368]{1,0:T(8,128)(2,1)S(1)}, bf16[368,368]{1,0:T(8,128)(2,1)S(1)}, u32[]{:S(2)}, u32[]{:S(2)}) collective-permute-start(bf16[368,368]{1,0:T(8,128)(2,1)S(1)} %copy.78), channel_id=1, source_target_pairs={{448,0},{480,32},{0,64},{32,96},{64,128},{96,160},{128,192},{160,2... | collective-permute-start | bytes 812552 | tf_op jit(solution)/shard_map/while/body/eval_jaxpr/ppermute | solution.py:12
  201.5 17.0 %collective-permute-start = (bf16[368,368]{1,0:T(8,128)(2,1)S(1)}, bf16[368,368]{1,0:T(8,128)(2,1)S(1)}, u32[]{:S(2)}, u32[]{:S(2)}) collective-permute-start(bf16[368,368]{1,0:T(8,128)(2,1)S(1)} %copy.78), channel_id=1, source_target_pairs={{448,0},{480,32},{0,64},{32,96},{64,128},{96,160},{128,192},{160,2... | collective-permute-start | bytes 812552 | tf_op jit(solution)/shard_map/while/body/eval_jaxpr/ppermute | solution.py:12
  218.6 16.7 %collective-permute-start = (bf16[368,368]{1,0:T(8,128)(2,1)S(1)}, bf16[368,368]{1,0:T(8,128)(2,1)S(1)}, u32[]{:S(2)}, u32[]{:S(2)}) collective-permute-start(bf16[368,368]{1,0:T(8,128)(2,1)S(1)} %copy.78), channel_id=1, source_target_pairs={{448,0},{480,32},{0,64},{32,96},{64,128},{96,160},{128,192},{160,2... | collective-permute-start | bytes 812552 | tf_op jit(solution)/shard_map/while/body/eval_jaxpr/ppermute | solution.py:12
  235.3 17.0 %collective-permute-start = (bf16[368,368]{1,0:T(8,128)(2,1)S(1)}, bf16[368,368]{1,0:T(8,128)(2,1)S(1)}, u32[]{:S(2)}, u32[]{:S(2)}) collective-permute-start(bf16[368,368]{1,0:T(8,128)(2,1)S(1)} %copy.78), channel_id=1, source_target_pairs={{448,0},{480,32},{0,64},{32,96},{64,128},{96,160},{128,192},{160,2... | collective-permute-start | bytes 812552 | tf_op jit(solution)/shard_map/while/body/eval_jaxpr/ppermute | solution.py:12
  252.3 1.3 copy-start.1
  253.6 197.2 %all-reduce.7.cloned.1.call-start = ((), (), s32[]{:S(2)}) async-start(), calls=%async_computation.1 | async-start | bytes 1130496 | tf_op jit(solution)/shard_map/psum | solution.py:40
  285.5 13.9 %collective-permute-start.4 = (bf16[368,368]{1,0:T(8,128)(2,1)S(1)}, bf16[368,368]{1,0:T(8,128)(2,1)S(1)}, u32[]{:S(2)}, u32[]{:S(2)}) collective-permute-start(bf16[368,368]{1,0:T(8,128)(2,1)S(1)} %get-tuple-element.787), channel_id=1, source_target_pairs={{480,0},{0,32},{32,64},{64,96},{96,128},{128,160},{160,192},{192,2... | collective-permute-start | bytes 812552 | tf_op jit(solution)/shard_map/ppermute | solution.py:12
  299.5 15.6 %collective-permute-start.1 = (bf16[368,368]{1,0:T(8,128)(2,1)S(1)}, bf16[368,368]{1,0:T(8,128)(2,1)S(1)}, u32[]{:S(2)}, u32[]{:S(2)}) collective-permute-start(bf16[368,368]{1,0:T(8,128)(2,1)S(1)} %copy.88), channel_id=1, source_target_pairs={{448,0},{480,32},{0,64},{32,96},{64,128},{96,160},{128,192},{160,2... | collective-permute-start | bytes 812552 | tf_op jit(solution)/shard_map/while/body/eval_jaxpr/ppermute | solution.py:12
  315.2 16.7 %collective-permute-start.1 = (bf16[368,368]{1,0:T(8,128)(2,1)S(1)}, bf16[368,368]{1,0:T(8,128)(2,1)S(1)}, u32[]{:S(2)}, u32[]{:S(2)}) collective-permute-start(bf16[368,368]{1,0:T(8,128)(2,1)S(1)} %copy.88), channel_id=1, source_target_pairs={{448,0},{480,32},{0,64},{32,96},{64,128},{96,160},{128,192},{160,2... | collective-permute-start | bytes 812552 | tf_op jit(solution)/shard_map/while/body/eval_jaxpr/ppermute | solution.py:12
  331.9 17.1 %collective-permute-start.1 = (bf16[368,368]{1,0:T(8,128)(2,1)S(1)}, bf16[368,368]{1,0:T(8,128)(2,1)S(1)}, u32[]{:S(2)}, u32[]{:S(2)}) collective-permute-start(bf16[368,368]{1,0:T(8,128)(2,1)S(1)} %copy.88), channel_id=1, source_target_pairs={{448,0},{480,32},{0,64},{32,96},{64,128},{96,160},{128,192},{160,2... | collective-permute-start | bytes 812552 | tf_op jit(solution)/shard_map/while/body/eval_jaxpr/ppermute | solution.py:12
  349.1 16.7 %collective-permute-start.1 = (bf16[368,368]{1,0:T(8,128)(2,1)S(1)}, bf16[368,368]{1,0:T(8,128)(2,1)S(1)}, u32[]{:S(2)}, u32[]{:S(2)}) collective-permute-start(bf16[368,368]{1,0:T(8,128)(2,1)S(1)} %copy.88), channel_id=1, source_target_pairs={{448,0},{480,32},{0,64},{32,96},{64,128},{96,160},{128,192},{160,2... | collective-permute-start | bytes 812552 | tf_op jit(solution)/shard_map/while/body/eval_jaxpr/ppermute | solution.py:12
  365.9 17.1 %collective-permute-start.1 = (bf16[368,368]{1,0:T(8,128)(2,1)S(1)}, bf16[368,368]{1,0:T(8,128)(2,1)S(1)}, u32[]{:S(2)}, u32[]{:S(2)}) collective-permute-start(bf16[368,368]{1,0:T(8,128)(2,1)S(1)} %copy.88), channel_id=1, source_target_pairs={{448,0},{480,32},{0,64},{32,96},{64,128},{96,160},{128,192},{160,2... | collective-permute-start | bytes 812552 | tf_op jit(solution)/shard_map/while/body/eval_jaxpr/ppermute | solution.py:12
  383.1 16.6 %collective-permute-start.1 = (bf16[368,368]{1,0:T(8,128)(2,1)S(1)}, bf16[368,368]{1,0:T(8,128)(2,1)S(1)}, u32[]{:S(2)}, u32[]{:S(2)}) collective-permute-start(bf16[368,368]{1,0:T(8,128)(2,1)S(1)} %copy.88), channel_id=1, source_target_pairs={{448,0},{480,32},{0,64},{32,96},{64,128},{96,160},{128,192},{160,2... | collective-permute-start | bytes 812552 | tf_op jit(solution)/shard_map/while/body/eval_jaxpr/ppermute | solution.py:12
  399.7 17.1 %collective-permute-start.1 = (bf16[368,368]{1,0:T(8,128)(2,1)S(1)}, bf16[368,368]{1,0:T(8,128)(2,1)S(1)}, u32[]{:S(2)}, u32[]{:S(2)}) collective-permute-start(bf16[368,368]{1,0:T(8,128)(2,1)S(1)} %copy.88), channel_id=1, source_target_pairs={{448,0},{480,32},{0,64},{32,96},{64,128},{96,160},{128,192},{160,2... | collective-permute-start | bytes 812552 | tf_op jit(solution)/shard_map/while/body/eval_jaxpr/ppermute | solution.py:12
  416.8 1.5 copy-start.2
  418.1 200.0 %all-reduce.9.cloned.1.call-start = ((), (), s32[]{:S(2)}) async-start(), calls=%async_computation.2 | async-start | bytes 1130496 | tf_op jit(solution)/shard_map/psum | solution.py:40
  452.8 13.9 %collective-permute-start.5 = (bf16[368,368]{1,0:T(8,128)(2,1)S(1)}, bf16[368,368]{1,0:T(8,128)(2,1)S(1)}, u32[]{:S(2)}, u32[]{:S(2)}) collective-permute-start(bf16[368,368]{1,0:T(8,128)(2,1)S(1)} %get-tuple-element.801), channel_id=1, source_target_pairs={{480,0},{0,32},{32,64},{64,96},{96,128},{128,160},{160,192},{192,2... | collective-permute-start | bytes 812552 | tf_op jit(solution)/shard_map/ppermute | solution.py:12
  466.8 15.6 %collective-permute-start.2 = (bf16[368,368]{1,0:T(8,128)(2,1)S(1)}, bf16[368,368]{1,0:T(8,128)(2,1)S(1)}, u32[]{:S(2)}, u32[]{:S(2)}) collective-permute-start(bf16[368,368]{1,0:T(8,128)(2,1)S(1)} %copy.98), channel_id=1, source_target_pairs={{448,0},{480,32},{0,64},{32,96},{64,128},{96,160},{128,192},{160,2... | collective-permute-start | bytes 812552 | tf_op jit(solution)/shard_map/while/body/eval_jaxpr/ppermute | solution.py:12
  482.5 16.7 %collective-permute-start.2 = (bf16[368,368]{1,0:T(8,128)(2,1)S(1)}, bf16[368,368]{1,0:T(8,128)(2,1)S(1)}, u32[]{:S(2)}, u32[]{:S(2)}) collective-permute-start(bf16[368,368]{1,0:T(8,128)(2,1)S(1)} %copy.98), channel_id=1, source_target_pairs={{448,0},{480,32},{0,64},{32,96},{64,128},{96,160},{128,192},{160,2... | collective-permute-start | bytes 812552 | tf_op jit(solution)/shard_map/while/body/eval_jaxpr/ppermute | solution.py:12
  499.2 17.1 %collective-permute-start.2 = (bf16[368,368]{1,0:T(8,128)(2,1)S(1)}, bf16[368,368]{1,0:T(8,128)(2,1)S(1)}, u32[]{:S(2)}, u32[]{:S(2)}) collective-permute-start(bf16[368,368]{1,0:T(8,128)(2,1)S(1)} %copy.98), channel_id=1, source_target_pairs={{448,0},{480,32},{0,64},{32,96},{64,128},{96,160},{128,192},{160,2... | collective-permute-start | bytes 812552 | tf_op jit(solution)/shard_map/while/body/eval_jaxpr/ppermute | solution.py:12
  516.4 16.7 %collective-permute-start.2 = (bf16[368,368]{1,0:T(8,128)(2,1)S(1)}, bf16[368,368]{1,0:T(8,128)(2,1)S(1)}, u32[]{:S(2)}, u32[]{:S(2)}) collective-permute-start(bf16[368,368]{1,0:T(8,128)(2,1)S(1)} %copy.98), channel_id=1, source_target_pairs={{448,0},{480,32},{0,64},{32,96},{64,128},{96,160},{128,192},{160,2... | collective-permute-start | bytes 812552 | tf_op jit(solution)/shard_map/while/body/eval_jaxpr/ppermute | solution.py:12
  533.2 17.1 %collective-permute-start.2 = (bf16[368,368]{1,0:T(8,128)(2,1)S(1)}, bf16[368,368]{1,0:T(8,128)(2,1)S(1)}, u32[]{:S(2)}, u32[]{:S(2)}) collective-permute-start(bf16[368,368]{1,0:T(8,128)(2,1)S(1)} %copy.98), channel_id=1, source_target_pairs={{448,0},{480,32},{0,64},{32,96},{64,128},{96,160},{128,192},{160,2... | collective-permute-start | bytes 812552 | tf_op jit(solution)/shard_map/while/body/eval_jaxpr/ppermute | solution.py:12
  550.3 16.6 %collective-permute-start.2 = (bf16[368,368]{1,0:T(8,128)(2,1)S(1)}, bf16[368,368]{1,0:T(8,128)(2,1)S(1)}, u32[]{:S(2)}, u32[]{:S(2)}) collective-permute-start(bf16[368,368]{1,0:T(8,128)(2,1)S(1)} %copy.98), channel_id=1, source_target_pairs={{448,0},{480,32},{0,64},{32,96},{64,128},{96,160},{128,192},{160,2... | collective-permute-start | bytes 812552 | tf_op jit(solution)/shard_map/while/body/eval_jaxpr/ppermute | solution.py:12
  567.0 17.1 %collective-permute-start.2 = (bf16[368,368]{1,0:T(8,128)(2,1)S(1)}, bf16[368,368]{1,0:T(8,128)(2,1)S(1)}, u32[]{:S(2)}, u32[]{:S(2)}) collective-permute-start(bf16[368,368]{1,0:T(8,128)(2,1)S(1)} %copy.98), channel_id=1, source_target_pairs={{448,0},{480,32},{0,64},{32,96},{64,128},{96,160},{128,192},{160,2... | collective-permute-start | bytes 812552 | tf_op jit(solution)/shard_map/while/body/eval_jaxpr/ppermute | solution.py:12
  584.1 1.3 copy-start.3
  584.5 33.7 %copy-start = (f32[368,368]{1,0:T(8,128)S(1)}, f32[368,368]{1,0:T(8,128)}, u32[]{:S(2)}) copy-start(f32[368,368]{1,0:T(8,128)} %get-tuple-element.788) | copy-start | bytes 1625092
Sparse Core Ops, SparseCore 0:
  11.2 111.9 all-gather.2
  253.7 29.8 all-reduce.4
  418.2 32.5 all-reduce.6
  585.5 32.5 all-reduce.8
where the time goes:
time: 628 us; the launch traced here: 627 us
  waiting for transfers between devices  383 us (61%)
  blocking collectives  67.2 us (11%)
  local copies, waits for them, and re-layouts  66.4 us (11%)
  starting transfers between devices  49.2 us (8%)
  other arithmetic  23.2 us (4%)
  matrix products  17.6 us (3%)
  between operations  17.4 us (3%)
    ppermute x24, waiting for transfers between devices, shifted(): return lax.ppermute(block, axis, route)  254 us
    psum x3, waiting for transfers between devices, finish_term(): return tile_mask(indices, counts, block_size) * lax.psum(total_sum, 'layer')  93 us
    ppermute x24, starting transfers between devices, shifted(): return lax.ppermute(block, axis, route)  48.9 us
    all_gather x1, blocking collectives, per_device(): lax.all_gather(ham_index, 'col', axis=2, tiled=True)  43.8 us
    all_gather x1, waiting for transfers between devices, per_device(): lax.all_gather(ham_blocks, 'col', axis=1, tiled=True)  35.1 us
    unnamed x1, blocking collectives  23.4 us
    dynamic_slice x22, local copies, waits for them, and re-layouts, ham_tile(): lax.dynamic_slice_in_dim(panel, which * capacity * block_size, capacity *...  22.6 us
    lt x26, other arithmetic, selector(): in_use = jnp.arange(capacity) < counts[0, 0]  14.1 us
  transfers between devices with their start and end apart: 28, of which 27 were waited for; matrix products, arithmetic and copies ran while one was open for 14% of the time, Pallas kernels for 0%

commit v1 on v0

v1 whole, which is shorter than its diff:
```python
import functools

import jax
import jax.numpy as jnp
from jax import lax
from jax.experimental import pallas as pl
from jax.experimental.pallas import tpu as pltpu
from jax.sharding import Mesh, PartitionSpec as P

BLK = 92
HALF = 46
BT = 4
CAP = 8
ROWS = 96
COLS = 48
LANES = 128
SIDE = BT * BLK
WIRE = 768
META = 736
TILES = 16
BF = jnp.bfloat16
F32 = jnp.float32
VMEM = pl.BlockSpec(memory_space=pltpu.VMEM)
SMEM = pl.BlockSpec(memory_space=pltpu.SMEM)
PARAMS = pltpu.CompilerParams(vmem_limit_bytes=48 * 1024 * 1024)


def dot_nt(a, b):
    return lax.dot_general(a, b, (((1,), (1,)), ((), ())), preferred_element_type=F32)


def one_hot(shape, shift, width):
    q = lax.broadcasted_iota(jnp.int32, shape, 0)
    x = lax.broadcasted_iota(jnp.int32, shape, 1)
    return jnp.where((x == q + shift) & (q < width), 1.0, 0.0).astype(BF)


def prep_kernel(layer_ref, code_ref, ham_ref, dens_ref, hmeta_ref, dmeta_ref,
                hwire_ref, dwire_ref, dense_ref, pad_ref):
    layer = layer_ref[0]
    lane = lax.broadcasted_iota(jnp.int32, (COLS, LANES), 1)
    pad_ref[...] = jnp.zeros_like(pad_ref)
    pad_ref[0:BLK, 0:META] = ham_ref[...]
    start = pl.multiple_of(layer * COLS, 16)
    hwire_ref[...] = pad_ref[pl.ds(start, COLS), :]
    last = hwire_ref[:, WIRE - LANES:]
    hwire_ref[:, WIRE - LANES:] = jnp.where(lane >= META - (WIRE - LANES), hmeta_ref[...], last)
    dens = dens_ref[...]
    dense_ref[...] = jnp.zeros_like(dense_ref)
    pieces = []
    for s in range(CAP):
        pick = one_hot((COLS, META), s * BLK + layer * HALF, HALF)
        piece = dot_nt(pick, dens)
        pieces.append(piece.astype(BF))
        code = code_ref[0, s]
        at = jnp.maximum(code, 0)
        i, j = at // BT, at % BT
        x = lax.broadcasted_iota(jnp.int32, (META, BT * COLS), 0)
        y = lax.broadcasted_iota(jnp.int32, (META, BT * COLS), 1) - j * COLS
        spread = jnp.where(
            (x == y + (s * BLK + layer * HALF)) & (y >= 0) & (y < HALF) & (code >= 0), 1.0, 0.0
        ).astype(BF)
        block = jnp.dot(dens, spread, preferred_element_type=F32)
        block = jnp.concatenate([block, jnp.zeros((ROWS - BLK, BT * COLS), F32)], axis=0)
        rows = pl.ds(pl.multiple_of(i * ROWS, ROWS), ROWS)
        dense_ref[rows, :] = dense_ref[rows, :] + block
    pieces.append(jnp.zeros((COLS, WIRE - META), BF))
    wire = jnp.concatenate(pieces, axis=1)
    tail = jnp.where(lane >= META - (WIRE - LANES), dmeta_ref[...], wire[:, WIRE - LANES:])
    dwire_ref[0, :, 0:WIRE - LANES] = wire[:, 0:WIRE - LANES]
    dwire_ref[0, :, WIRE - LANES:] = tail
    for n in range(1, TILES):
        dwire_ref[n] = dwire_ref[0]


def ham_kernel(layer_ref, code_ref, own_ref, other_ref, out_ref):
    layer = layer_ref[0]
    out_ref[...] = jnp.zeros_like(out_ref)

    def tile(k, carry):
        for ref, part in ((own_ref, layer), (other_ref, 1 - layer)):
            wire = ref[k]
            for s in range(CAP):
                code = code_ref[k, s]
                at = jnp.maximum(code, 0)
                where = jnp.where(code >= 0, k, TILES)
                rows = pl.ds(pl.multiple_of((at // BT) * ROWS + part * COLS, 16), COLS)
                lanes = pl.ds(pl.multiple_of((at % BT) * LANES, LANES), BLK)
                out_ref[where, rows, lanes] = wire[:, s * BLK:(s + 1) * BLK]
        return carry

    lax.fori_loop(0, TILES, tile, 0)


def product(ham_ref, code_ref, wire_ref, right_ref):
    right_ref[...] = jnp.zeros_like(right_ref)

    def tile(k, carry):
        wire = wire_ref[k]
        for s in range(CAP):
            code = code_ref[k, s]
            at = jnp.maximum(code, 0)
            where = jnp.where(code >= 0, k, TILES)
            rows = pl.ds(pl.multiple_of((at % BT) * COLS, 16), COLS)
            lanes = pl.ds(pl.multiple_of((at // BT) * LANES, LANES), BLK)
            right_ref[where, rows, lanes] = wire[:, s * BLK:(s + 1) * BLK]
        return carry

    lax.fori_loop(0, TILES, tile, 0)
    total = jnp.zeros((BT * ROWS, BT * COLS), F32)

    def add(k, total):
        return total + dot_nt(ham_ref[k], right_ref[k])

    return lax.fori_loop(0, TILES, add, total)


def keep(code_ref, total):
    row = lax.broadcasted_iota(jnp.int32, total.shape, 0) // ROWS
    col = lax.broadcasted_iota(jnp.int32, total.shape, 1) // COLS
    place = row * BT + col
    kept = place == code_ref[0, 0]
    for s in range(1, CAP):
        kept = kept | (place == code_ref[0, s])
    return jnp.where(kept, total, 0.0)


def pack(code_ref, term, rounded_ref, wire_ref):
    rounded_ref[...] = term.astype(BF)
    pieces = []
    for s in range(CAP):
        at = jnp.maximum(code_ref[0, s], 0)
        pick = one_hot((COLS, BT * COLS), (at % BT) * COLS, COLS)
        rows = pl.ds(pl.multiple_of((at // BT) * ROWS, 16), ROWS)
        pieces.append(dot_nt(pick, rounded_ref[rows, :]).astype(BF)[:, 0:BLK])
    pieces.append(jnp.zeros((COLS, WIRE - META), BF))
    wire = jnp.concatenate(pieces, axis=1)
    for n in range(TILES):
        wire_ref[n] = wire


def first_kernel(code_ref, keep_ref, ham_ref, wire_ref, term_ref, out_ref, right_ref, rounded_ref):
    term = keep(keep_ref, product(ham_ref, code_ref, wire_ref, right_ref))
    term_ref[...] = term
    pack(keep_ref, term, rounded_ref, out_ref)


def second_kernel(code_ref, keep_ref, ham_ref, wire_ref, dense_ref, real_ref, out_ref, right_ref,
                  rounded_ref):
    term = keep(keep_ref, product(ham_ref, code_ref, wire_ref, right_ref))
    real_ref[...] = dense_ref[...] - 0.5 * term
    pack(keep_ref, term, rounded_ref, out_ref)


def third_kernel(code_ref, keep_ref, ham_ref, wire_ref, first_ref, imag_ref, right_ref):
    term = keep(keep_ref, product(ham_ref, code_ref, wire_ref, right_ref))
    imag_ref[...] = term / 6.0 - first_ref[...]


def join_kernel(layer_ref, own_ref, other_ref, out_ref):
    swap = layer_ref[0] == 1
    own, other = own_ref[...], other_ref[...]
    low, high = jnp.where(swap, other, own), jnp.where(swap, own, other)
    pieces = []
    for j in range(BT):
        pieces += [low[:, j * COLS:j * COLS + HALF], high[:, j * COLS:j * COLS + HALF]]
    whole = jnp.concatenate(pieces, axis=1)
    for i in range(BT):
        out_ref[i * BLK:(i + 1) * BLK, :] = whole[i * ROWS:i * ROWS + BLK, :]


def call(kernel, scalars, arrays, out_shape, scratch=()):
    return pl.pallas_call(
        kernel,
        out_shape=out_shape,
        in_specs=[SMEM] * len(scalars) + [VMEM] * len(arrays),
        out_specs=jax.tree.map(lambda _: VMEM, out_shape),
        scratch_shapes=list(scratch),
        compiler_params=PARAMS,
    )(*scalars, *arrays)


def shape(*dims, dtype=BF):
    return jax.ShapeDtypeStruct(dims, dtype)


def codes(index, count):
    slot = jnp.arange(CAP)
    return jnp.where(slot < count[0, 0], index[0, 0] * BT + index[1, 0], -1)[None, :]


def wire_meta(*lists):
    flat = jnp.concatenate([one[0] for one in lists]).astype(BF)
    flat = jnp.pad(flat, (LANES - (WIRE - META), WIRE - META - flat.shape[0]))
    return jnp.broadcast_to(flat[None, :], (COLS, LANES))


def read_meta(wires, which):
    return wires[:, 0, META + which * CAP:META + (which + 1) * CAP].astype(jnp.int32)


def swap(values, axis):
    return lax.ppermute(values, axis, [(0, 1), (1, 0)])


def per_device(ham_blocks, ham_index, ham_count, dens_blocks, dens_index, dens_count, first_index,
               first_count, second_index, second_count, third_index, third_count):
    layer = lax.axis_index("layer").astype(jnp.int32).reshape(1)
    ham_code = codes(ham_index, ham_count)
    dens_code = codes(dens_index, dens_count)
    first_code = codes(first_index, first_count)
    second_code = codes(second_index, second_count)
    third_code = codes(third_index, third_count)
    ham_wire, dens_wire, dens_half = call(
        prep_kernel,
        (layer, dens_code),
        (ham_blocks, dens_blocks, wire_meta(ham_code), wire_meta(dens_code, first_code, second_code)),
        (shape(COLS, WIRE), shape(TILES, COLS, WIRE), shape(BT * ROWS, BT * COLS, dtype=F32)),
        [pltpu.VMEM((ROWS, WIRE), BF)],
    )
    far = swap(ham_wire, "y_hi")
    y_hi = lax.axis_index("y_hi")
    pair = jnp.where(y_hi == 0, jnp.stack([ham_wire, far]), jnp.stack([far, ham_wire]))
    depth = lax.axis_size("z")
    panel = lax.all_to_all(jnp.broadcast_to(pair, (depth,) + pair.shape), "z", 0, 0)
    panel = panel.reshape(TILES, COLS, WIRE)
    other = swap(panel, "layer")

    def gather(wires):
        return lax.all_to_all(wires, ("x", "y_lo"), 0, 0)

    right = gather(dens_wire)
    in_dens, in_first, in_second = (read_meta(right, n) for n in range(3))
    ham = call(
        ham_kernel, (layer, read_meta(panel, 0)), (panel, other),
        shape(TILES + 1, BT * ROWS, BT * LANES),
    )
    half = shape(BT * ROWS, BT * COLS, dtype=F32)
    dense_right = pltpu.VMEM((TILES + 1, BT * COLS, BT * LANES), BF)
    rounded = pltpu.VMEM((BT * ROWS, BT * COLS), BF)
    wires = shape(TILES, COLS, WIRE)
    first_term, first_wire = call(
        first_kernel, (in_dens, first_code), (ham, right), (half, wires), [dense_right, rounded]
    )
    real_half, second_wire = call(
        second_kernel, (in_first, second_code), (ham, gather(first_wire), dens_half), (half, wires),
        [dense_right, rounded],
    )
    imag_half = call(
        third_kernel, (in_second, third_code), (ham, gather(second_wire), first_term), half,
        [dense_right],
    )

    def join(part):
        return call(join_kernel, (layer,), (part, swap(part, "layer")), shape(SIDE, SIDE, dtype=F32))

    return join(real_half), join(imag_half)


def solution(mesh):
    axes = ("x", "y_lo", "z", "y_hi", "layer")
    split = Mesh(mesh.devices.reshape(4, 4, 8, 2, 2), axes)
    row, col = ("x", "y_lo"), ("z", "y_hi")
    blocks, index = P(row, col), P(None, row, col)
    in_specs = (blocks, index, blocks) * 2 + (index, blocks) * 3
    return jax.shard_map(
        per_device, mesh=split, in_specs=in_specs, out_specs=(blocks, blocks), check_vma=False
    )
```

time: 628 us -> 217 us (0.35)
  waiting for transfers between devices: 383 us -> 82.2 us
  local copies, waits for them, and re-layouts: 66.4 us -> 3.44 us
  Pallas kernels: 0 us -> 45.9 us
  blocking collectives: 67.2 us -> 38.2 us
  other arithmetic: 23.2 us -> 4.18 us
  matrix products: 17.6 us -> 0 us
  between operations: 17.4 us -> 4.04 us
  starting transfers between devices: 49.2 us -> 38.1 us
    ppermute x24 -> x4, waiting for transfers between devices: 254 us -> 1.81 us  [swap(): return lax.ppermute(values, axis, [(0, 1), (1, 0)])]
    psum x3 -> x0, waiting for transfers between devices: 93 us -> none  [finish_term(): return tile_mask(indices, counts, block_size) * lax.psum(total_sum, 'layer')]
    all_to_all x0 -> x3, waiting for transfers between devices: none -> 80.4 us  [gather(): return lax.all_to_all(wires, ('x', 'y_lo'), 0, 0)]
    pallas_call x0 -> x7, Pallas kernels: none -> 45.9 us  [call(): pl.pallas_call(kernel, out_shape=out_shape, in_specs=[SMEM] * len(scalars...]
    all_gather x1 -> x0, blocking collectives: 43.8 us -> none  [per_device(): lax.all_gather(ham_index, 'col', axis=2, tiled=True)]
    all_to_all x0 -> x1, blocking collectives: none -> 38.2 us  [per_device(): lax.all_to_all(jnp.broadcast_to(pair, (depth,) + pair.shape), 'z', 0, 0)]
    dynamic_slice x43 -> x0, local copies, waits for them, and re-layouts: 35.2 us -> none  [the longest x22 22.6 us: ham_tile(): lax.dynamic_slice_in_dim(panel, which * capacity * block_size, capacity *...]
    all_gather x1 -> x0, waiting for transfers between devices: 35.1 us -> none  [per_device(): lax.all_gather(ham_blocks, 'col', axis=1, tiled=True)]
  transfers between devices with their start and end apart: 28 -> 7, of which waited for: 27 -> 4; matrix products, arithmetic and copies ran while one was open for 14% -> 1% of each run, Pallas kernels for 0% -> 5%
where the time goes in v1:
time: 217 us; the launch traced here: 216 us
  waiting for transfers between devices  82.2 us (38%)
  Pallas kernels  45.9 us (21%)
  blocking collectives  38.2 us (18%)
  starting transfers between devices  38.1 us (18%)
  other arithmetic  4.18 us (2%)
  between operations  4.04 us (2%)
  local copies, waits for them, and re-layouts  3.44 us (2%)
    all_to_all x3, waiting for transfers between devices, gather(): return lax.all_to_all(wires, ('x', 'y_lo'), 0, 0)  80.4 us
    pallas_call x7, Pallas kernels, call(): pl.pallas_call(kernel, out_shape=out_shape, in_specs=[SMEM] * len(scalars...  45.9 us
    all_to_all x1, blocking collectives, per_device(): lax.all_to_all(jnp.broadcast_to(pair, (depth,) + pair.shape), 'z', 0, 0)  38.2 us
    all_to_all x3, starting transfers between devices, gather(): return lax.all_to_all(wires, ('x', 'y_lo'), 0, 0)  19.1 us
    ppermute x4, starting transfers between devices, swap(): return lax.ppermute(values, axis, [(0, 1), (1, 0)])  18.9 us
  transfers between devices with their start and end apart: 7, of which 4 were waited for; matrix products, arithmetic and copies ran while one was open for 1% of the time, Pallas kernels for 5%

profile of v1, /device:TPU:1, one launch (start us, length us, event | category | flops | bytes accessed | tf_op | source)
XLA Modules:
  0.0 216.0 jit_solution(7453553891307016289)
XLA Ops:
  3.2 0.7 fusion.3
  3.9 0.7 compare_select_fusion.7.code_ref
  4.6 0.7 fusion
  5.3 0.1 pad.8
  5.3 0.7 fusion.1
  6.0 0.1 select_maximum_fusion
  6.1 0.0 copy-start.2
  6.1 0.9 copy-done.2
  7.0 0.0 copy-start.3
  7.0 0.9 copy-done.3
  8.0 3.0 %shard_map.131 = (bf16[48,768]{1,0:T(8,128)(2,1)S(1)}, bf16[16,48,768]{2,1,0:T(8,128)(2,1)}, f32[384,192]{1,0:T(8,128)S(1)}) custom-call(s32[1]{0:T(128)} %bitcast.layer_ref, s32[1,8]{1,0:T(1,128)S(1)} %compare_select_fusion.7.code_ref, bf16[92,736]{1,0:T(8,128)(2,1)S(1)} %copy-done.2, bf16[92,736]{1,0:T(8,128)(2,1)S(1)} %copy-done.3, ...), custom_call_target="tpu_custom_call" | custom-call | tf_op jit(solution)/shard_map/pallas_call | solution.py:173
  11.0 0.0 copy-start
  11.0 0.7 copy-done
  11.7 8.3 %collective-permute-start = (bf16[48,768]{1,0:T(8,128)(2,1)S(1)}, bf16[48,768]{1,0:T(8,128)(2,1)S(1)}, u32[]{:S(2)}, u32[]{:S(2)}) collective-permute-start(bf16[48,768]{1,0:T(8,128)(2,1)S(1)} %get-tuple-element.10), channel_id=1, source_target_pairs={{0,2},{2,0},{1,3},{3,1},{4,6},{6,4},{5,7},{7,5},{8,10},{10,8},{9,1... | collective-permute-start | bytes 221192 | tf_op jit(solution)/shard_map/ppermute | solution.py:203
  20.0 1.8 collective-permute-done
  21.8 0.1 broadcast_in_dim.33
  21.9 38.2 %all_to_all.20 = bf16[8,2,48,768]{3,2,1,0:T(8,128)(2,1)S(1)} all-to-all(bf16[8,2,48,768]{3,2,1,0:T(8,128)(2,1)S(1)} %broadcast_in_dim.33), channel_id=1, replica_groups=mesh['x'=4,'y_lo'=4,'z'=8,'y_hi'=2,'layer'=2] {'z'}, dimensions={0} | all-to-all | bytes 2359296 | tf_op jit(solution)/shard_map/all_to_all | solution.py:225
  60.1 0.0 copy-start.7
  60.1 10.6 %all-to-all-start = ((bf16[16,48,768]{2,1,0:T(8,128)(2,1)}), bf16[16,48,768]{2,1,0:T(8,128)(2,1)S(1)}, u32[]{:S(2)}, u32[]{:S(2)}) async-start(bf16[16,48,768]{2,1,0:T(8,128)(2,1)} %get-tuple-element.9), calls=%async_computation | async-start | bytes 2359296 | tf_op jit(solution)/shard_map/all_to_all | solution.py:230
  70.6 4.3 %collective-permute-start.1 = (bf16[16,48,768]{2,1,0:T(8,128)(2,1)S(1)}, bf16[16,48,768]{2,1,0:T(8,128)(2,1)S(1)}, u32[]{:S(2)}, u32[]{:S(2)}) collective-permute-start(bf16[16,48,768]{2,1,0:T(8,128)(2,1)S(1)} %bitcast.37), channel_id=1, source_target_pairs={{0,1},{1,0},{2,3},{3,2},{4,5},{5,4},{6,7},{7,6},{8,9},{9,8},{10,11... | collective-permute-start | bytes 3538952 | tf_op jit(solution)/shard_map/ppermute | solution.py:203
  74.9 0.0 copy-done.7
  74.9 0.5 compare_select_fusion.1.keep_ref
  75.5 0.7 slice_convert_fusion.2
  76.2 24.2 %all-to-all-done.wire_ref = bf16[16,48,768]{2,1,0:T(8,128)(2,1)S(1)} async-done(((bf16[16,48,768]{2,1,0:T(8,128)(2,1)}), bf16[16,48,768]{2,1,0:T(8,128)(2,1)S(1)}, u32[]{:S(2)}, u32[]{:S(2)}) %all-to-all-start) | async-done | bytes 1179680 | tf_op jit(solution)/shard_map/all_to_all | solution.py:230
  100.4 0.1 slice_convert_fusion
  100.5 0.0 collective-permute-done.1.other_ref
  100.5 0.0 copy-start.4
  100.5 0.7 copy-done.4
  101.2 0.0 copy-start.5
  101.2 6.8 %shard_map.132.ham_ref = bf16[17,384,512]{2,1,0:T(8,128)(2,1)} custom-call(s32[1]{0:T(128)} %bitcast.layer_ref, s32[16,8]{1,0:T(8,128)S(1)} %bitcast.44, bf16[16,48,768]{2,1,0:T(8,128)(2,1)S(1)} %bitcast.39, bf16[16,48,768]{2,1,0:T(8,128)(2,1)S(1)} %collective-permute-done.1.other_ref), custom_call_target="tpu_custom_call" | custom-call | tf_op jit(solution)/shard_map/pallas_call | solution.py:173
  108.0 0.0 copy-done.5
  108.0 11.6 %shard_map.133 = (f32[384,192]{1,0:T(8,128)S(1)}, bf16[16,48,768]{2,1,0:T(8,128)(2,1)}) custom-call(s32[16,8]{1,0:T(8,128)S(1)} %bitcast.43, s32[1,8]{1,0:T(1,128)S(1)} %copy-done.5, bf16[17,384,512]{2,1,0:T(8,128)(2,1)} %shard_map.132.ham_ref, bf16[16,48,768]{2,1,0:T(8,128)(2,1)S(1)} %all-to-all-done.wire_ref), custom_call_target="tpu_custom_call" | custom-call | tf_op jit(solution)/shard_map/pallas_call | solution.py:173
  119.7 0.0 copy-start.6
  119.7 3.8 %all-to-all-start.2 = ((bf16[16,48,768]{2,1,0:T(8,128)(2,1)}), bf16[16,48,768]{2,1,0:T(8,128)(2,1)S(1)}, u32[]{:S(2)}, u32[]{:S(2)}) async-start(bf16[16,48,768]{2,1,0:T(8,128)(2,1)} %get-tuple-element.11), calls=%async_computation.2 | async-start | bytes 2359296 | tf_op jit(solution)/shard_map/all_to_all | solution.py:230
  123.5 0.0 copy-done.6
  123.5 29.8 %all-to-all-done.2.wire_ref = bf16[16,48,768]{2,1,0:T(8,128)(2,1)S(1)} async-done(((bf16[16,48,768]{2,1,0:T(8,128)(2,1)}), bf16[16,48,768]{2,1,0:T(8,128)(2,1)S(1)}, u32[]{:S(2)}, u32[]{:S(2)}) %all-to-all-start.2) | async-done | bytes 1179680 | tf_op jit(solution)/shard_map/all_to_all | solution.py:230
  153.3 0.0 copy-done.1
  153.3 11.6 %shard_map.134 = (f32[384,192]{1,0:T(8,128)S(1)}, bf16[16,48,768]{2,1,0:T(8,128)(2,1)}) custom-call(s32[16,8]{1,0:T(8,128)S(1)} %bitcast.42, s32[1,8]{1,0:T(1,128)S(1)} %compare_select_fusion.2.keep_ref, bf16[17,384,512]{2,1,0:T(8,128)(2,1)} %shard_map.132.ham_ref, bf16[16,48,768]{2,1,0:T(8,128)(2,1)S(1)} %all-to-all-done.2.wire_ref, f32[384,192]{1,0:T(8,128)S(1)} %copy-done.1), custom_call_target="tpu_custom_call" | custom-call | tf_op jit(solution)/shard_map/pallas_call | solution.py:173
  164.9 4.7 %all-to-all-start.3 = ((bf16[16,48,768]{2,1,0:T(8,128)(2,1)}), bf16[16,48,768]{2,1,0:T(8,128)(2,1)S(1)}, u32[]{:S(2)}, u32[]{:S(2)}) async-start(bf16[16,48,768]{2,1,0:T(8,128)(2,1)} %get-tuple-element.14), calls=%async_computation.3 | async-start | bytes 2359296 | tf_op jit(solution)/shard_map/all_to_all | solution.py:230
  170.3 0.0 copy-done.8
  170.4 2.8 %collective-permute-start.2 = (f32[384,192]{1,0:T(8,128)S(1)}, f32[384,192]{1,0:T(8,128)S(1)}, u32[]{:S(2)}, u32[]{:S(2)}) collective-permute-start(f32[384,192]{1,0:T(8,128)S(1)} %get-tuple-element.13.own_ref), channel_id=1, source_target_pairs={{0,1},{1,0},{2,3},{3,2},{4,5},{5,4},{6,7},{7,6},{8,9},{9,8},{10,11... | collective-permute-start | bytes 884744 | tf_op jit(solution)/shard_map/ppermute | solution.py:203
  173.1 26.4 %all-to-all-done.3.wire_ref = bf16[16,48,768]{2,1,0:T(8,128)(2,1)S(1)} async-done(((bf16[16,48,768]{2,1,0:T(8,128)(2,1)}), bf16[16,48,768]{2,1,0:T(8,128)(2,1)S(1)}, u32[]{:S(2)}, u32[]{:S(2)}) %all-to-all-start.3) | async-done | bytes 1179680 | tf_op jit(solution)/shard_map/all_to_all | solution.py:230
  199.5 10.1 %shard_map.136.own_ref = f32[384,192]{1,0:T(8,128)S(1)} custom-call(s32[16,8]{1,0:T(8,128)S(1)} %bitcast.41, s32[1,8]{1,0:T(1,128)S(1)} %compare_select_fusion.keep_ref, bf16[17,384,512]{2,1,0:T(8,128)(2,1)} %shard_map.132.ham_ref, bf16[16,48,768]{2,1,0:T(8,128)(2,1)S(1)} %all-to-all-done.3.wire_ref, f32[384,192]{1,0:T(8,128)S(1)} %get-tuple-element.15.first_ref), custom_call_target="tpu_custom_call" | custom-call | tf_op jit(solution)/shard_map/pallas_call | solution.py:173
  209.7 3.6 %collective-permute-start.3 = (f32[384,192]{1,0:T(8,128)S(1)}, f32[384,192]{1,0:T(8,128)S(1)}, u32[]{:S(2)}, u32[]{:S(2)}) collective-permute-start(f32[384,192]{1,0:T(8,128)S(1)} %shard_map.136.own_ref), channel_id=1, source_target_pairs={{0,1},{1,0},{2,3},{3,2},{4,5},{5,4},{6,7},{7,6},{8,9},{9,8},{10,11... | collective-permute-start | bytes 884744 | tf_op jit(solution)/shard_map/ppermute | solution.py:203
  213.3 0.0 collective-permute-done.2.other_ref
  213.3 1.3 shard_map.135
  214.7 0.0 collective-permute-done.3.other_ref
  214.7 1.3 shard_map.137
  (7 shorter events, 0.0 us)
Async XLA Ops:
  6.1 0.9 copy-start.2
  7.0 0.9 copy-start.3
  11.0 0.7 copy-start
  11.7 10.1 %collective-permute-start = (bf16[48,768]{1,0:T(8,128)(2,1)S(1)}, bf16[48,768]{1,0:T(8,128)(2,1)S(1)}, u32[]{:S(2)}, u32[]{:S(2)}) collective-permute-start(bf16[48,768]{1,0:T(8,128)(2,1)S(1)} %get-tuple-element.10), channel_id=1, source_target_pairs={{0,2},{2,0},{1,3},{3,1},{4,6},{6,4},{5,7},{7,5},{8,10},{10,8},{9,1... | collective-permute-start | bytes 221192 | tf_op jit(solution)/shard_map/ppermute | solution.py:203
  60.1 14.8 %copy-start.7 = (s32[2,1,8]{2,1,0:T(1,128)S(1)}, s32[2,1,8]{2,1,0:T(1,128)}, u32[]{:S(2)}) copy-start(s32[2,1,8]{2,1,0:T(1,128)} %param.18) | copy-start | bytes 196
  60.1 40.3 %all-to-all-start = ((bf16[16,48,768]{2,1,0:T(8,128)(2,1)}), bf16[16,48,768]{2,1,0:T(8,128)(2,1)S(1)}, u32[]{:S(2)}, u32[]{:S(2)}) async-start(bf16[16,48,768]{2,1,0:T(8,128)(2,1)} %get-tuple-element.9), calls=%async_computation | async-start | bytes 2359296 | tf_op jit(solution)/shard_map/all_to_all | solution.py:230
  70.6 29.9 %collective-permute-start.1 = (bf16[16,48,768]{2,1,0:T(8,128)(2,1)S(1)}, bf16[16,48,768]{2,1,0:T(8,128)(2,1)S(1)}, u32[]{:S(2)}, u32[]{:S(2)}) collective-permute-start(bf16[16,48,768]{2,1,0:T(8,128)(2,1)S(1)} %bitcast.37), channel_id=1, source_target_pairs={{0,1},{1,0},{2,3},{3,2},{4,5},{5,4},{6,7},{7,6},{8,9},{9,8},{10,11... | collective-permute-start | bytes 3538952 | tf_op jit(solution)/shard_map/ppermute | solution.py:203
  100.5 0.7 copy-start.4
  101.2 6.8 %copy-start.5 = (s32[1,8]{1,0:T(1,128)S(1)}, s32[1,8]{1,0:T(1,128)}, u32[]{:S(2)}) copy-start(s32[1,8]{1,0:T(1,128)} %compare_select_fusion.1.keep_ref) | copy-start | bytes 100
  119.7 3.8 %copy-start.6 = (s32[2,1,8]{2,1,0:T(1,128)S(1)}, s32[2,1,8]{2,1,0:T(1,128)}, u32[]{:S(2)}) copy-start(s32[2,1,8]{2,1,0:T(1,128)} %param.20) | copy-start | bytes 196
  119.7 33.6 %copy-start.1 = (f32[384,192]{1,0:T(8,128)S(1)}, f32[384,192]{1,0:T(8,128)}, u32[]{:S(2)}) copy-start(f32[384,192]{1,0:T(8,128)} %copy-done) | copy-start | bytes 884740
  119.7 33.6 %all-to-all-start.2 = ((bf16[16,48,768]{2,1,0:T(8,128)(2,1)}), bf16[16,48,768]{2,1,0:T(8,128)(2,1)S(1)}, u32[]{:S(2)}, u32[]{:S(2)}) async-start(bf16[16,48,768]{2,1,0:T(8,128)(2,1)} %get-tuple-element.11), calls=%async_computation.2 | async-start | bytes 2359296 | tf_op jit(solution)/shard_map/all_to_all | solution.py:230
  164.9 5.4 %copy-start.8 = (s32[2,1,8]{2,1,0:T(1,128)S(1)}, s32[2,1,8]{2,1,0:T(1,128)}, u32[]{:S(2)}) copy-start(s32[2,1,8]{2,1,0:T(1,128)} %param.22) | copy-start | bytes 196
  164.9 34.6 %all-to-all-start.3 = ((bf16[16,48,768]{2,1,0:T(8,128)(2,1)}), bf16[16,48,768]{2,1,0:T(8,128)(2,1)S(1)}, u32[]{:S(2)}, u32[]{:S(2)}) async-start(bf16[16,48,768]{2,1,0:T(8,128)(2,1)} %get-tuple-element.14), calls=%async_computation.3 | async-start | bytes 2359296 | tf_op jit(solution)/shard_map/all_to_all | solution.py:230
  170.4 42.9 %collective-permute-start.2 = (f32[384,192]{1,0:T(8,128)S(1)}, f32[384,192]{1,0:T(8,128)S(1)}, u32[]{:S(2)}, u32[]{:S(2)}) collective-permute-start(f32[384,192]{1,0:T(8,128)S(1)} %get-tuple-element.13.own_ref), channel_id=1, source_target_pairs={{0,1},{1,0},{2,3},{3,2},{4,5},{5,4},{6,7},{7,6},{8,9},{9,8},{10,11... | collective-permute-start | bytes 884744 | tf_op jit(solution)/shard_map/ppermute | solution.py:203
  209.7 5.0 %collective-permute-start.3 = (f32[384,192]{1,0:T(8,128)S(1)}, f32[384,192]{1,0:T(8,128)S(1)}, u32[]{:S(2)}, u32[]{:S(2)}) collective-permute-start(f32[384,192]{1,0:T(8,128)S(1)} %shard_map.136.own_ref), channel_id=1, source_target_pairs={{0,1},{1,0},{2,3},{3,2},{4,5},{5,4},{6,7},{7,6},{8,9},{9,8},{10,11... | collective-permute-start | bytes 884744 | tf_op jit(solution)/shard_map/ppermute | solution.py:203

commit v2 on v1

v2 whole, which is shorter than its diff:
```python
import itertools

import jax
import jax.numpy as jnp
from jax import lax
from jax.experimental import pallas as pl
from jax.experimental.pallas import tpu as pltpu
from jax.sharding import Mesh, PartitionSpec as P

BLK = 92
HALF = 46
BT = 4
CAP = 8
ROWS = 96
COLS = 48
LANES = 128
SIDE = BT * BLK
WIRE = 768
META = 736
TILES = 16
AXES = ("x", "y_lo", "z", "y_hi", "layer")
BF = jnp.bfloat16
F32 = jnp.float32
VMEM = pl.BlockSpec(memory_space=pltpu.VMEM)
SMEM = pl.BlockSpec(memory_space=pltpu.SMEM)
PARAMS = pltpu.CompilerParams(vmem_limit_bytes=16 * 1024 * 1024)


def dot_nt(a, b):
    return lax.dot_general(a, b, (((1,), (1,)), ((), ())), preferred_element_type=F32)


def one_hot(shape, shift, width):
    q = lax.broadcasted_iota(jnp.int32, shape, 0)
    x = lax.broadcasted_iota(jnp.int32, shape, 1)
    return jnp.where((x == q + shift) & (q < width), 1.0, 0.0).astype(BF)


def code_of(index_ref, count_ref, s):
    return jnp.where(s < count_ref[0, 0], index_ref[0, 0, s] * BT + index_ref[1, 0, s], -1)


def prep_kernel(hidx_ref, hcnt_ref, didx_ref, dcnt_ref, fidx_ref, fcnt_ref, sidx_ref, scnt_ref,
                ham_ref, dens_ref, out_ref):
    layer = lax.axis_index("layer")
    lane = lax.broadcasted_iota(jnp.int32, (ROWS, LANES), 1) - (META - (WIRE - LANES))

    def noted(tail, *lists):
        for n, (index_ref, count_ref) in enumerate(lists):
            for s in range(CAP):
                code = code_of(index_ref, count_ref, s).astype(F32)
                tail = jnp.where(lane == n * CAP + s, code, tail)
        return tail.astype(BF)

    @pl.when(layer == 0)
    def _():
        dens = dens_ref[...]
        r = lax.broadcasted_iota(jnp.int32, (2 * COLS, META), 0)
        x = lax.broadcasted_iota(jnp.int32, (2 * COLS, META), 1)
        q = r % COLS
        pieces = []
        for s in range(CAP):
            pick = (x == q + (r // COLS) * HALF + s * BLK) & (q < HALF)
            pieces.append(dot_nt(jnp.where(pick, 1.0, 0.0).astype(BF), dens))
        pieces.append(jnp.zeros((2 * COLS, WIRE - META), F32))
        wire = jnp.concatenate(pieces, axis=1)
        out_ref[:, 0:WIRE - LANES] = wire[:, 0:WIRE - LANES].astype(BF)
        out_ref[:, WIRE - LANES:] = noted(
            wire[:, WIRE - LANES:], (didx_ref, dcnt_ref), (fidx_ref, fcnt_ref), (sidx_ref, scnt_ref)
        )

    @pl.when(layer == 1)
    def _():
        out_ref[...] = jnp.zeros_like(out_ref)
        out_ref[0:BLK, 0:META] = ham_ref[...]
        tail = out_ref[:, WIRE - LANES:].astype(F32)
        out_ref[:, WIRE - LANES:] = noted(tail, (hidx_ref, hcnt_ref))


def dense_kernel(didx_ref, dcnt_ref, dens_ref, dense_ref):
    layer = lax.axis_index("layer")
    dens = dens_ref[...]
    dense_ref[...] = jnp.zeros_like(dense_ref)
    for s in range(CAP):
        code = code_of(didx_ref, dcnt_ref, s)
        at = jnp.maximum(code, 0)
        i, j = at // BT, at % BT
        x = lax.broadcasted_iota(jnp.int32, (META, BT * COLS), 0)
        y = lax.broadcasted_iota(jnp.int32, (META, BT * COLS), 1) - j * COLS
        spread = jnp.where(
            (x == y + (s * BLK + layer * HALF)) & (y >= 0) & (y < HALF) & (code >= 0), 1.0, 0.0
        ).astype(BF)
        block = jnp.dot(dens, spread, preferred_element_type=F32)
        block = jnp.concatenate([block, jnp.zeros((ROWS - BLK, BT * COLS), F32)], axis=0)
        rows = pl.ds(pl.multiple_of(i * ROWS, ROWS), ROWS)
        dense_ref[rows, :] = dense_ref[rows, :] + block


def ham_kernel(code_ref, own_ref, other_ref, out_ref):
    layer = lax.axis_index("layer")
    out_ref[...] = jnp.zeros_like(out_ref)

    def unpack(from_ref):
        def tile(k, carry):
            wire = from_ref[k]
            for s in range(CAP):
                code = code_ref[k, s]
                at = jnp.maximum(code, 0)
                where = jnp.where(code >= 0, k, TILES)
                rows = pl.ds(pl.multiple_of((at // BT) * ROWS, 16), ROWS)
                lanes = pl.ds(pl.multiple_of((at % BT) * LANES, LANES), BLK)
                out_ref[where, rows, lanes] = wire[:, s * BLK:(s + 1) * BLK]
            return carry

        lax.fori_loop(0, TILES, tile, 0)

    pl.when(layer == 1)(lambda: unpack(own_ref))
    pl.when(layer == 0)(lambda: unpack(other_ref))


def unpack_right(code_ref, wire_ref, right_ref, first_row):
    def tile(k, carry):
        wire = wire_ref[k, pl.ds(first_row, COLS), :]
        row = k // 4 * 4 + k % 2 * 2 + k // 2 % 2
        for s in range(CAP):
            code = code_ref[k, s]
            at = jnp.maximum(code, 0)
            where = jnp.where(code >= 0, row, TILES)
            rows = pl.ds(pl.multiple_of((at % BT) * COLS, 16), COLS)
            lanes = pl.ds(pl.multiple_of((at // BT) * LANES, LANES), BLK)
            right_ref[where, rows, lanes] = wire[:, s * BLK:(s + 1) * BLK]
        return carry

    lax.fori_loop(0, TILES, tile, 0)


def multiply(ham_ref, right_ref):
    def add(n, total):
        for k in range(BT):
            total = total + dot_nt(ham_ref[n * BT + k], right_ref[n * BT + k])
        return total

    return lax.fori_loop(0, TILES // BT, add, jnp.zeros((BT * ROWS, BT * COLS), F32))


def product(ham_ref, code_ref, wire_ref, right_ref):
    right_ref[...] = jnp.zeros_like(right_ref)
    unpack_right(code_ref, wire_ref, right_ref, 0)
    return multiply(ham_ref, right_ref)


def keep(codes, total):
    row = lax.broadcasted_iota(jnp.int32, total.shape, 0) // ROWS
    col = lax.broadcasted_iota(jnp.int32, total.shape, 1) // COLS
    place = row * BT + col
    kept = place == codes[0]
    for s in range(1, CAP):
        kept = kept | (place == codes[s])
    return jnp.where(kept, total, 0.0)


def pack(codes, term, rounded_ref, wire_ref):
    rounded_ref[...] = term.astype(BF)
    pieces = []
    for s in range(CAP):
        at = jnp.maximum(codes[s], 0)
        pick = one_hot((COLS, BT * COLS), (at % BT) * COLS, COLS)
        rows = pl.ds(pl.multiple_of((at // BT) * ROWS, 16), ROWS)
        pieces.append(dot_nt(pick, rounded_ref[rows, :]).astype(BF)[:, 0:BLK])
    pieces.append(jnp.zeros((COLS, WIRE - META), BF))
    wire_ref[...] = jnp.concatenate(pieces, axis=1)


def all_codes(index_ref, count_ref):
    return [code_of(index_ref, count_ref, s) for s in range(CAP)]


def first_kernel(code_ref, index_ref, count_ref, ham_ref, own_ref, other_ref, term_ref, out_ref,
                 right_ref, rounded_ref):
    layer = lax.axis_index("layer")
    right_ref[...] = jnp.zeros_like(right_ref)
    pl.when(layer == 0)(lambda: unpack_right(code_ref, own_ref, right_ref, 0))
    pl.when(layer == 1)(lambda: unpack_right(code_ref, other_ref, right_ref, COLS))
    codes = all_codes(index_ref, count_ref)
    term = keep(codes, multiply(ham_ref, right_ref))
    term_ref[...] = term
    pack(codes, term, rounded_ref, out_ref)


def second_kernel(code_ref, index_ref, count_ref, ham_ref, wire_ref, dense_ref, real_ref, out_ref,
                  right_ref, rounded_ref):
    codes = all_codes(index_ref, count_ref)
    term = keep(codes, product(ham_ref, code_ref, wire_ref, right_ref))
    real_ref[...] = dense_ref[...] - 0.5 * term
    pack(codes, term, rounded_ref, out_ref)


def third_kernel(code_ref, index_ref, count_ref, ham_ref, wire_ref, first_ref, imag_ref, right_ref):
    codes = all_codes(index_ref, count_ref)
    term = keep(codes, product(ham_ref, code_ref, wire_ref, right_ref))
    imag_ref[...] = term / 6.0 - first_ref[...]


def join_kernel(own_ref, other_ref, out_ref):
    swap = lax.axis_index("layer") == 1
    own, other = own_ref[...], other_ref[...]
    low, high = jnp.where(swap, other, own), jnp.where(swap, own, other)
    pieces = []
    for j in range(BT):
        pieces += [low[:, j * COLS:j * COLS + HALF], high[:, j * COLS:j * COLS + HALF]]
    whole = jnp.concatenate(pieces, axis=1)
    for i in range(BT):
        out_ref[i * BLK:(i + 1) * BLK, :] = whole[i * ROWS:i * ROWS + BLK, :]


def call(kernel, scalars, arrays, out_shape, scratch=()):
    return pl.pallas_call(
        kernel,
        out_shape=out_shape,
        in_specs=[SMEM] * len(scalars) + [VMEM] * len(arrays),
        out_specs=jax.tree.map(lambda _: VMEM, out_shape),
        scratch_shapes=list(scratch),
        compiler_params=PARAMS,
    )(*scalars, *arrays)


def shape(*dims, dtype=BF):
    return jax.ShapeDtypeStruct(dims, dtype)


def place(x, y_lo, z, y_hi, layer):
    return (((x * 4 + y_lo) * 8 + z) * 2 + y_hi) * 2 + layer


def everywhere():
    return list(itertools.product(range(4), range(4), range(8), range(2), range(2)))


def pair_route(both):
    route = []
    for x, y_lo, z, y_hi, layer in everywhere():
        to = (x, y_lo, z, 1 - y_hi, layer) if both and layer else (x, y_lo ^ 2, z, y_hi, layer)
        route.append((place(x, y_lo, z, y_hi, layer), place(*to)))
    return route


def groups(both):
    found = {}
    for x, y_lo, z, y_hi, layer in everywhere():
        key = (layer, x, y_lo, y_hi) if both and layer else (layer, y_lo // 2, z, y_hi)
        found.setdefault(key, []).append(place(x, y_lo, z, y_hi, layer))
    return sorted(found.values())


def gather(piece, first, both):
    far = lax.ppermute(piece, AXES, pair_route(both))
    pair = jnp.where(first, jnp.stack([piece, far]), jnp.stack([far, piece]))
    return lax.all_to_all(
        jnp.broadcast_to(pair, (8,) + pair.shape), AXES, 0, 0, axis_index_groups=groups(both)
    )


def swap(values):
    return lax.ppermute(values, "layer", [(0, 1), (1, 0)])


def per_device(ham_blocks, ham_index, ham_count, dens_blocks, dens_index, dens_count, first_index,
               first_count, second_index, second_count, third_index, third_count):
    layer = lax.axis_index("layer")
    y_first = lax.axis_index("y_lo") < 2
    payload = call(
        prep_kernel,
        (ham_index, ham_count, dens_index, dens_count, first_index, first_count, second_index,
         second_count),
        (ham_blocks, dens_blocks),
        shape(ROWS, WIRE),
    )
    first = jnp.where(layer == 0, y_first, lax.axis_index("y_hi") == 0)
    panel = gather(payload, first, True)
    panel = panel.reshape((TILES,) + panel.shape[2:])
    other = swap(panel)
    notes = jnp.stack([panel[:, 0, META:], other[:, 0, META:]])
    ham_note = notes[1 - layer].astype(jnp.int32)
    dens_note = notes[layer].astype(jnp.int32)
    ham = call(
        ham_kernel, (ham_note[:, 0:CAP],), (panel, other), shape(TILES + 1, BT * ROWS, BT * LANES)
    )
    half = shape(BT * ROWS, BT * COLS, dtype=F32)
    dense_half = call(dense_kernel, (dens_index, dens_count), (dens_blocks,), half)
    dense_right = pltpu.VMEM((TILES + 1, BT * COLS, BT * LANES), BF)
    rounded = pltpu.VMEM((BT * ROWS, BT * COLS), BF)
    wire = shape(COLS, WIRE)

    def codes(which):
        return dens_note[:, which * CAP:(which + 1) * CAP]

    def gathered(piece):
        tiles = gather(piece, y_first, False)
        return tiles.reshape((TILES,) + tiles.shape[2:])

    first_term, first_wire = call(
        first_kernel, (codes(0), first_index, first_count), (ham, panel, other), (half, wire),
        [dense_right, rounded],
    )
    real_half, second_wire = call(
        second_kernel, (codes(1), second_index, second_count),
        (ham, gathered(first_wire), dense_half), (half, wire), [dense_right, rounded],
    )
    imag_half = call(
        third_kernel, (codes(2), third_index, third_count),
        (ham, gathered(second_wire), first_term), half, [dense_right],
    )

    def join(part):
        return call(join_kernel, (), (part, swap(part)), shape(SIDE, SIDE, dtype=F32))

    return join(real_half), join(imag_half)


def solution(mesh):
    split = Mesh(mesh.devices.reshape(4, 4, 8, 2, 2), AXES)
    row, col = ("x", "y_lo"), ("z", "y_hi")
    blocks, index = P(row, col), P(None, row, col)
    in_specs = (blocks, index, blocks) * 2 + (index, blocks) * 3
    return jax.shard_map(
        per_device, mesh=split, in_specs=in_specs, out_specs=(blocks, blocks), check_vma=False
    )
```

time: 217 us -> 175 us (0.81)
  waiting for transfers between devices: 82.2 us -> 39 us
  local copies, waits for them, and re-layouts: 3.44 us -> 26.2 us
  Pallas kernels: 45.9 us -> 27 us
  other arithmetic: 4.18 us -> 0.09 us
  blocking collectives: 38.2 us -> 41.6 us
    all_to_all x3 -> x2, waiting for transfers between devices: 80.4 us -> 23.9 us  [gather(): lax.all_to_all(jnp.broadcast_to(pair, (8,) + pair.shape), AXES, 0, 0, axi...]
    pallas_call x7 -> x8, Pallas kernels: 45.9 us -> 27 us  [call(): pl.pallas_call(kernel, out_shape=out_shape, in_specs=[SMEM] * len(scalars...]
    ppermute x4 -> x6, waiting for transfers between devices: 1.81 us -> 15.1 us  [the longest x3 11.3 us: gather(): far = lax.ppermute(piece, AXES, pair_route(both))]
    all_to_all x3 -> x2, starting transfers between devices: 19.1 us -> 7.59 us  [gather(): lax.all_to_all(jnp.broadcast_to(pair, (8,) + pair.shape), AXES, 0, 0, axi...]
    ppermute x4 -> x6, starting transfers between devices: 18.9 us -> 28.5 us  [the longest x3 16.5 us: gather(): far = lax.ppermute(piece, AXES, pair_route(both))]
    unnamed x18 -> x28, local copies, waits for them, and re-layouts: 3.27 us -> 10.4 us
    reshape x0 -> x2, local copies, waits for them, and re-layouts: none -> 5.76 us  [per_device(): panel = panel.reshape((TILES,) + panel.shape[2:])]
    all_to_all x1, blocking collectives: 38.2 us -> 41.6 us  [gather(): lax.all_to_all(jnp.broadcast_to(pair, (8,) + pair.shape), AXES, 0, 0, axi...]
  transfers between devices with their start and end apart: 7 -> 8, of which waited for: 4 -> 6; matrix products, arithmetic and copies ran while one was open for 1% -> 0% of each run, Pallas kernels for 5% -> 5%
where the time goes in v2:
time: 175 us; the launch traced here: 174 us
  blocking collectives  41.6 us (24%)
  waiting for transfers between devices  39 us (22%)
  starting transfers between devices  36.1 us (21%)
  Pallas kernels  27 us (15%)
  local copies, waits for them, and re-layouts  26.2 us (15%)
  between operations  4.13 us (2%)
    all_to_all x1, blocking collectives, gather(): lax.all_to_all(jnp.broadcast_to(pair, (8,) + pair.shape), AXES, 0, 0, axi...  41.6 us
    pallas_call x8, Pallas kernels, call(): pl.pallas_call(kernel, out_shape=out_shape, in_specs=[SMEM] * len(scalars...  27 us
    all_to_all x2, waiting for transfers between devices, gather(): lax.all_to_all(jnp.broadcast_to(pair, (8,) + pair.shape), AXES, 0, 0, axi...  23.9 us
    ppermute x3, starting transfers between devices, gather(): far = lax.ppermute(piece, AXES, pair_route(both))  16.5 us
    ppermute x3, starting transfers between devices, swap(): return lax.ppermute(values, 'layer', [(0, 1), (1, 0)])  12.1 us
    ppermute x3, waiting for transfers between devices, gather(): far = lax.ppermute(piece, AXES, pair_route(both))  11.3 us
    unnamed x28, local copies, waits for them, and re-layouts  10.4 us
    all_to_all x2, starting transfers between devices, gather(): lax.all_to_all(jnp.broadcast_to(pair, (8,) + pair.shape), AXES, 0, 0, axi...  7.59 us
  transfers between devices with their start and end apart: 8, of which 6 were waited for; matrix products, arithmetic and copies ran while one was open for 0% of the time, Pallas kernels for 5%

profile of v2, /device:TPU:1, one launch (start us, length us, event | category | flops | bytes accessed | tf_op | source)
XLA Modules:
  0.0 174.2 jit_solution(2872268900229396162)
XLA Ops:
  3.2 0.0 copy-start.3
  3.2 0.9 copy-done.3
  4.1 0.9 copy-done.5
  5.0 0.7 copy-done.6
  5.7 0.7 copy-done.8
  6.4 0.7 copy-done.10
  7.1 0.7 copy-done.12
  7.8 0.6 shard_map.131
  8.4 8.3 %collective-permute-start = (bf16[96,768]{1,0:T(8,128)(2,1)S(1)}, bf16[96,768]{1,0:T(8,128)(2,1)S(1)}, u32[]{:S(2)}, u32[]{:S(2)}) collective-permute-start(bf16[96,768]{1,0:T(8,128)(2,1)S(1)} %shard_map.131), channel_id=1, source_target_pairs={{0,64},{1,3},{2,66},{3,1},{4,68},{5,7},{6,70},{7,5},{8,72},{9,11},... | collective-permute-start | bytes 442376 | tf_op jit(solution)/shard_map/ppermute | solution.py:256
  16.7 2.6 %collective-permute-done = bf16[96,768]{1,0:T(8,128)(2,1)S(1)} collective-permute-done((bf16[96,768]{1,0:T(8,128)(2,1)S(1)}, bf16[96,768]{1,0:T(8,128)(2,1)S(1)}, u32[]{:S(2)}, u32[]{:S(2)}) %collective-permute-start) | collective-permute-done | bytes 147488 | tf_op jit(solution)/shard_map/ppermute | solution.py:256
  19.4 0.3 copy.19
  19.7 1.2 broadcast_in_dim.9
  20.9 41.6 %all_to_all.15 = bf16[8,2,96,768]{3,1,2,0:T(2,128)(2,1)S(1)} all-to-all(bf16[8,2,96,768]{3,1,2,0:T(2,128)(2,1)S(1)} %broadcast_in_dim.9), channel_id=1, replica_groups={{0,32,128,160,256,288,384,416},{1,5,9,13,17,21,25,29},{2,34,130,162,258..., dimensions={0} | all-to-all | bytes 4718592 | tf_op jit(solution)/shard_map/all_to_all | solution.py:258
  62.5 3.1 %copy.20 = bf16[8,2,96,768]{3,1,0,2:T(2,128)(2,1)} copy(bf16[8,2,96,768]{3,1,2,0:T(2,128)(2,1)S(1)} %all_to_all.15) | data formatting | bytes 4718592 | tf_op jit(solution)/shard_map/all_to_all | solution.py:258
  65.6 5.0 %reshape.17 = bf16[16,96,768]{2,0,1:T(8,128)(2,1)S(1)} reshape(bf16[8,2,96,768]{3,1,0,2:T(2,128)(2,1)} %copy.20) | data formatting | bytes 4718592 | tf_op jit(solution)/shard_map/reshape | solution.py:280
  70.6 1.9 %collective-permute-start.1 = (bf16[16,96,768]{2,0,1:T(8,128)(2,1)S(1)}, bf16[16,96,768]{2,0,1:T(8,128)(2,1)}, u32[]{:S(2)}, u32[]{:S(2)}) collective-permute-start(bf16[16,96,768]{2,0,1:T(8,128)(2,1)S(1)} %reshape.17), channel_id=1, source_target_pairs={{0,1},{1,0},{2,3},{3,2},{4,5},{5,4},{6,7},{7,6},{8,9},{9,8},{10,11... | collective-permute-start | bytes 7077896 | tf_op jit(solution)/shard_map/ppermute | solution.py:264
  72.6 0.7 copy.21.own_ref
  73.3 0.1 slice_bitcast_fusion.1
  73.4 3.8 %collective-permute-done.1 = bf16[16,96,768]{2,0,1:T(8,128)(2,1)} collective-permute-done((bf16[16,96,768]{2,0,1:T(8,128)(2,1)S(1)}, bf16[16,96,768]{2,0,1:T(8,128)(2,1)}, u32[]{:S(2)}, u32[]{:S(2)}) %collective-permute-start.1) | collective-permute-done | bytes 2359328 | tf_op jit(solution)/shard_map/ppermute | solution.py:264
  77.2 0.8 slice_bitcast_fusion
  78.0 0.1 fusion.5
  78.1 2.4 %copy.22.other_ref = bf16[16,96,768]{2,1,0:T(8,128)(2,1)S(1)} copy(bf16[16,96,768]{2,0,1:T(8,128)(2,1)} %collective-permute-done.1) | data formatting | bytes 4718592 | tf_op jit(solution)/shard_map/ppermute | solution.py:264
  80.5 0.0 copy-start.9
  80.5 4.0 %shard_map.132.ham_ref = bf16[17,384,512]{2,1,0:T(8,128)(2,1)S(1)} custom-call(s32[16,8]{1,0:T(8,128)S(1)} %slice_convert_fusion.code_ref, bf16[16,96,768]{2,1,0:T(8,128)(2,1)S(1)} %copy.21.own_ref, bf16[16,96,768]{2,1,0:T(8,128)(2,1)S(1)} %copy.22.other_ref), custom_call_target="tpu_custom_call" | custom-call | tf_op jit(solution)/shard_map/pallas_call | solution.py:217
  84.5 6.1 %shard_map.133 = (f32[384,192]{1,0:T(8,128)S(1)}, bf16[48,768]{1,0:T(8,128)(2,1)S(1)}) custom-call(s32[16,8]{1,0:T(8,128)S(1)} %get-tuple-element.11.code_ref, s32[2,1,8]{2,1,0:T(1,128)S(1)} %copy-done.9, s32[1,1]{1,0:T(1,128)S(6)} %copy.27.fcnt_ref.count_ref, bf16[17,384,512]{2,1,0:T(8,128)(2,1)S(1)} %shard_map.132.ham_ref, ...), custom_call_target="tpu_custom_call" | custom-call | tf_op jit(solution)/shard_map/pallas_call | solution.py:217
  90.7 0.0 copy-start.4
  90.7 0.0 copy-start.7
  90.7 0.0 copy-start.11
  90.7 6.3 %collective-permute-start.2 = (bf16[48,768]{1,0:T(8,128)(2,1)S(1)}, bf16[48,768]{1,0:T(8,128)(2,1)S(1)}, u32[]{:S(2)}, u32[]{:S(2)}) collective-permute-start(bf16[48,768]{1,0:T(8,128)(2,1)S(1)} %get-tuple-element.6), channel_id=1, source_target_pairs={{0,64},{1,65},{2,66},{3,67},{4,68},{5,69},{6,70},{7,71},{8,72},{9,... | collective-permute-start | bytes 221192 | tf_op jit(solution)/shard_map/ppermute | solution.py:256
  97.0 3.8 %collective-permute-done.2 = bf16[48,768]{1,0:T(8,128)(2,1)S(1)} collective-permute-done((bf16[48,768]{1,0:T(8,128)(2,1)S(1)}, bf16[48,768]{1,0:T(8,128)(2,1)S(1)}, u32[]{:S(2)}, u32[]{:S(2)}) %collective-permute-start.2) | collective-permute-done | bytes 73760 | tf_op jit(solution)/shard_map/ppermute | solution.py:256
  100.8 1.1 broadcast_in_dim.10
  101.9 4.0 %all-to-all-start.1 = ((bf16[8,2,48,768]{3,2,1,0:T(8,128)(2,1)}), bf16[8,2,48,768]{3,2,1,0:T(8,128)(2,1)S(1)}, u32[]{:S(2)}, u32[]{:S(2)}) async-start(bf16[8,2,48,768]{3,2,1,0:T(8,128)(2,1)} %broadcast_in_dim.10), calls=%async_computation.1 | async-start | bytes 2359296 | tf_op jit(solution)/shard_map/all_to_all | solution.py:258
  106.0 1.7 shard_map.134.dense_ref
  107.7 14.8 %all-to-all-done.1 = bf16[8,2,48,768]{3,2,1,0:T(8,128)(2,1)S(1)} async-done(((bf16[8,2,48,768]{3,2,1,0:T(8,128)(2,1)}), bf16[8,2,48,768]{3,2,1,0:T(8,128)(2,1)S(1)}, u32[]{:S(2)}, u32[]{:S(2)}) %all-to-all-start.1) | async-done | bytes 1179680 | tf_op jit(solution)/shard_map/all_to_all | solution.py:258
  122.5 2.9 %copy-done.1 = bf16[17,384,512]{2,1,0:T(8,128)(2,1)S(1)} copy-done((bf16[17,384,512]{2,1,0:T(8,128)(2,1)S(1)}, bf16[17,384,512]{2,1,0:T(8,128)(2,1)}, u32[]{:S(2)}) %copy-start.1) | copy-done | bytes 6684696
  125.4 6.1 %shard_map.135 = (f32[384,192]{1,0:T(8,128)S(1)}, bf16[48,768]{1,0:T(8,128)(2,1)S(1)}) custom-call(s32[16,8]{1,0:T(8,128)S(1)} %get-tuple-element.12.code_ref, s32[2,1,8]{2,1,0:T(1,128)S(1)} %copy-done.11, s32[1,1]{1,0:T(1,128)S(6)} %copy.28.scnt_ref.count_ref, bf16[17,384,512]{2,1,0:T(8,128)(2,1)S(1)} %copy-done.1, bf16[16,48,768]{2,1,0:T(8,128)(2,1)S(1)} %bitcast.22, ...), custom_call_target="tpu_custom_call" | custom-call | tf_op jit(solution)/shard_map/pallas_call | solution.py:217
  131.5 0.0 copy-start.13
  131.5 1.9 %collective-permute-start.4 = (bf16[48,768]{1,0:T(8,128)(2,1)S(1)}, bf16[48,768]{1,0:T(8,128)(2,1)S(1)}, u32[]{:S(2)}, u32[]{:S(2)}) collective-permute-start(bf16[48,768]{1,0:T(8,128)(2,1)S(1)} %get-tuple-element.8), channel_id=1, source_target_pairs={{0,64},{1,65},{2,66},{3,67},{4,68},{5,69},{6,70},{7,71},{8,72},{9,... | collective-permute-start | bytes 221192 | tf_op jit(solution)/shard_map/ppermute | solution.py:256
  133.4 4.9 %collective-permute-done.4 = bf16[48,768]{1,0:T(8,128)(2,1)S(1)} collective-permute-done((bf16[48,768]{1,0:T(8,128)(2,1)S(1)}, bf16[48,768]{1,0:T(8,128)(2,1)S(1)}, u32[]{:S(2)}, u32[]{:S(2)}) %collective-permute-start.4) | collective-permute-done | bytes 73760 | tf_op jit(solution)/shard_map/ppermute | solution.py:256
  138.3 1.1 broadcast_in_dim.11
  139.4 3.6 %all-to-all-start.2 = ((bf16[8,2,48,768]{3,2,1,0:T(8,128)(2,1)}), bf16[8,2,48,768]{3,2,1,0:T(8,128)(2,1)S(1)}, u32[]{:S(2)}, u32[]{:S(2)}) async-start(bf16[8,2,48,768]{3,2,1,0:T(8,128)(2,1)} %broadcast_in_dim.11), calls=%async_computation.2 | async-start | bytes 2359296 | tf_op jit(solution)/shard_map/all_to_all | solution.py:258
  143.6 4.6 %collective-permute-start.3 = (f32[384,192]{1,0:T(8,128)S(1)}, f32[384,192]{1,0:T(8,128)S(1)}, u32[]{:S(2)}, u32[]{:S(2)}) collective-permute-start(f32[384,192]{1,0:T(8,128)S(1)} %get-tuple-element.7.own_ref), channel_id=1, source_target_pairs={{0,1},{1,0},{2,3},{3,2},{4,5},{5,4},{6,7},{7,6},{8,9},{9,8},{10,11... | collective-permute-start | bytes 884744 | tf_op jit(solution)/shard_map/ppermute | solution.py:264
  148.3 9.1 %all-to-all-done.2 = bf16[8,2,48,768]{3,2,1,0:T(8,128)(2,1)S(1)} async-done(((bf16[8,2,48,768]{3,2,1,0:T(8,128)(2,1)}), bf16[8,2,48,768]{3,2,1,0:T(8,128)(2,1)S(1)}, u32[]{:S(2)}, u32[]{:S(2)}) %all-to-all-start.2) | async-done | bytes 1179680 | tf_op jit(solution)/shard_map/all_to_all | solution.py:258
  157.4 2.9 %copy-done.2 = bf16[17,384,512]{2,1,0:T(8,128)(2,1)S(1)} copy-done((bf16[17,384,512]{2,1,0:T(8,128)(2,1)S(1)}, bf16[17,384,512]{2,1,0:T(8,128)(2,1)}, u32[]{:S(2)}) %copy-start.2) | copy-done | bytes 6684696
  160.3 5.7 %shard_map.137.own_ref = f32[384,192]{1,0:T(8,128)S(1)} custom-call(s32[16,8]{1,0:T(8,128)S(1)} %get-tuple-element.10.code_ref, s32[2,1,8]{2,1,0:T(1,128)S(1)} %copy-done.13, s32[1,1]{1,0:T(1,128)S(6)} %copy.29.count_ref, bf16[17,384,512]{2,1,0:T(8,128)(2,1)S(1)} %copy-done.2, bf16[16,48,768]{2,1,0:T(8,128)(2,1)S(1)} %bitcast.21, ...), custom_call_target="tpu_custom_call" | custom-call | tf_op jit(solution)/shard_map/pallas_call | solution.py:217
  166.0 5.5 %collective-permute-start.5 = (f32[384,192]{1,0:T(8,128)S(1)}, f32[384,192]{1,0:T(8,128)S(1)}, u32[]{:S(2)}, u32[]{:S(2)}) collective-permute-start(f32[384,192]{1,0:T(8,128)S(1)} %shard_map.137.own_ref), channel_id=1, source_target_pairs={{0,1},{1,0},{2,3},{3,2},{4,5},{5,4},{6,7},{7,6},{8,9},{9,8},{10,11... | collective-permute-start | bytes 884744 | tf_op jit(solution)/shard_map/ppermute | solution.py:264
  171.6 1.3 shard_map.136
  172.9 1.3 shard_map.138
  (21 shorter events, 0.1 us)
Async XLA Ops:
  3.2 0.9 copy-start.3
  4.1 0.9 copy-start.5
  5.0 0.7 copy-start.6
  5.7 0.7 copy-start.8
  6.4 0.7 copy-start.10
  7.1 0.7 copy-start.12
  8.4 10.9 %collective-permute-start = (bf16[96,768]{1,0:T(8,128)(2,1)S(1)}, bf16[96,768]{1,0:T(8,128)(2,1)S(1)}, u32[]{:S(2)}, u32[]{:S(2)}) collective-permute-start(bf16[96,768]{1,0:T(8,128)(2,1)S(1)} %shard_map.131), channel_id=1, source_target_pairs={{0,64},{1,3},{2,66},{3,1},{4,68},{5,7},{6,70},{7,5},{8,72},{9,11},... | collective-permute-start | bytes 442376 | tf_op jit(solution)/shard_map/ppermute | solution.py:256
  70.6 6.6 %collective-permute-start.1 = (bf16[16,96,768]{2,0,1:T(8,128)(2,1)S(1)}, bf16[16,96,768]{2,0,1:T(8,128)(2,1)}, u32[]{:S(2)}, u32[]{:S(2)}) collective-permute-start(bf16[16,96,768]{2,0,1:T(8,128)(2,1)S(1)} %reshape.17), channel_id=1, source_target_pairs={{0,1},{1,0},{2,3},{3,2},{4,5},{5,4},{6,7},{7,6},{8,9},{9,8},{10,11... | collective-permute-start | bytes 7077896 | tf_op jit(solution)/shard_map/ppermute | solution.py:264
  80.5 4.0 %copy-start.9 = (s32[2,1,8]{2,1,0:T(1,128)S(1)}, s32[2,1,8]{2,1,0:T(1,128)}, u32[]{:S(2)}) copy-start(s32[2,1,8]{2,1,0:T(1,128)} %index_ref.3) | copy-start | bytes 196
  84.5 6.2 %copy-start = (bf16[17,384,512]{2,1,0:T(8,128)(2,1)}, bf16[17,384,512]{2,1,0:T(8,128)(2,1)S(1)}, u32[]{:S(2)}) copy-start(bf16[17,384,512]{2,1,0:T(8,128)(2,1)S(1)} %shard_map.132.ham_ref) | copy-start | bytes 20054020
  90.7 15.3 %copy-start.4 = (bf16[92,736]{1,0:T(8,128)(2,1)S(1)}, bf16[92,736]{1,0:T(8,128)(2,1)}, u32[]{:S(2)}) copy-start(bf16[92,736]{1,0:T(8,128)(2,1)} %dens_ref.3) | copy-start | bytes 406276
  90.7 15.3 %copy-start.7 = (s32[2,1,8]{2,1,0:T(1,128)S(1)}, s32[2,1,8]{2,1,0:T(1,128)}, u32[]{:S(2)}) copy-start(s32[2,1,8]{2,1,0:T(1,128)} %didx_ref.3) | copy-start | bytes 196
  90.7 31.8 %copy-start.11 = (s32[2,1,8]{2,1,0:T(1,128)S(1)}, s32[2,1,8]{2,1,0:T(1,128)}, u32[]{:S(2)}) copy-start(s32[2,1,8]{2,1,0:T(1,128)} %index_ref.4) | copy-start | bytes 196
  90.7 10.1 %collective-permute-start.2 = (bf16[48,768]{1,0:T(8,128)(2,1)S(1)}, bf16[48,768]{1,0:T(8,128)(2,1)S(1)}, u32[]{:S(2)}, u32[]{:S(2)}) collective-permute-start(bf16[48,768]{1,0:T(8,128)(2,1)S(1)} %get-tuple-element.6), channel_id=1, source_target_pairs={{0,64},{1,65},{2,66},{3,67},{4,68},{5,69},{6,70},{7,71},{8,72},{9,... | collective-permute-start | bytes 221192 | tf_op jit(solution)/shard_map/ppermute | solution.py:256
  101.9 20.5 %all-to-all-start.1 = ((bf16[8,2,48,768]{3,2,1,0:T(8,128)(2,1)}), bf16[8,2,48,768]{3,2,1,0:T(8,128)(2,1)S(1)}, u32[]{:S(2)}, u32[]{:S(2)}) async-start(bf16[8,2,48,768]{3,2,1,0:T(8,128)(2,1)} %broadcast_in_dim.10), calls=%async_computation.1 | async-start | bytes 2359296 | tf_op jit(solution)/shard_map/all_to_all | solution.py:258
  122.5 2.9 %copy-start.1 = (bf16[17,384,512]{2,1,0:T(8,128)(2,1)S(1)}, bf16[17,384,512]{2,1,0:T(8,128)(2,1)}, u32[]{:S(2)}) copy-start(bf16[17,384,512]{2,1,0:T(8,128)(2,1)} %copy-done) | copy-start | bytes 20054020
  131.5 25.9 %copy-start.13 = (s32[2,1,8]{2,1,0:T(1,128)S(1)}, s32[2,1,8]{2,1,0:T(1,128)}, u32[]{:S(2)}) copy-start(s32[2,1,8]{2,1,0:T(1,128)} %index_ref.5) | copy-start | bytes 196
  131.5 6.8 %collective-permute-start.4 = (bf16[48,768]{1,0:T(8,128)(2,1)S(1)}, bf16[48,768]{1,0:T(8,128)(2,1)S(1)}, u32[]{:S(2)}, u32[]{:S(2)}) collective-permute-start(bf16[48,768]{1,0:T(8,128)(2,1)S(1)} %get-tuple-element.8), channel_id=1, source_target_pairs={{0,64},{1,65},{2,66},{3,67},{4,68},{5,69},{6,70},{7,71},{8,72},{9,... | collective-permute-start | bytes 221192 | tf_op jit(solution)/shard_map/ppermute | solution.py:256
  139.4 18.0 %all-to-all-start.2 = ((bf16[8,2,48,768]{3,2,1,0:T(8,128)(2,1)}), bf16[8,2,48,768]{3,2,1,0:T(8,128)(2,1)S(1)}, u32[]{:S(2)}, u32[]{:S(2)}) async-start(bf16[8,2,48,768]{3,2,1,0:T(8,128)(2,1)} %broadcast_in_dim.11), calls=%async_computation.2 | async-start | bytes 2359296 | tf_op jit(solution)/shard_map/all_to_all | solution.py:258
  143.6 27.9 %collective-permute-start.3 = (f32[384,192]{1,0:T(8,128)S(1)}, f32[384,192]{1,0:T(8,128)S(1)}, u32[]{:S(2)}, u32[]{:S(2)}) collective-permute-start(f32[384,192]{1,0:T(8,128)S(1)} %get-tuple-element.7.own_ref), channel_id=1, source_target_pairs={{0,1},{1,0},{2,3},{3,2},{4,5},{5,4},{6,7},{7,6},{8,9},{9,8},{10,11... | collective-permute-start | bytes 884744 | tf_op jit(solution)/shard_map/ppermute | solution.py:264
  157.4 2.9 %copy-start.2 = (bf16[17,384,512]{2,1,0:T(8,128)(2,1)S(1)}, bf16[17,384,512]{2,1,0:T(8,128)(2,1)}, u32[]{:S(2)}) copy-start(bf16[17,384,512]{2,1,0:T(8,128)(2,1)} %copy-done) | copy-start | bytes 20054020
  166.0 6.9 %collective-permute-start.5 = (f32[384,192]{1,0:T(8,128)S(1)}, f32[384,192]{1,0:T(8,128)S(1)}, u32[]{:S(2)}, u32[]{:S(2)}) collective-permute-start(f32[384,192]{1,0:T(8,128)S(1)} %shard_map.137.own_ref), channel_id=1, source_target_pairs={{0,1},{1,0},{2,3},{3,2},{4,5},{5,4},{6,7},{7,6},{8,9},{9,8},{10,11... | collective-permute-start | bytes 884744 | tf_op jit(solution)/shard_map/ppermute | solution.py:264

commit v3 on v2

--- a/solution.py
+++ b/solution.py
@@ -17,13 +17,14 @@
 SIDE = BT * BLK
 WIRE = 768
 META = 736
+TAIL = WIRE - LANES
 TILES = 16
 AXES = ("x", "y_lo", "z", "y_hi", "layer")
 BF = jnp.bfloat16
 F32 = jnp.float32
 VMEM = pl.BlockSpec(memory_space=pltpu.VMEM)
 SMEM = pl.BlockSpec(memory_space=pltpu.SMEM)
-PARAMS = pltpu.CompilerParams(vmem_limit_bytes=16 * 1024 * 1024)
+HBM = pl.BlockSpec(memory_space=pltpu.HBM)
 
 
 def dot_nt(a, b):
@@ -40,10 +41,18 @@
     return jnp.where(s < count_ref[0, 0], index_ref[0, 0, s] * BT + index_ref[1, 0, s], -1)
 
 
-def prep_kernel(hidx_ref, hcnt_ref, didx_ref, dcnt_ref, fidx_ref, fcnt_ref, sidx_ref, scnt_ref,
-                ham_ref, dens_ref, out_ref):
+def prep_kernel(hidx_hbm, hcnt_ref, didx_hbm, dcnt_ref, fidx_hbm, fcnt_ref, sidx_hbm, scnt_ref,
+                ham_hbm, dens_hbm, out_ref, hidx_ref, didx_ref, fidx_ref, sidx_ref, ham_ref,
+                dens_ref, sems):
+    pairs = ((ham_hbm, ham_ref), (dens_hbm, dens_ref), (hidx_hbm, hidx_ref), (didx_hbm, didx_ref),
+             (fidx_hbm, fidx_ref), (sidx_hbm, sidx_ref))
+    copies = [pltpu.make_async_copy(src, dst, sems.at[n]) for n, (src, dst) in enumerate(pairs)]
+    for one in copies:
+        one.start()
+    for one in copies:
+        one.wait()
     layer = lax.axis_index("layer")
-    lane = lax.broadcasted_iota(jnp.int32, (ROWS, LANES), 1) - (META - (WIRE - LANES))
+    lane = lax.broadcasted_iota(jnp.int32, (ROWS, LANES), 1) - (META - TAIL)
 
     def noted(tail, *lists):
         for n, (index_ref, count_ref) in enumerate(lists):
@@ -64,17 +73,17 @@
             pieces.append(dot_nt(jnp.where(pick, 1.0, 0.0).astype(BF), dens))
         pieces.append(jnp.zeros((2 * COLS, WIRE - META), F32))
         wire = jnp.concatenate(pieces, axis=1)
-        out_ref[:, 0:WIRE - LANES] = wire[:, 0:WIRE - LANES].astype(BF)
-        out_ref[:, WIRE - LANES:] = noted(
-            wire[:, WIRE - LANES:], (didx_ref, dcnt_ref), (fidx_ref, fcnt_ref), (sidx_ref, scnt_ref)
+        out_ref[:, 0:TAIL] = wire[:, 0:TAIL].astype(BF)
+        out_ref[:, TAIL:] = noted(
+            wire[:, TAIL:], (didx_ref, dcnt_ref), (fidx_ref, fcnt_ref), (sidx_ref, scnt_ref)
         )
 
     @pl.when(layer == 1)
     def _():
         out_ref[...] = jnp.zeros_like(out_ref)
         out_ref[0:BLK, 0:META] = ham_ref[...]
-        tail = out_ref[:, WIRE - LANES:].astype(F32)
-        out_ref[:, WIRE - LANES:] = noted(tail, (hidx_ref, hcnt_ref))
+        tail = out_ref[:, TAIL:].astype(F32)
+        out_ref[:, TAIL:] = noted(tail, (hidx_ref, hcnt_ref))
 
 
 def dense_kernel(didx_ref, dcnt_ref, dens_ref, dense_ref):
@@ -96,34 +105,27 @@
         dense_ref[rows, :] = dense_ref[rows, :] + block
 
 
-def ham_kernel(code_ref, own_ref, other_ref, out_ref):
-    layer = lax.axis_index("layer")
-    out_ref[...] = jnp.zeros_like(out_ref)
-
-    def unpack(from_ref):
-        def tile(k, carry):
-            wire = from_ref[k]
-            for s in range(CAP):
-                code = code_ref[k, s]
-                at = jnp.maximum(code, 0)
-                where = jnp.where(code >= 0, k, TILES)
-                rows = pl.ds(pl.multiple_of((at // BT) * ROWS, 16), ROWS)
-                lanes = pl.ds(pl.multiple_of((at % BT) * LANES, LANES), BLK)
-                out_ref[where, rows, lanes] = wire[:, s * BLK:(s + 1) * BLK]
-            return carry
-
-        lax.fori_loop(0, TILES, tile, 0)
-
-    pl.when(layer == 1)(lambda: unpack(own_ref))
-    pl.when(layer == 0)(lambda: unpack(other_ref))
-
-
-def unpack_right(code_ref, wire_ref, right_ref, first_row):
+def unpack_ham(code_ref, from_ref, out_ref):
+    def tile(k, carry):
+        wire = from_ref[k]
+        for s in range(CAP):
+            code = code_ref[k, META - TAIL + s]
+            at = jnp.maximum(code, 0)
+            where = jnp.where(code >= 0, k, TILES)
+            rows = pl.ds(pl.multiple_of((at // BT) * ROWS, 16), ROWS)
+            lanes = pl.ds(pl.multiple_of((at % BT) * LANES, LANES), BLK)
+            out_ref[where, rows, lanes] = wire[:, s * BLK:(s + 1) * BLK]
+        return carry
+
+    lax.fori_loop(0, TILES, tile, 0)
+
+
+def unpack_right(code_ref, which, wire_ref, right_ref, first_row):
     def tile(k, carry):
         wire = wire_ref[k, pl.ds(first_row, COLS), :]
         row = k // 4 * 4 + k % 2 * 2 + k // 2 % 2
         for s in range(CAP):
-            code = code_ref[k, s]
+            code = code_ref[k, META - TAIL + which * CAP + s]
             at = jnp.maximum(code, 0)
             where = jnp.where(code >= 0, row, TILES)
             rows = pl.ds(pl.multiple_of((at % BT) * COLS, 16), COLS)
@@ -134,19 +136,32 @@
     lax.fori_loop(0, TILES, tile, 0)
 
 
-def multiply(ham_ref, right_ref):
-    def add(n, total):
-        for k in range(BT):
-            total = total + dot_nt(ham_ref[n * BT + k], right_ref[n * BT + k])
-        return total
-
-    return lax.fori_loop(0, TILES // BT, add, jnp.zeros((BT * ROWS, BT * COLS), F32))
-
-
-def product(ham_ref, code_ref, wire_ref, right_ref):
+def parts(src_ref, dst_ref, sems):
+    return [
+        pltpu.make_async_copy(
+            src_ref.at[pl.ds(n * BT, BT)], dst_ref.at[pl.ds(n * BT, BT)], sems.at[n]
+        )
+        for n in range(TILES // BT)
+    ]
+
+
+def multiply(ham_ref, right_ref, before=None):
+    total = jnp.zeros((BT * ROWS, BT * COLS), F32)
+    for n in range(TILES // BT):
+        if before:
+            before[n].wait()
+        for k in range(n * BT, (n + 1) * BT):
+            total = total + dot_nt(ham_ref[k], right_ref[k])
+    return total
+
+
+def product(ham_hbm, ham_ref, sems, code_ref, which, wire_ref, right_ref):
+    copies = parts(ham_hbm, ham_ref, sems)
+    for one in copies:
+        one.start()
     right_ref[...] = jnp.zeros_like(right_ref)
-    unpack_right(code_ref, wire_ref, right_ref, 0)
-    return multiply(ham_ref, right_ref)
+    unpack_right(code_ref, which, wire_ref, right_ref, 0)
+    return multiply(ham_ref, right_ref, copies)
 
 
 def keep(codes, total):
@@ -175,29 +190,50 @@
     return [code_of(index_ref, count_ref, s) for s in range(CAP)]
 
 
-def first_kernel(code_ref, index_ref, count_ref, ham_ref, own_ref, other_ref, term_ref, out_ref,
-                 right_ref, rounded_ref):
+def first_kernel(index_ref, count_ref, own_ref, other_ref, ham_out, code_out, term_ref, out_ref,
+                 ham_ref, right_ref, rounded_ref, note_ref, hcode_ref, dcode_ref, sems):
     layer = lax.axis_index("layer")
+    for k in range(TILES):
+        own = own_ref[k, 0:16, TAIL:][0:1].astype(F32).astype(jnp.int32)
+        other = other_ref[k, 0:16, TAIL:][0:1].astype(F32).astype(jnp.int32)
+        note_ref[0, k:k + 1, :] = jnp.where(layer == 0, own, other)
+        note_ref[1, k:k + 1, :] = jnp.where(layer == 0, other, own)
+    code_out[...] = note_ref[0]
+    dens_codes = pltpu.make_async_copy(note_ref.at[0], dcode_ref, sems.at[0])
+    ham_codes = pltpu.make_async_copy(note_ref.at[1], hcode_ref, sems.at[1])
+    dens_codes.start()
+    ham_codes.start()
+    ham_ref[...] = jnp.zeros_like(ham_ref)
     right_ref[...] = jnp.zeros_like(right_ref)
-    pl.when(layer == 0)(lambda: unpack_right(code_ref, own_ref, right_ref, 0))
-    pl.when(layer == 1)(lambda: unpack_right(code_ref, other_ref, right_ref, COLS))
+    dens_codes.wait()
+    ham_codes.wait()
+    pl.when(layer == 1)(lambda: unpack_ham(hcode_ref, own_ref, ham_ref))
+    pl.when(layer == 0)(lambda: unpack_ham(hcode_ref, other_ref, ham_ref))
+    copies = parts(ham_ref, ham_out, sems)
+    for one in copies:
+        one.start()
+    pl.when(layer == 0)(lambda: unpack_right(dcode_ref, 0, own_ref, right_ref, 0))
+    pl.when(layer == 1)(lambda: unpack_right(dcode_ref, 0, other_ref, right_ref, COLS))
     codes = all_codes(index_ref, count_ref)
     term = keep(codes, multiply(ham_ref, right_ref))
     term_ref[...] = term
     pack(codes, term, rounded_ref, out_ref)
-
-
-def second_kernel(code_ref, index_ref, count_ref, ham_ref, wire_ref, dense_ref, real_ref, out_ref,
-                  right_ref, rounded_ref):
+    for one in copies:
+        one.wait()
+
+
+def second_kernel(code_ref, index_ref, count_ref, ham_hbm, wire_ref, dense_ref, real_ref, out_ref,
+                  ham_ref, right_ref, rounded_ref, sems):
     codes = all_codes(index_ref, count_ref)
-    term = keep(codes, product(ham_ref, code_ref, wire_ref, right_ref))
+    term = keep(codes, product(ham_hbm, ham_ref, sems, code_ref, 1, wire_ref, right_ref))
     real_ref[...] = dense_ref[...] - 0.5 * term
     pack(codes, term, rounded_ref, out_ref)
 
 
-def third_kernel(code_ref, index_ref, count_ref, ham_ref, wire_ref, first_ref, imag_ref, right_ref):
+def third_kernel(code_ref, index_ref, count_ref, ham_hbm, wire_ref, first_ref, imag_ref, ham_ref,
+                 right_ref, sems):
     codes = all_codes(index_ref, count_ref)
-    term = keep(codes, product(ham_ref, code_ref, wire_ref, right_ref))
+    term = keep(codes, product(ham_hbm, ham_ref, sems, code_ref, 2, wire_ref, right_ref))
     imag_ref[...] = term / 6.0 - first_ref[...]
 
 
@@ -213,15 +249,15 @@
         out_ref[i * BLK:(i + 1) * BLK, :] = whole[i * ROWS:i * ROWS + BLK, :]
 
 
-def call(kernel, scalars, arrays, out_shape, scratch=()):
+def call(kernel, in_specs, arrays, out_shape, scratch=(), out_specs=None, vmem=24 << 20):
     return pl.pallas_call(
         kernel,
         out_shape=out_shape,
-        in_specs=[SMEM] * len(scalars) + [VMEM] * len(arrays),
-        out_specs=jax.tree.map(lambda _: VMEM, out_shape),
+        in_specs=in_specs,
+        out_specs=out_specs or jax.tree.map(lambda _: VMEM, out_shape),
         scratch_shapes=list(scratch),
-        compiler_params=PARAMS,
-    )(*scalars, *arrays)
+        compiler_params=pltpu.CompilerParams(vmem_limit_bytes=vmem),
+    )(*arrays)
 
 
 def shape(*dims, dtype=BF):
@@ -268,53 +304,65 @@
                first_count, second_index, second_count, third_index, third_count):
     layer = lax.axis_index("layer")
     y_first = lax.axis_index("y_lo") < 2
+    index = pltpu.SMEM((2, 1, CAP), jnp.int32)
+    packed = pltpu.VMEM((BLK, META), BF)
     payload = call(
         prep_kernel,
+        [HBM, SMEM] * 4 + [HBM, HBM],
         (ham_index, ham_count, dens_index, dens_count, first_index, first_count, second_index,
-         second_count),
-        (ham_blocks, dens_blocks),
+         second_count, ham_blocks, dens_blocks),
         shape(ROWS, WIRE),
+        [index] * 4 + [packed, packed, pltpu.SemaphoreType.DMA((6,))],
+        vmem=62900000,
     )
     first = jnp.where(layer == 0, y_first, lax.axis_index("y_hi") == 0)
     panel = gather(payload, first, True)
     panel = panel.reshape((TILES,) + panel.shape[2:])
     other = swap(panel)
-    notes = jnp.stack([panel[:, 0, META:], other[:, 0, META:]])
-    ham_note = notes[1 - layer].astype(jnp.int32)
-    dens_note = notes[layer].astype(jnp.int32)
-    ham = call(
-        ham_kernel, (ham_note[:, 0:CAP],), (panel, other), shape(TILES + 1, BT * ROWS, BT * LANES)
-    )
     half = shape(BT * ROWS, BT * COLS, dtype=F32)
-    dense_half = call(dense_kernel, (dens_index, dens_count), (dens_blocks,), half)
+    dense_half = call(
+        dense_kernel, [SMEM, SMEM, VMEM], (dens_index, dens_count, dens_blocks), half
+    )
+    ham_shape = (TILES + 1, BT * ROWS, BT * LANES)
+    dense_ham = pltpu.VMEM(ham_shape, BF)
     dense_right = pltpu.VMEM((TILES + 1, BT * COLS, BT * LANES), BF)
     rounded = pltpu.VMEM((BT * ROWS, BT * COLS), BF)
+    sems = pltpu.SemaphoreType.DMA((TILES // BT,))
+    code = pltpu.SMEM((TILES, LANES), jnp.int32)
     wire = shape(COLS, WIRE)
-
-    def codes(which):
-        return dens_note[:, which * CAP:(which + 1) * CAP]
 
     def gathered(piece):
         tiles = gather(piece, y_first, False)
         return tiles.reshape((TILES,) + tiles.shape[2:])
 
-    first_term, first_wire = call(
-        first_kernel, (codes(0), first_index, first_count), (ham, panel, other), (half, wire),
-        [dense_right, rounded],
+    ham, codes, first_term, first_wire = call(
+        first_kernel,
+        [SMEM, SMEM, VMEM, VMEM],
+        (first_index, first_count, panel, other),
+        (shape(*ham_shape), shape(TILES, LANES, dtype=jnp.int32), half, wire),
+        [dense_ham, dense_right, rounded, pltpu.VMEM((2, TILES, LANES), jnp.int32), code, code, sems],
+        (HBM, VMEM, VMEM, VMEM),
     )
     real_half, second_wire = call(
-        second_kernel, (codes(1), second_index, second_count),
-        (ham, gathered(first_wire), dense_half), (half, wire), [dense_right, rounded],
-    )
+        second_kernel,
+        [SMEM, SMEM, SMEM, HBM, VMEM, VMEM],
+        (codes, second_index, second_count, ham, gathered(first_wire), dense_half),
+        (half, wire),
+        [dense_ham, dense_right, rounded, sems],
+    )
+    real_part = join(real_half)
     imag_half = call(
-        third_kernel, (codes(2), third_index, third_count),
-        (ham, gathered(second_wire), first_term), half, [dense_right],
-    )
-
-    def join(part):
-        return call(join_kernel, (), (part, swap(part)), shape(SIDE, SIDE, dtype=F32))
-
-    return join(real_half), join(imag_half)
+        third_kernel,
+        [SMEM, SMEM, SMEM, HBM, VMEM, VMEM],
+        (codes, third_index, third_count, ham, gathered(second_wire), first_term),
+        half,
+        [dense_ham, dense_right, sems],
+    )
+    return real_part, join(imag_half)
+
+
+def join(part):
+    return call(join_kernel, [VMEM, VMEM], (part, swap(part)), shape(SIDE, SIDE, dtype=F32))
 
 
 def solution(mesh):

time: 175 us -> 165 us (0.943)
  local copies, waits for them, and re-layouts: 26.2 us -> 11.1 us
  Pallas kernels: 27 us -> 31 us
    reshape x2 -> x0, local copies, waits for them, and re-layouts: 5.76 us -> none  [per_device(): panel = panel.reshape((TILES,) + panel.shape[2:])]
    pallas_call x8 -> x7, Pallas kernels: 27 us -> 31 us  [call(): pl.pallas_call(kernel, out_shape=out_shape, in_specs=in_specs, out_specs=...]
    all_to_all x1 -> x0, local copies, waits for them, and re-layouts: 3.06 us -> none  [gather(): lax.all_to_all(jnp.broadcast_to(pair, (8,) + pair.shape), AXES, 0, 0, axi...]
    ppermute x1 -> x0, local copies, waits for them, and re-layouts: 2.39 us -> none  [swap(): return lax.ppermute(values, 'layer', [(0, 1), (1, 0)])]
    unnamed x28 -> x16, local copies, waits for them, and re-layouts: 10.4 us -> 8.59 us
  transfers between devices with their start and end apart: 8 -> 8, of which waited for: 6 -> 6; matrix products, arithmetic and copies ran while one was open for 0% -> 0% of each run, Pallas kernels for 5% -> 6%
where the time goes in v3:
time: 165 us
  blocking collectives  41.6 us (25%)
  waiting for transfers between devices  40 us (24%)
  starting transfers between devices  36.1 us (22%)
  Pallas kernels  31 us (19%)
  local copies, waits for them, and re-layouts  11.1 us (7%)
  between operations  4.04 us (2%)
    all_to_all x1, blocking collectives, gather(): lax.all_to_all(jnp.broadcast_to(pair, (8,) + pair.shape), AXES, 0, 0, axi...  41.6 us
    pallas_call x7, Pallas kernels, call(): pl.pallas_call(kernel, out_shape=out_shape, in_specs=in_specs, out_specs=...  31 us
    all_to_all x2, waiting for transfers between devices, gather(): lax.all_to_all(jnp.broadcast_to(pair, (8,) + pair.shape), AXES, 0, 0, axi...  23.9 us
    ppermute x3, starting transfers between devices, gather(): far = lax.ppermute(piece, AXES, pair_route(both))  16.4 us
    ppermute x3, starting transfers between devices, swap(): return lax.ppermute(values, 'layer', [(0, 1), (1, 0)])  12.1 us
    ppermute x3, waiting for transfers between devices, gather(): far = lax.ppermute(piece, AXES, pair_route(both))  11.6 us
    unnamed x16, local copies, waits for them, and re-layouts  8.59 us
    all_to_all x2, starting transfers between devices, gather(): lax.all_to_all(jnp.broadcast_to(pair, (8,) + pair.shape), AXES, 0, 0, axi...  7.58 us
  transfers between devices with their start and end apart: 8, of which 6 were waited for; matrix products, arithmetic and copies ran while one was open for 0% of the time, Pallas kernels for 6%

profile of v3, /device:TPU:1, one launch (start us, length us, event | category | flops | bytes accessed | tf_op | source)
XLA Modules:
  0.0 164.8 jit_solution(2772902526358873213)
XLA Ops:
  3.2 1.8 %shard_map.131 = bf16[96,768]{1,0:T(8,128)(2,1)} custom-call(s32[2,1,8]{2,1,0:T(1,128)} %hidx_hbm.1, s32[1,1]{1,0:T(1,128)S(6)} %copy.14.hcnt_ref, s32[2,1,8]{2,1,0:T(1,128)} %didx_ref.1, s32[1,1]{1,0:T(1,128)S(6)} %copy.15.dcnt_ref, s32[2,1,8]{2,1,0:T(1,128)} %index_ref.3, s32[1,1]{1,0:T(1,128)S(6)} %copy.16.fcnt_ref.count_ref, s32[2,1,8]{2,1,0:T(1,128)} %index_ref.4, ...), custom_call_target="tpu_custom_call" | custom-call | tf_op jit(solution)/shard_map/pallas_call | solution.py:253
  5.0 8.3 %collective-permute-start = (bf16[96,768]{1,0:T(8,128)(2,1)}, bf16[96,768]{1,0:T(8,128)(2,1)S(1)}, u32[]{:S(2)}, u32[]{:S(2)}) collective-permute-start(bf16[96,768]{1,0:T(8,128)(2,1)} %shard_map.131), channel_id=1, source_target_pairs={{0,64},{1,3},{2,66},{3,1},{4,68},{5,7},{6,70},{7,5},{8,72},{9,11},... | collective-permute-start | bytes 442376 | tf_op jit(solution)/shard_map/ppermute | solution.py:292
  13.3 2.9 %collective-permute-done = bf16[96,768]{1,0:T(8,128)(2,1)S(1)} collective-permute-done((bf16[96,768]{1,0:T(8,128)(2,1)}, bf16[96,768]{1,0:T(8,128)(2,1)S(1)}, u32[]{:S(2)}, u32[]{:S(2)}) %collective-permute-start) | collective-permute-done | bytes 147488 | tf_op jit(solution)/shard_map/ppermute | solution.py:292
  16.2 1.0 maximum_select_fusion
  17.2 0.2 broadcast_in_dim.9
  17.5 0.0 copy-start.5
  17.5 41.6 %all_to_all.15 = bf16[8,2,96,768]{3,2,1,0:T(8,128)(2,1)S(1)} all-to-all(bf16[8,2,96,768]{3,2,1,0:T(8,128)(2,1)S(1)} %broadcast_in_dim.9), channel_id=1, replica_groups={{0,32,128,160,256,288,384,416},{1,5,9,13,17,21,25,29},{2,34,130,162,258..., dimensions={0} | all-to-all | bytes 4718592 | tf_op jit(solution)/shard_map/all_to_all | solution.py:294
  59.1 1.9 %collective-permute-start.1 = (bf16[16,96,768]{2,1,0:T(8,128)(2,1)S(1)}, bf16[16,96,768]{2,1,0:T(8,128)(2,1)S(1)}, u32[]{:S(2)}, u32[]{:S(2)}) collective-permute-start(bf16[16,96,768]{2,1,0:T(8,128)(2,1)S(1)} %bitcast.9), channel_id=1, source_target_pairs={{0,1},{1,0},{2,3},{3,2},{4,5},{5,4},{6,7},{7,6},{8,9},{9,8},{10,11... | collective-permute-start | bytes 7077896 | tf_op jit(solution)/shard_map/ppermute | solution.py:300
  61.0 4.5 %collective-permute-done.1.other_ref = bf16[16,96,768]{2,1,0:T(8,128)(2,1)S(1)} collective-permute-done((bf16[16,96,768]{2,1,0:T(8,128)(2,1)S(1)}, bf16[16,96,768]{2,1,0:T(8,128)(2,1)S(1)}, u32[]{:S(2)}, u32[]{:S(2)}) %collective-permute-start.1) | collective-permute-done | bytes 2359328 | tf_op jit(solution)/shard_map/ppermute | solution.py:300
  65.5 0.0 copy-done.5
  65.5 9.9 %shard_map.132 = (bf16[17,384,512]{2,1,0:T(8,128)(2,1)S(1)}, s32[16,128]{1,0:T(8,128)S(1)}, f32[384,192]{1,0:T(8,128)S(1)}, bf16[48,768]{1,0:T(8,128)(2,1)S(1)}) custom-call(s32[2,1,8]{2,1,0:T(1,128)S(1)} %copy-done.5, s32[1,1]{1,0:T(1,128)S(6)} %copy.16.fcnt_ref.count_ref, bf16[16,96,768]{2,1,0:T(8,128)(2,1)S(1)} %bitcast.10, ...), custom_call_target="tpu_custom_call" | custom-call | tf_op jit(solution)/shard_map/pallas_call | solution.py:253
  75.4 0.0 copy-start
  75.4 2.8 %copy-done = bf16[17,384,512]{2,1,0:T(8,128)(2,1)} copy-done((bf16[17,384,512]{2,1,0:T(8,128)(2,1)}, bf16[17,384,512]{2,1,0:T(8,128)(2,1)S(1)}, u32[]{:S(2)}) %copy-start) | copy-done | bytes 6684696
  78.2 0.0 copy-start.3
  78.2 0.0 copy-start.4
  78.2 0.0 copy-start.6
  78.2 6.2 %collective-permute-start.2 = (bf16[48,768]{1,0:T(8,128)(2,1)S(1)}, bf16[48,768]{1,0:T(8,128)(2,1)S(1)}, u32[]{:S(2)}, u32[]{:S(2)}) collective-permute-start(bf16[48,768]{1,0:T(8,128)(2,1)S(1)} %get-tuple-element.10), channel_id=1, source_target_pairs={{0,64},{1,65},{2,66},{3,67},{4,68},{5,69},{6,70},{7,71},{8,72},{9,... | collective-permute-start | bytes 221192 | tf_op jit(solution)/shard_map/ppermute | solution.py:292
  84.5 3.8 %collective-permute-done.2 = bf16[48,768]{1,0:T(8,128)(2,1)S(1)} collective-permute-done((bf16[48,768]{1,0:T(8,128)(2,1)S(1)}, bf16[48,768]{1,0:T(8,128)(2,1)S(1)}, u32[]{:S(2)}, u32[]{:S(2)}) %collective-permute-start.2) | collective-permute-done | bytes 73760 | tf_op jit(solution)/shard_map/ppermute | solution.py:292
  88.3 1.1 broadcast_in_dim.10
  89.4 4.0 %all-to-all-start.1 = ((bf16[8,2,48,768]{3,2,1,0:T(8,128)(2,1)}), bf16[8,2,48,768]{3,2,1,0:T(8,128)(2,1)S(1)}, u32[]{:S(2)}, u32[]{:S(2)}) async-start(bf16[8,2,48,768]{3,2,1,0:T(8,128)(2,1)} %broadcast_in_dim.10), calls=%async_computation.1 | async-start | bytes 2359296 | tf_op jit(solution)/shard_map/all_to_all | solution.py:294
  93.5 0.0 copy-done.3
  93.5 0.0 copy-done.4
  93.5 1.7 %shard_map.133.dense_ref = f32[384,192]{1,0:T(8,128)S(1)} custom-call(s32[2,1,8]{2,1,0:T(1,128)S(1)} %copy-done.4, s32[1,1]{1,0:T(1,128)S(6)} %copy.15.dcnt_ref, bf16[92,736]{1,0:T(8,128)(2,1)S(1)} %copy-done.3), custom_call_target="tpu_custom_call" | custom-call | tf_op jit(solution)/shard_map/pallas_call | solution.py:253
  95.2 14.8 %all-to-all-done.1 = bf16[8,2,48,768]{3,2,1,0:T(8,128)(2,1)S(1)} async-done(((bf16[8,2,48,768]{3,2,1,0:T(8,128)(2,1)}), bf16[8,2,48,768]{3,2,1,0:T(8,128)(2,1)S(1)}, u32[]{:S(2)}, u32[]{:S(2)}) %all-to-all-start.1) | async-done | bytes 1179680 | tf_op jit(solution)/shard_map/all_to_all | solution.py:294
  110.0 0.0 copy-done.6
  110.0 0.0 copy-start.1
  110.0 2.9 %copy-done.1 = bf16[17,384,512]{2,1,0:T(8,128)(2,1)S(1)} copy-done((bf16[17,384,512]{2,1,0:T(8,128)(2,1)S(1)}, bf16[17,384,512]{2,1,0:T(8,128)(2,1)}, u32[]{:S(2)}) %copy-start.1) | copy-done | bytes 6684696
  112.9 7.5 %shard_map.134 = (f32[384,192]{1,0:T(8,128)S(1)}, bf16[48,768]{1,0:T(8,128)(2,1)S(1)}) custom-call(s32[16,128]{1,0:T(8,128)S(1)} %get-tuple-element.8.code_ref, s32[2,1,8]{2,1,0:T(1,128)S(1)} %copy-done.6, s32[1,1]{1,0:T(1,128)S(6)} %copy.17.scnt_ref.count_ref, bf16[17,384,512]{2,1,0:T(8,128)(2,1)S(1)} %copy-done.1, bf16[16,48,768]{2,1,0:T(8,128)(2,1)S(1)} %bitcast.12, ...), custom_call_target="tpu_custom_call" | custom-call | tf_op jit(solution)/shard_map/pallas_call | solution.py:253
  120.4 0.0 copy-start.7
  120.5 1.9 %collective-permute-start.4 = (bf16[48,768]{1,0:T(8,128)(2,1)S(1)}, bf16[48,768]{1,0:T(8,128)(2,1)S(1)}, u32[]{:S(2)}, u32[]{:S(2)}) collective-permute-start(bf16[48,768]{1,0:T(8,128)(2,1)S(1)} %get-tuple-element.12), channel_id=1, source_target_pairs={{0,64},{1,65},{2,66},{3,67},{4,68},{5,69},{6,70},{7,71},{8,72},{9,... | collective-permute-start | bytes 221192 | tf_op jit(solution)/shard_map/ppermute | solution.py:292
  122.4 4.9 %collective-permute-done.4 = bf16[48,768]{1,0:T(8,128)(2,1)S(1)} collective-permute-done((bf16[48,768]{1,0:T(8,128)(2,1)S(1)}, bf16[48,768]{1,0:T(8,128)(2,1)S(1)}, u32[]{:S(2)}, u32[]{:S(2)}) %collective-permute-start.4) | collective-permute-done | bytes 73760 | tf_op jit(solution)/shard_map/ppermute | solution.py:292
  127.3 1.1 broadcast_in_dim.11
  128.4 3.6 %all-to-all-start.2 = ((bf16[8,2,48,768]{3,2,1,0:T(8,128)(2,1)}), bf16[8,2,48,768]{3,2,1,0:T(8,128)(2,1)S(1)}, u32[]{:S(2)}, u32[]{:S(2)}) async-start(bf16[8,2,48,768]{3,2,1,0:T(8,128)(2,1)} %broadcast_in_dim.11), calls=%async_computation.2 | async-start | bytes 2359296 | tf_op jit(solution)/shard_map/all_to_all | solution.py:294
  132.6 4.6 %collective-permute-start.3 = (f32[384,192]{1,0:T(8,128)S(1)}, f32[384,192]{1,0:T(8,128)S(1)}, u32[]{:S(2)}, u32[]{:S(2)}) collective-permute-start(f32[384,192]{1,0:T(8,128)S(1)} %get-tuple-element.11.own_ref), channel_id=1, source_target_pairs={{0,1},{1,0},{2,3},{3,2},{4,5},{5,4},{6,7},{7,6},{8,9},{9,8},{10,11... | collective-permute-start | bytes 884744 | tf_op jit(solution)/shard_map/ppermute | solution.py:300
  137.2 9.1 %all-to-all-done.2 = bf16[8,2,48,768]{3,2,1,0:T(8,128)(2,1)S(1)} async-done(((bf16[8,2,48,768]{3,2,1,0:T(8,128)(2,1)}), bf16[8,2,48,768]{3,2,1,0:T(8,128)(2,1)S(1)}, u32[]{:S(2)}, u32[]{:S(2)}) %all-to-all-start.2) | async-done | bytes 1179680 | tf_op jit(solution)/shard_map/all_to_all | solution.py:294
  146.4 0.0 copy-done.7
  146.4 0.0 copy-start.2
  146.4 2.9 %copy-done.2 = bf16[17,384,512]{2,1,0:T(8,128)(2,1)S(1)} copy-done((bf16[17,384,512]{2,1,0:T(8,128)(2,1)S(1)}, bf16[17,384,512]{2,1,0:T(8,128)(2,1)}, u32[]{:S(2)}) %copy-start.2) | copy-done | bytes 6684696
  149.3 7.2 %shard_map.136.own_ref = f32[384,192]{1,0:T(8,128)S(1)} custom-call(s32[16,128]{1,0:T(8,128)S(1)} %get-tuple-element.8.code_ref, s32[2,1,8]{2,1,0:T(1,128)S(1)} %copy-done.7, s32[1,1]{1,0:T(1,128)S(6)} %copy.18.count_ref, bf16[17,384,512]{2,1,0:T(8,128)(2,1)S(1)} %copy-done.2, bf16[16,48,768]{2,1,0:T(8,128)(2,1)S(1)} %bitcast.11, ...), custom_call_target="tpu_custom_call" | custom-call | tf_op jit(solution)/shard_map/pallas_call | solution.py:253
  156.5 5.5 %collective-permute-start.5 = (f32[384,192]{1,0:T(8,128)S(1)}, f32[384,192]{1,0:T(8,128)S(1)}, u32[]{:S(2)}, u32[]{:S(2)}) collective-permute-start(f32[384,192]{1,0:T(8,128)S(1)} %shard_map.136.own_ref), channel_id=1, source_target_pairs={{0,1},{1,0},{2,3},{3,2},{4,5},{5,4},{6,7},{7,6},{8,9},{9,8},{10,11... | collective-permute-start | bytes 884744 | tf_op jit(solution)/shard_map/ppermute | solution.py:300
  162.1 0.0 collective-permute-done.3.other_ref
  162.1 1.3 shard_map.135
  163.4 0.0 collective-permute-done.5.other_ref
  163.4 1.3 shard_map.137
  (2 shorter events, 0.0 us)
Async XLA Ops:
  5.0 11.2 %collective-permute-start = (bf16[96,768]{1,0:T(8,128)(2,1)}, bf16[96,768]{1,0:T(8,128)(2,1)S(1)}, u32[]{:S(2)}, u32[]{:S(2)}) collective-permute-start(bf16[96,768]{1,0:T(8,128)(2,1)} %shard_map.131), channel_id=1, source_target_pairs={{0,64},{1,3},{2,66},{3,1},{4,68},{5,7},{6,70},{7,5},{8,72},{9,11},... | collective-permute-start | bytes 442376 | tf_op jit(solution)/shard_map/ppermute | solution.py:292
  17.5 48.0 %copy-start.5 = (s32[2,1,8]{2,1,0:T(1,128)S(1)}, s32[2,1,8]{2,1,0:T(1,128)}, u32[]{:S(2)}) copy-start(s32[2,1,8]{2,1,0:T(1,128)} %index_ref.3) | copy-start | bytes 196
  59.1 6.4 %collective-permute-start.1 = (bf16[16,96,768]{2,1,0:T(8,128)(2,1)S(1)}, bf16[16,96,768]{2,1,0:T(8,128)(2,1)S(1)}, u32[]{:S(2)}, u32[]{:S(2)}) collective-permute-start(bf16[16,96,768]{2,1,0:T(8,128)(2,1)S(1)} %bitcast.9), channel_id=1, source_target_pairs={{0,1},{1,0},{2,3},{3,2},{4,5},{5,4},{6,7},{7,6},{8,9},{9,8},{10,11... | collective-permute-start | bytes 7077896 | tf_op jit(solution)/shard_map/ppermute | solution.py:300
  75.4 2.8 %copy-start = (bf16[17,384,512]{2,1,0:T(8,128)(2,1)}, bf16[17,384,512]{2,1,0:T(8,128)(2,1)S(1)}, u32[]{:S(2)}) copy-start(bf16[17,384,512]{2,1,0:T(8,128)(2,1)S(1)} %get-tuple-element.9.ham_hbm) | copy-start | bytes 20054020
  78.2 15.3 %copy-start.3 = (bf16[92,736]{1,0:T(8,128)(2,1)S(1)}, bf16[92,736]{1,0:T(8,128)(2,1)}, u32[]{:S(2)}) copy-start(bf16[92,736]{1,0:T(8,128)(2,1)} %dens_ref.1) | copy-start | bytes 406276
  78.2 15.3 %copy-start.4 = (s32[2,1,8]{2,1,0:T(1,128)S(1)}, s32[2,1,8]{2,1,0:T(1,128)}, u32[]{:S(2)}) copy-start(s32[2,1,8]{2,1,0:T(1,128)} %didx_ref.1) | copy-start | bytes 196
  78.2 31.8 %copy-start.6 = (s32[2,1,8]{2,1,0:T(1,128)S(1)}, s32[2,1,8]{2,1,0:T(1,128)}, u32[]{:S(2)}) copy-start(s32[2,1,8]{2,1,0:T(1,128)} %index_ref.4) | copy-start | bytes 196
  78.2 10.1 %collective-permute-start.2 = (bf16[48,768]{1,0:T(8,128)(2,1)S(1)}, bf16[48,768]{1,0:T(8,128)(2,1)S(1)}, u32[]{:S(2)}, u32[]{:S(2)}) collective-permute-start(bf16[48,768]{1,0:T(8,128)(2,1)S(1)} %get-tuple-element.10), channel_id=1, source_target_pairs={{0,64},{1,65},{2,66},{3,67},{4,68},{5,69},{6,70},{7,71},{8,72},{9,... | collective-permute-start | bytes 221192 | tf_op jit(solution)/shard_map/ppermute | solution.py:292
  89.4 20.5 %all-to-all-start.1 = ((bf16[8,2,48,768]{3,2,1,0:T(8,128)(2,1)}), bf16[8,2,48,768]{3,2,1,0:T(8,128)(2,1)S(1)}, u32[]{:S(2)}, u32[]{:S(2)}) async-start(bf16[8,2,48,768]{3,2,1,0:T(8,128)(2,1)} %broadcast_in_dim.10), calls=%async_computation.1 | async-start | bytes 2359296 | tf_op jit(solution)/shard_map/all_to_all | solution.py:294
  110.0 2.9 %copy-start.1 = (bf16[17,384,512]{2,1,0:T(8,128)(2,1)S(1)}, bf16[17,384,512]{2,1,0:T(8,128)(2,1)}, u32[]{:S(2)}) copy-start(bf16[17,384,512]{2,1,0:T(8,128)(2,1)} %copy-done) | copy-start | bytes 20054020
  120.4 25.9 %copy-start.7 = (s32[2,1,8]{2,1,0:T(1,128)S(1)}, s32[2,1,8]{2,1,0:T(1,128)}, u32[]{:S(2)}) copy-start(s32[2,1,8]{2,1,0:T(1,128)} %index_ref.5) | copy-start | bytes 196
  120.5 6.8 %collective-permute-start.4 = (bf16[48,768]{1,0:T(8,128)(2,1)S(1)}, bf16[48,768]{1,0:T(8,128)(2,1)S(1)}, u32[]{:S(2)}, u32[]{:S(2)}) collective-permute-start(bf16[48,768]{1,0:T(8,128)(2,1)S(1)} %get-tuple-element.12), channel_id=1, source_target_pairs={{0,64},{1,65},{2,66},{3,67},{4,68},{5,69},{6,70},{7,71},{8,72},{9,... | collective-permute-start | bytes 221192 | tf_op jit(solution)/shard_map/ppermute | solution.py:292
  128.4 18.0 %all-to-all-start.2 = ((bf16[8,2,48,768]{3,2,1,0:T(8,128)(2,1)}), bf16[8,2,48,768]{3,2,1,0:T(8,128)(2,1)S(1)}, u32[]{:S(2)}, u32[]{:S(2)}) async-start(bf16[8,2,48,768]{3,2,1,0:T(8,128)(2,1)} %broadcast_in_dim.11), calls=%async_computation.2 | async-start | bytes 2359296 | tf_op jit(solution)/shard_map/all_to_all | solution.py:294
  132.6 29.5 %collective-permute-start.3 = (f32[384,192]{1,0:T(8,128)S(1)}, f32[384,192]{1,0:T(8,128)S(1)}, u32[]{:S(2)}, u32[]{:S(2)}) collective-permute-start(f32[384,192]{1,0:T(8,128)S(1)} %get-tuple-element.11.own_ref), channel_id=1, source_target_pairs={{0,1},{1,0},{2,3},{3,2},{4,5},{5,4},{6,7},{7,6},{8,9},{9,8},{10,11... | collective-permute-start | bytes 884744 | tf_op jit(solution)/shard_map/ppermute | solution.py:300
  146.4 2.9 %copy-start.2 = (bf16[17,384,512]{2,1,0:T(8,128)(2,1)S(1)}, bf16[17,384,512]{2,1,0:T(8,128)(2,1)}, u32[]{:S(2)}) copy-start(bf16[17,384,512]{2,1,0:T(8,128)(2,1)} %copy-done) | copy-start | bytes 20054020
  156.5 6.9 %collective-permute-start.5 = (f32[384,192]{1,0:T(8,128)S(1)}, f32[384,192]{1,0:T(8,128)S(1)}, u32[]{:S(2)}, u32[]{:S(2)}) collective-permute-start(f32[384,192]{1,0:T(8,128)S(1)} %shard_map.136.own_ref), channel_id=1, source_target_pairs={{0,1},{1,0},{2,3},{3,2},{4,5},{5,4},{6,7},{7,6},{8,9},{9,8},{10,11... | collective-permute-start | bytes 884744 | tf_op jit(solution)/shard_map/ppermute | solution.py:300

commit v4 on v3

--- a/solution.py
+++ b/solution.py
@@ -230,14 +230,16 @@
     pack(codes, term, rounded_ref, out_ref)
 
 
-def third_kernel(code_ref, index_ref, count_ref, ham_hbm, wire_ref, first_ref, imag_ref, ham_ref,
-                 right_ref, sems):
+def third_kernel(code_ref, index_ref, count_ref, ham_hbm, wire_ref, first_ref, joined_ref, imag_ref,
+                 ham_ref, right_ref, sems):
+    del joined_ref
     codes = all_codes(index_ref, count_ref)
     term = keep(codes, product(ham_hbm, ham_ref, sems, code_ref, 2, wire_ref, right_ref))
     imag_ref[...] = term / 6.0 - first_ref[...]
 
 
-def join_kernel(own_ref, other_ref, out_ref):
+def join_kernel(own_ref, other_ref, out_ref, done_ref):
+    done_ref[...] = jnp.zeros_like(done_ref)
     swap = lax.axis_index("layer") == 1
     own, other = own_ref[...], other_ref[...]
     low, high = jnp.where(swap, other, own), jnp.where(swap, own, other)
@@ -342,6 +344,7 @@
         (shape(*ham_shape), shape(TILES, LANES, dtype=jnp.int32), half, wire),
         [dense_ham, dense_right, rounded, pltpu.VMEM((2, TILES, LANES), jnp.int32), code, code, sems],
         (HBM, VMEM, VMEM, VMEM),
+        vmem=45 << 20,
     )
     real_half, second_wire = call(
         second_kernel,
@@ -349,20 +352,25 @@
         (codes, second_index, second_count, ham, gathered(first_wire), dense_half),
         (half, wire),
         [dense_ham, dense_right, rounded, sems],
-    )
-    real_part = join(real_half)
+        vmem=50 << 20,
+    )
+    real_part, joined = join(real_half)
     imag_half = call(
         third_kernel,
-        [SMEM, SMEM, SMEM, HBM, VMEM, VMEM],
-        (codes, third_index, third_count, ham, gathered(second_wire), first_term),
+        [SMEM, SMEM, SMEM, HBM, VMEM, VMEM, VMEM],
+        (codes, third_index, third_count, ham, gathered(second_wire), first_term, joined),
         half,
         [dense_ham, dense_right, sems],
-    )
-    return real_part, join(imag_half)
+        vmem=50 << 20,
+    )
+    return real_part, join(imag_half)[0]
 
 
 def join(part):
-    return call(join_kernel, [VMEM, VMEM], (part, swap(part)), shape(SIDE, SIDE, dtype=F32))
+    return call(
+        join_kernel, [VMEM, VMEM], (part, swap(part)),
+        (shape(SIDE, SIDE, dtype=F32), shape(8, LANES, dtype=F32)),
+    )
 
 
 def solution(mesh):

time: 165 us -> 155 us (0.939)
  local copies, waits for them, and re-layouts: 11.1 us -> 2.49 us
    unnamed x16 -> x10, local copies, waits for them, and re-layouts: 8.59 us -> 0.03 us
    all_to_all x2, waiting for transfers between devices: 23.9 us -> 21.9 us  [gather(): lax.all_to_all(jnp.broadcast_to(pair, (8,) + pair.shape), AXES, 0, 0, axi...]
    ppermute x3, waiting for transfers between devices: 4.51 us -> 6.51 us  [swap(): return lax.ppermute(values, 'layer', [(0, 1), (1, 0)])]
  transfers between devices with their start and end apart: 8 -> 8, of which waited for: 6 -> 8; matrix products, arithmetic and copies ran while one was open for 0% -> 0% of each run, Pallas kernels for 6% -> 2%
where the time goes in v4:
time: 155 us
  blocking collectives  41.6 us (27%)
  waiting for transfers between devices  40 us (26%)
  starting transfers between devices  36.1 us (23%)
  Pallas kernels  29.7 us (19%)
  between operations  4.04 us (3%)
  local copies, waits for them, and re-layouts  2.49 us (2%)
    all_to_all x1, blocking collectives, gather(): lax.all_to_all(jnp.broadcast_to(pair, (8,) + pair.shape), AXES, 0, 0, axi...  41.6 us
    pallas_call x7, Pallas kernels, call(): pl.pallas_call(kernel, out_shape=out_shape, in_specs=in_specs, out_specs=...  29.7 us
    all_to_all x2, waiting for transfers between devices, gather(): lax.all_to_all(jnp.broadcast_to(pair, (8,) + pair.shape), AXES, 0, 0, axi...  21.9 us
    ppermute x3, starting transfers between devices, gather(): far = lax.ppermute(piece, AXES, pair_route(both))  16.5 us
    ppermute x3, starting transfers between devices, swap(): return lax.ppermute(values, 'layer', [(0, 1), (1, 0)])  12.1 us
    ppermute x3, waiting for transfers between devices, gather(): far = lax.ppermute(piece, AXES, pair_route(both))  11.6 us
    all_to_all x2, starting transfers between devices, gather(): lax.all_to_all(jnp.broadcast_to(pair, (8,) + pair.shape), AXES, 0, 0, axi...  7.58 us
    ppermute x3, waiting for transfers between devices, swap(): return lax.ppermute(values, 'layer', [(0, 1), (1, 0)])  6.51 us
  transfers between devices with their start and end apart: 8, of which 8 were waited for; matrix products, arithmetic and copies ran while one was open for 0% of the time, Pallas kernels for 2%

profile of v4, /device:TPU:1, one launch (start us, length us, event | category | flops | bytes accessed | tf_op | source)
XLA Modules:
  0.0 154.9 jit_solution(5086642175374942725)
XLA Ops:
  3.2 1.8 %shard_map.131 = bf16[96,768]{1,0:T(8,128)(2,1)} custom-call(s32[2,1,8]{2,1,0:T(1,128)} %hidx_hbm.1, s32[1,1]{1,0:T(1,128)S(6)} %copy.14.hcnt_ref, s32[2,1,8]{2,1,0:T(1,128)} %didx_ref.1, s32[1,1]{1,0:T(1,128)S(6)} %copy.15.dcnt_ref, s32[2,1,8]{2,1,0:T(1,128)} %index_ref.3, s32[1,1]{1,0:T(1,128)S(6)} %copy.16.fcnt_ref.count_ref, s32[2,1,8]{2,1,0:T(1,128)} %index_ref.4, ...), custom_call_target="tpu_custom_call" | custom-call | tf_op jit(solution)/shard_map/pallas_call | solution.py:255
  5.0 8.3 %collective-permute-start = (bf16[96,768]{1,0:T(8,128)(2,1)}, bf16[96,768]{1,0:T(8,128)(2,1)S(1)}, u32[]{:S(2)}, u32[]{:S(2)}) collective-permute-start(bf16[96,768]{1,0:T(8,128)(2,1)} %shard_map.131), channel_id=1, source_target_pairs={{0,64},{1,3},{2,66},{3,1},{4,68},{5,7},{6,70},{7,5},{8,72},{9,11},... | collective-permute-start | bytes 442376 | tf_op jit(solution)/shard_map/ppermute | solution.py:294
  13.3 2.9 %collective-permute-done = bf16[96,768]{1,0:T(8,128)(2,1)S(1)} collective-permute-done((bf16[96,768]{1,0:T(8,128)(2,1)}, bf16[96,768]{1,0:T(8,128)(2,1)S(1)}, u32[]{:S(2)}, u32[]{:S(2)}) %collective-permute-start) | collective-permute-done | bytes 147488 | tf_op jit(solution)/shard_map/ppermute | solution.py:294
  16.2 1.0 maximum_select_fusion
  17.2 0.2 broadcast_in_dim.9
  17.5 0.0 copy-start.2
  17.5 41.6 %all_to_all.15 = bf16[8,2,96,768]{3,2,1,0:T(8,128)(2,1)S(1)} all-to-all(bf16[8,2,96,768]{3,2,1,0:T(8,128)(2,1)S(1)} %broadcast_in_dim.9), channel_id=1, replica_groups={{0,32,128,160,256,288,384,416},{1,5,9,13,17,21,25,29},{2,34,130,162,258..., dimensions={0} | all-to-all | bytes 4718592 | tf_op jit(solution)/shard_map/all_to_all | solution.py:296
  59.1 1.9 %collective-permute-start.1 = (bf16[16,96,768]{2,1,0:T(8,128)(2,1)S(1)}, bf16[16,96,768]{2,1,0:T(8,128)(2,1)S(1)}, u32[]{:S(2)}, u32[]{:S(2)}) collective-permute-start(bf16[16,96,768]{2,1,0:T(8,128)(2,1)S(1)} %bitcast.9), channel_id=1, source_target_pairs={{0,1},{1,0},{2,3},{3,2},{4,5},{5,4},{6,7},{7,6},{8,9},{9,8},{10,11... | collective-permute-start | bytes 7077896 | tf_op jit(solution)/shard_map/ppermute | solution.py:302
  61.0 4.5 %collective-permute-done.1.other_ref = bf16[16,96,768]{2,1,0:T(8,128)(2,1)S(1)} collective-permute-done((bf16[16,96,768]{2,1,0:T(8,128)(2,1)S(1)}, bf16[16,96,768]{2,1,0:T(8,128)(2,1)S(1)}, u32[]{:S(2)}, u32[]{:S(2)}) %collective-permute-start.1) | collective-permute-done | bytes 2359328 | tf_op jit(solution)/shard_map/ppermute | solution.py:302
  65.5 0.0 copy-done.2
  65.5 9.5 %shard_map.132 = (bf16[17,384,512]{2,1,0:T(8,128)(2,1)}, s32[16,128]{1,0:T(8,128)S(1)}, f32[384,192]{1,0:T(8,128)S(1)}, bf16[48,768]{1,0:T(8,128)(2,1)S(1)}) custom-call(s32[2,1,8]{2,1,0:T(1,128)S(1)} %copy-done.2, s32[1,1]{1,0:T(1,128)S(6)} %copy.16.fcnt_ref.count_ref, bf16[16,96,768]{2,1,0:T(8,128)(2,1)S(1)} %bitcast.10, ...), custom_call_target="tpu_custom_call" | custom-call | tf_op jit(solution)/shard_map/pallas_call | solution.py:255
  75.0 0.0 copy-start
  75.0 0.0 copy-start.1
  75.0 0.0 copy-start.3
  75.0 6.3 %collective-permute-start.2 = (bf16[48,768]{1,0:T(8,128)(2,1)S(1)}, bf16[48,768]{1,0:T(8,128)(2,1)S(1)}, u32[]{:S(2)}, u32[]{:S(2)}) collective-permute-start(bf16[48,768]{1,0:T(8,128)(2,1)S(1)} %get-tuple-element.13), channel_id=1, source_target_pairs={{0,64},{1,65},{2,66},{3,67},{4,68},{5,69},{6,70},{7,71},{8,72},{9,... | collective-permute-start | bytes 221192 | tf_op jit(solution)/shard_map/ppermute | solution.py:294
  81.3 3.8 %collective-permute-done.2 = bf16[48,768]{1,0:T(8,128)(2,1)S(1)} collective-permute-done((bf16[48,768]{1,0:T(8,128)(2,1)S(1)}, bf16[48,768]{1,0:T(8,128)(2,1)S(1)}, u32[]{:S(2)}, u32[]{:S(2)}) %collective-permute-start.2) | collective-permute-done | bytes 73760 | tf_op jit(solution)/shard_map/ppermute | solution.py:294
  85.1 1.1 broadcast_in_dim.10
  86.3 4.0 %all-to-all-start.1 = ((bf16[8,2,48,768]{3,2,1,0:T(8,128)(2,1)}), bf16[8,2,48,768]{3,2,1,0:T(8,128)(2,1)S(1)}, u32[]{:S(2)}, u32[]{:S(2)}) async-start(bf16[8,2,48,768]{3,2,1,0:T(8,128)(2,1)} %broadcast_in_dim.10), calls=%async_computation.1 | async-start | bytes 2359296 | tf_op jit(solution)/shard_map/all_to_all | solution.py:296
  90.3 0.0 copy-done
  90.3 0.0 copy-done.1
  90.3 1.7 %shard_map.133.dense_ref = f32[384,192]{1,0:T(8,128)S(1)} custom-call(s32[2,1,8]{2,1,0:T(1,128)S(1)} %copy-done.1, s32[1,1]{1,0:T(1,128)S(6)} %copy.15.dcnt_ref, bf16[92,736]{1,0:T(8,128)(2,1)S(1)} %copy-done), custom_call_target="tpu_custom_call" | custom-call | tf_op jit(solution)/shard_map/pallas_call | solution.py:255
  92.0 14.8 %all-to-all-done.1 = bf16[8,2,48,768]{3,2,1,0:T(8,128)(2,1)S(1)} async-done(((bf16[8,2,48,768]{3,2,1,0:T(8,128)(2,1)}), bf16[8,2,48,768]{3,2,1,0:T(8,128)(2,1)S(1)}, u32[]{:S(2)}, u32[]{:S(2)}) %all-to-all-start.1) | async-done | bytes 1179680 | tf_op jit(solution)/shard_map/all_to_all | solution.py:296
  106.8 0.0 copy-done.3
  106.8 7.1 %shard_map.134 = (f32[384,192]{1,0:T(8,128)S(1)}, bf16[48,768]{1,0:T(8,128)(2,1)S(1)}) custom-call(s32[16,128]{1,0:T(8,128)S(1)} %get-tuple-element.11.code_ref, s32[2,1,8]{2,1,0:T(1,128)S(1)} %copy-done.3, s32[1,1]{1,0:T(1,128)S(6)} %copy.17.scnt_ref.count_ref, bf16[17,384,512]{2,1,0:T(8,128)(2,1)} %get-tuple-element.12.ham_hbm, ...), custom_call_target="tpu_custom_call" | custom-call | tf_op jit(solution)/shard_map/pallas_call | solution.py:255
  113.9 1.9 %collective-permute-start.4 = (bf16[48,768]{1,0:T(8,128)(2,1)S(1)}, bf16[48,768]{1,0:T(8,128)(2,1)S(1)}, u32[]{:S(2)}, u32[]{:S(2)}) collective-permute-start(bf16[48,768]{1,0:T(8,128)(2,1)S(1)} %get-tuple-element.16), channel_id=1, source_target_pairs={{0,64},{1,65},{2,66},{3,67},{4,68},{5,69},{6,70},{7,71},{8,72},{9,... | collective-permute-start | bytes 221192 | tf_op jit(solution)/shard_map/ppermute | solution.py:294
  115.9 4.9 %collective-permute-done.4 = bf16[48,768]{1,0:T(8,128)(2,1)S(1)} collective-permute-done((bf16[48,768]{1,0:T(8,128)(2,1)S(1)}, bf16[48,768]{1,0:T(8,128)(2,1)S(1)}, u32[]{:S(2)}, u32[]{:S(2)}) %collective-permute-start.4) | collective-permute-done | bytes 73760 | tf_op jit(solution)/shard_map/ppermute | solution.py:294
  120.7 0.0 copy-start.4
  120.7 1.1 broadcast_in_dim.11
  121.9 3.6 %all-to-all-start.2 = ((bf16[8,2,48,768]{3,2,1,0:T(8,128)(2,1)}), bf16[8,2,48,768]{3,2,1,0:T(8,128)(2,1)S(1)}, u32[]{:S(2)}, u32[]{:S(2)}) async-start(bf16[8,2,48,768]{3,2,1,0:T(8,128)(2,1)} %broadcast_in_dim.11), calls=%async_computation.2 | async-start | bytes 2359296 | tf_op jit(solution)/shard_map/all_to_all | solution.py:296
  125.4 4.6 %collective-permute-start.3 = (f32[384,192]{1,0:T(8,128)S(1)}, f32[384,192]{1,0:T(8,128)S(1)}, u32[]{:S(2)}, u32[]{:S(2)}) collective-permute-start(f32[384,192]{1,0:T(8,128)S(1)} %get-tuple-element.14.own_ref), channel_id=1, source_target_pairs={{0,1},{1,0},{2,3},{3,2},{4,5},{5,4},{6,7},{7,6},{8,9},{9,8},{10,11... | collective-permute-start | bytes 884744 | tf_op jit(solution)/shard_map/ppermute | solution.py:302
  130.7 0.7 collective-permute-done.3.other_ref
  131.4 1.3 shard_map.135
  132.7 7.1 %all-to-all-done.2 = bf16[8,2,48,768]{3,2,1,0:T(8,128)(2,1)S(1)} async-done(((bf16[8,2,48,768]{3,2,1,0:T(8,128)(2,1)}), bf16[8,2,48,768]{3,2,1,0:T(8,128)(2,1)S(1)}, u32[]{:S(2)}, u32[]{:S(2)}) %all-to-all-start.2) | async-done | bytes 1179680 | tf_op jit(solution)/shard_map/all_to_all | solution.py:296
  139.9 0.0 copy-done.4
  139.9 6.8 %shard_map.136.own_ref = f32[384,192]{1,0:T(8,128)S(1)} custom-call(s32[16,128]{1,0:T(8,128)S(1)} %get-tuple-element.11.code_ref, s32[2,1,8]{2,1,0:T(1,128)S(1)} %copy-done.4, s32[1,1]{1,0:T(1,128)S(6)} %copy.18.count_ref, bf16[17,384,512]{2,1,0:T(8,128)(2,1)} %get-tuple-element.12.ham_hbm, bf16[16,48,768]{2,1,0:T(8,128)(2,1)S(1)} %bitcast.11, ...), custom_call_target="tpu_custom_call" | custom-call | tf_op jit(solution)/shard_map/pallas_call | solution.py:255
  146.7 5.5 %collective-permute-start.5 = (f32[384,192]{1,0:T(8,128)S(1)}, f32[384,192]{1,0:T(8,128)S(1)}, u32[]{:S(2)}, u32[]{:S(2)}) collective-permute-start(f32[384,192]{1,0:T(8,128)S(1)} %shard_map.136.own_ref), channel_id=1, source_target_pairs={{0,1},{1,0},{2,3},{3,2},{4,5},{5,4},{6,7},{7,6},{8,9},{9,8},{10,11... | collective-permute-start | bytes 884744 | tf_op jit(solution)/shard_map/ppermute | solution.py:302
  152.2 1.3 collective-permute-done.5.other_ref
  153.5 1.3 shard_map.137
  (2 shorter events, 0.0 us)
Async XLA Ops:
  5.0 11.2 %collective-permute-start = (bf16[96,768]{1,0:T(8,128)(2,1)}, bf16[96,768]{1,0:T(8,128)(2,1)S(1)}, u32[]{:S(2)}, u32[]{:S(2)}) collective-permute-start(bf16[96,768]{1,0:T(8,128)(2,1)} %shard_map.131), channel_id=1, source_target_pairs={{0,64},{1,3},{2,66},{3,1},{4,68},{5,7},{6,70},{7,5},{8,72},{9,11},... | collective-permute-start | bytes 442376 | tf_op jit(solution)/shard_map/ppermute | solution.py:294
  17.5 48.0 %copy-start.2 = (s32[2,1,8]{2,1,0:T(1,128)S(1)}, s32[2,1,8]{2,1,0:T(1,128)}, u32[]{:S(2)}) copy-start(s32[2,1,8]{2,1,0:T(1,128)} %index_ref.3) | copy-start | bytes 196
  59.1 6.4 %collective-permute-start.1 = (bf16[16,96,768]{2,1,0:T(8,128)(2,1)S(1)}, bf16[16,96,768]{2,1,0:T(8,128)(2,1)S(1)}, u32[]{:S(2)}, u32[]{:S(2)}) collective-permute-start(bf16[16,96,768]{2,1,0:T(8,128)(2,1)S(1)} %bitcast.9), channel_id=1, source_target_pairs={{0,1},{1,0},{2,3},{3,2},{4,5},{5,4},{6,7},{7,6},{8,9},{9,8},{10,11... | collective-permute-start | bytes 7077896 | tf_op jit(solution)/shard_map/ppermute | solution.py:302
  75.0 15.3 %copy-start = (bf16[92,736]{1,0:T(8,128)(2,1)S(1)}, bf16[92,736]{1,0:T(8,128)(2,1)}, u32[]{:S(2)}) copy-start(bf16[92,736]{1,0:T(8,128)(2,1)} %dens_ref.1) | copy-start | bytes 406276
  75.0 15.3 %copy-start.1 = (s32[2,1,8]{2,1,0:T(1,128)S(1)}, s32[2,1,8]{2,1,0:T(1,128)}, u32[]{:S(2)}) copy-start(s32[2,1,8]{2,1,0:T(1,128)} %didx_ref.1) | copy-start | bytes 196
  75.0 31.8 %copy-start.3 = (s32[2,1,8]{2,1,0:T(1,128)S(1)}, s32[2,1,8]{2,1,0:T(1,128)}, u32[]{:S(2)}) copy-start(s32[2,1,8]{2,1,0:T(1,128)} %index_ref.4) | copy-start | bytes 196
  75.0 10.1 %collective-permute-start.2 = (bf16[48,768]{1,0:T(8,128)(2,1)S(1)}, bf16[48,768]{1,0:T(8,128)(2,1)S(1)}, u32[]{:S(2)}, u32[]{:S(2)}) collective-permute-start(bf16[48,768]{1,0:T(8,128)(2,1)S(1)} %get-tuple-element.13), channel_id=1, source_target_pairs={{0,64},{1,65},{2,66},{3,67},{4,68},{5,69},{6,70},{7,71},{8,72},{9,... | collective-permute-start | bytes 221192 | tf_op jit(solution)/shard_map/ppermute | solution.py:294
  86.3 20.5 %all-to-all-start.1 = ((bf16[8,2,48,768]{3,2,1,0:T(8,128)(2,1)}), bf16[8,2,48,768]{3,2,1,0:T(8,128)(2,1)S(1)}, u32[]{:S(2)}, u32[]{:S(2)}) async-start(bf16[8,2,48,768]{3,2,1,0:T(8,128)(2,1)} %broadcast_in_dim.10), calls=%async_computation.1 | async-start | bytes 2359296 | tf_op jit(solution)/shard_map/all_to_all | solution.py:296
  113.9 6.8 %collective-permute-start.4 = (bf16[48,768]{1,0:T(8,128)(2,1)S(1)}, bf16[48,768]{1,0:T(8,128)(2,1)S(1)}, u32[]{:S(2)}, u32[]{:S(2)}) collective-permute-start(bf16[48,768]{1,0:T(8,128)(2,1)S(1)} %get-tuple-element.16), channel_id=1, source_target_pairs={{0,64},{1,65},{2,66},{3,67},{4,68},{5,69},{6,70},{7,71},{8,72},{9,... | collective-permute-start | bytes 221192 | tf_op jit(solution)/shard_map/ppermute | solution.py:294
  120.7 19.1 %copy-start.4 = (s32[2,1,8]{2,1,0:T(1,128)S(1)}, s32[2,1,8]{2,1,0:T(1,128)}, u32[]{:S(2)}) copy-start(s32[2,1,8]{2,1,0:T(1,128)} %index_ref.5) | copy-start | bytes 196
  121.9 18.0 %all-to-all-start.2 = ((bf16[8,2,48,768]{3,2,1,0:T(8,128)(2,1)}), bf16[8,2,48,768]{3,2,1,0:T(8,128)(2,1)S(1)}, u32[]{:S(2)}, u32[]{:S(2)}) async-start(bf16[8,2,48,768]{3,2,1,0:T(8,128)(2,1)} %broadcast_in_dim.11), calls=%async_computation.2 | async-start | bytes 2359296 | tf_op jit(solution)/shard_map/all_to_all | solution.py:296
  125.4 6.0 %collective-permute-start.3 = (f32[384,192]{1,0:T(8,128)S(1)}, f32[384,192]{1,0:T(8,128)S(1)}, u32[]{:S(2)}, u32[]{:S(2)}) collective-permute-start(f32[384,192]{1,0:T(8,128)S(1)} %get-tuple-element.14.own_ref), channel_id=1, source_target_pairs={{0,1},{1,0},{2,3},{3,2},{4,5},{5,4},{6,7},{7,6},{8,9},{9,8},{10,11... | collective-permute-start | bytes 884744 | tf_op jit(solution)/shard_map/ppermute | solution.py:302
  146.7 6.9 %collective-permute-start.5 = (f32[384,192]{1,0:T(8,128)S(1)}, f32[384,192]{1,0:T(8,128)S(1)}, u32[]{:S(2)}, u32[]{:S(2)}) collective-permute-start(f32[384,192]{1,0:T(8,128)S(1)} %shard_map.136.own_ref), channel_id=1, source_target_pairs={{0,1},{1,0},{2,3},{3,2},{4,5},{5,4},{6,7},{7,6},{8,9},{9,8},{10,11... | collective-permute-start | bytes 884744 | tf_op jit(solution)/shard_map/ppermute | solution.py:302

commit v5 on v3

--- a/solution.py
+++ b/solution.py
@@ -105,63 +105,46 @@
         dense_ref[rows, :] = dense_ref[rows, :] + block
 
 
-def unpack_ham(code_ref, from_ref, out_ref):
-    def tile(k, carry):
-        wire = from_ref[k]
+def unpack_ham(code_ref, g, from_ref, ham_ref):
+    ham_ref[...] = jnp.zeros_like(ham_ref)
+    for t in range(BT):
+        wire = from_ref[g * BT + t]
         for s in range(CAP):
-            code = code_ref[k, META - TAIL + s]
+            code = code_ref[g * BT + t, META - TAIL + s]
             at = jnp.maximum(code, 0)
-            where = jnp.where(code >= 0, k, TILES)
+            where = jnp.where(code >= 0, t, BT)
             rows = pl.ds(pl.multiple_of((at // BT) * ROWS, 16), ROWS)
             lanes = pl.ds(pl.multiple_of((at % BT) * LANES, LANES), BLK)
-            out_ref[where, rows, lanes] = wire[:, s * BLK:(s + 1) * BLK]
-        return carry
-
-    lax.fori_loop(0, TILES, tile, 0)
-
-
-def unpack_right(code_ref, which, wire_ref, right_ref, first_row):
-    def tile(k, carry):
-        wire = wire_ref[k, pl.ds(first_row, COLS), :]
-        row = k // 4 * 4 + k % 2 * 2 + k // 2 % 2
+            ham_ref[where, rows, lanes] = wire[:, s * BLK:(s + 1) * BLK]
+
+
+def unpack_right(code_ref, which, g, wire_ref, right_ref, first_row=0):
+    right_ref[...] = jnp.zeros_like(right_ref)
+    for t in range(BT):
+        wire = wire_ref[g * BT + t, pl.ds(first_row, COLS), :]
         for s in range(CAP):
-            code = code_ref[k, META - TAIL + which * CAP + s]
+            code = code_ref[g * BT + t, META - TAIL + which * CAP + s]
             at = jnp.maximum(code, 0)
-            where = jnp.where(code >= 0, row, TILES)
+            where = jnp.where(code >= 0, t % 2 * 2 + t // 2, BT)
             rows = pl.ds(pl.multiple_of((at % BT) * COLS, 16), COLS)
             lanes = pl.ds(pl.multiple_of((at // BT) * LANES, LANES), BLK)
             right_ref[where, rows, lanes] = wire[:, s * BLK:(s + 1) * BLK]
-        return carry
-
-    lax.fori_loop(0, TILES, tile, 0)
-
-
-def parts(src_ref, dst_ref, sems):
-    return [
-        pltpu.make_async_copy(
-            src_ref.at[pl.ds(n * BT, BT)], dst_ref.at[pl.ds(n * BT, BT)], sems.at[n]
-        )
-        for n in range(TILES // BT)
-    ]
-
-
-def multiply(ham_ref, right_ref, before=None):
+
+
+def multiply(total, ham_ref, right_ref):
+    for t in range(BT):
+        total = total + dot_nt(ham_ref[t], right_ref[t])
+    return total
+
+
+def product(ham_refs, code_ref, which, wire_ref, right_refs):
     total = jnp.zeros((BT * ROWS, BT * COLS), F32)
-    for n in range(TILES // BT):
-        if before:
-            before[n].wait()
-        for k in range(n * BT, (n + 1) * BT):
-            total = total + dot_nt(ham_ref[k], right_ref[k])
+    unpack_right(code_ref, which, 0, wire_ref, right_refs[0])
+    for g in range(BT):
+        total = multiply(total, ham_refs[g], right_refs[g])
+        if g + 1 < BT:
+            unpack_right(code_ref, which, g + 1, wire_ref, right_refs[g + 1])
     return total
-
-
-def product(ham_hbm, ham_ref, sems, code_ref, which, wire_ref, right_ref):
-    copies = parts(ham_hbm, ham_ref, sems)
-    for one in copies:
-        one.start()
-    right_ref[...] = jnp.zeros_like(right_ref)
-    unpack_right(code_ref, which, wire_ref, right_ref, 0)
-    return multiply(ham_ref, right_ref, copies)
 
 
 def keep(codes, total):
@@ -190,8 +173,10 @@
     return [code_of(index_ref, count_ref, s) for s in range(CAP)]
 
 
-def first_kernel(index_ref, count_ref, own_ref, other_ref, ham_out, code_out, term_ref, out_ref,
-                 ham_ref, right_ref, rounded_ref, note_ref, hcode_ref, dcode_ref, sems):
+def first_kernel(index_ref, count_ref, own_ref, other_ref, dense_ref, *refs):
+    del dense_ref
+    ham_refs, (code_out, term_ref, out_ref), right_refs = refs[0:4], refs[4:7], refs[7:11]
+    rounded_ref, note_ref, hcode_ref, dcode_ref, sems = refs[11:]
     layer = lax.axis_index("layer")
     for k in range(TILES):
         own = own_ref[k, 0:16, TAIL:][0:1].astype(F32).astype(jnp.int32)
@@ -203,58 +188,89 @@
     ham_codes = pltpu.make_async_copy(note_ref.at[1], hcode_ref, sems.at[1])
     dens_codes.start()
     ham_codes.start()
-    ham_ref[...] = jnp.zeros_like(ham_ref)
-    right_ref[...] = jnp.zeros_like(right_ref)
     dens_codes.wait()
     ham_codes.wait()
-    pl.when(layer == 1)(lambda: unpack_ham(hcode_ref, own_ref, ham_ref))
-    pl.when(layer == 0)(lambda: unpack_ham(hcode_ref, other_ref, ham_ref))
-    copies = parts(ham_ref, ham_out, sems)
-    for one in copies:
-        one.start()
-    pl.when(layer == 0)(lambda: unpack_right(dcode_ref, 0, own_ref, right_ref, 0))
-    pl.when(layer == 1)(lambda: unpack_right(dcode_ref, 0, other_ref, right_ref, COLS))
+
+    def unpack(ham_from, dens_from, first_row):
+        for g in range(BT):
+            unpack_right(dcode_ref, 0, g, dens_from, right_refs[g], first_row)
+            unpack_ham(hcode_ref, g, ham_from, ham_refs[g])
+
+    pl.when(layer == 0)(lambda: unpack(other_ref, own_ref, 0))
+    pl.when(layer == 1)(lambda: unpack(own_ref, other_ref, COLS))
+    total = jnp.zeros((BT * ROWS, BT * COLS), F32)
+    for g in range(BT):
+        total = multiply(total, ham_refs[g], right_refs[g])
     codes = all_codes(index_ref, count_ref)
-    term = keep(codes, multiply(ham_ref, right_ref))
+    term = keep(codes, total)
     term_ref[...] = term
     pack(codes, term, rounded_ref, out_ref)
-    for one in copies:
-        one.wait()
-
-
-def second_kernel(code_ref, index_ref, count_ref, ham_hbm, wire_ref, dense_ref, real_ref, out_ref,
-                  ham_ref, right_ref, rounded_ref, sems):
+
+
+def second_kernel(code_ref, index_ref, count_ref, h0, h1, h2, h3, wire_ref, dense_ref, real_ref,
+                  out_ref, r0, r1, r2, r3, rounded_ref):
     codes = all_codes(index_ref, count_ref)
-    term = keep(codes, product(ham_hbm, ham_ref, sems, code_ref, 1, wire_ref, right_ref))
+    term = keep(codes, product((h0, h1, h2, h3), code_ref, 1, wire_ref, (r0, r1, r2, r3)))
     real_ref[...] = dense_ref[...] - 0.5 * term
     pack(codes, term, rounded_ref, out_ref)
 
 
-def third_kernel(code_ref, index_ref, count_ref, ham_hbm, wire_ref, first_ref, imag_ref, ham_ref,
-                 right_ref, sems):
+def third_kernel(code_ref, index_ref, count_ref, h0, h1, h2, h3, wire_ref, first_ref, real_ref,
+                 halves_ref, r0, r1, r2, r3):
     codes = all_codes(index_ref, count_ref)
-    term = keep(codes, product(ham_hbm, ham_ref, sems, code_ref, 2, wire_ref, right_ref))
-    imag_ref[...] = term / 6.0 - first_ref[...]
-
-
-def join_kernel(own_ref, other_ref, out_ref):
+    halves_ref[0] = real_ref[...]
+    term = keep(codes, product((h0, h1, h2, h3), code_ref, 2, wire_ref, (r0, r1, r2, r3)))
+    halves_ref[1] = term / 6.0 - first_ref[...]
+
+
+def join_kernel(own_ref, other_ref, *out_refs):
     swap = lax.axis_index("layer") == 1
-    own, other = own_ref[...], other_ref[...]
-    low, high = jnp.where(swap, other, own), jnp.where(swap, own, other)
-    pieces = []
-    for j in range(BT):
-        pieces += [low[:, j * COLS:j * COLS + HALF], high[:, j * COLS:j * COLS + HALF]]
-    whole = jnp.concatenate(pieces, axis=1)
-    for i in range(BT):
-        out_ref[i * BLK:(i + 1) * BLK, :] = whole[i * ROWS:i * ROWS + BLK, :]
-
-
-def call(kernel, in_specs, arrays, out_shape, scratch=(), out_specs=None, vmem=24 << 20):
+    for n, out_ref in enumerate(out_refs):
+        own, other = own_ref[n], other_ref[n]
+        low, high = jnp.where(swap, other, own), jnp.where(swap, own, other)
+        pieces = []
+        for j in range(BT):
+            pieces += [low[:, j * COLS:j * COLS + HALF], high[:, j * COLS:j * COLS + HALF]]
+        whole = jnp.concatenate(pieces, axis=1)
+        for i in range(BT):
+            out_ref[i * BLK:(i + 1) * BLK, :] = whole[i * ROWS:i * ROWS + BLK, :]
+
+
+def own_place(by_layer):
+    high = lax.axis_index("y_lo") // 2
+    if by_layer:
+        high = jnp.where(lax.axis_index("layer") == 0, high, lax.axis_index("y_hi"))
+    return high
+
+
+def own_kernel(piece_ref, out_ref):
+    at, piece = own_place(True), piece_ref[...]
+    for n in range(out_ref.shape[0]):
+        out_ref[n, at] = piece
+
+
+def far_kernel(far_ref, pairs_ref, out_ref):
+    del pairs_ref
+    at, far = 1 - own_place(True), far_ref[...]
+    for n in range(out_ref.shape[0]):
+        out_ref[n, at] = far
+
+
+def lay_kernel(piece_ref, far_ref, *refs):
+    out_ref = refs[-1]
+    at, piece, far = own_place(False), piece_ref[...], far_ref[...]
+    for n in range(out_ref.shape[0]):
+        out_ref[n, at] = piece
+        out_ref[n, 1 - at] = far
+
+
+def call(kernel, in_specs, arrays, out_shape, scratch=(), alias=None, vmem=24 << 20):
     return pl.pallas_call(
         kernel,
         out_shape=out_shape,
         in_specs=in_specs,
-        out_specs=out_specs or jax.tree.map(lambda _: VMEM, out_shape),
+        out_specs=jax.tree.map(lambda _: VMEM, out_shape),
+        input_output_aliases=alias or {},
         scratch_shapes=list(scratch),
         compiler_params=pltpu.CompilerParams(vmem_limit_bytes=vmem),
     )(*arrays)
@@ -288,12 +304,13 @@
     return sorted(found.values())
 
 
-def gather(piece, first, both):
-    far = lax.ppermute(piece, AXES, pair_route(both))
-    pair = jnp.where(first, jnp.stack([piece, far]), jnp.stack([far, piece]))
-    return lax.all_to_all(
-        jnp.broadcast_to(pair, (8,) + pair.shape), AXES, 0, 0, axis_index_groups=groups(both)
-    )
+def to_pair(piece, both):
+    return lax.ppermute(piece, AXES, pair_route(both))
+
+
+def spread(pairs, both):
+    tiles = lax.all_to_all(pairs, AXES, 0, 0, axis_index_groups=groups(both))
+    return tiles.reshape((TILES,) + tiles.shape[2:])
 
 
 def swap(values):
@@ -302,8 +319,6 @@
 
 def per_device(ham_blocks, ham_index, ham_count, dens_blocks, dens_index, dens_count, first_index,
                first_count, second_index, second_count, third_index, third_count):
-    layer = lax.axis_index("layer")
-    y_first = lax.axis_index("y_lo") < 2
     index = pltpu.SMEM((2, 1, CAP), jnp.int32)
     packed = pltpu.VMEM((BLK, META), BF)
     payload = call(
@@ -315,54 +330,52 @@
         [index] * 4 + [packed, packed, pltpu.SemaphoreType.DMA((6,))],
         vmem=62900000,
     )
-    first = jnp.where(layer == 0, y_first, lax.axis_index("y_hi") == 0)
-    panel = gather(payload, first, True)
-    panel = panel.reshape((TILES,) + panel.shape[2:])
-    other = swap(panel)
+    pairs = call(own_kernel, [VMEM], (payload,), shape(8, 2, ROWS, WIRE))
+    pairs = call(
+        far_kernel, [VMEM] * 2, (to_pair(payload, True), pairs), shape(8, 2, ROWS, WIRE),
+        alias={1: 0},
+    )
+    panel = spread(pairs, True)
     half = shape(BT * ROWS, BT * COLS, dtype=F32)
     dense_half = call(
         dense_kernel, [SMEM, SMEM, VMEM], (dens_index, dens_count, dens_blocks), half
     )
-    ham_shape = (TILES + 1, BT * ROWS, BT * LANES)
-    dense_ham = pltpu.VMEM(ham_shape, BF)
-    dense_right = pltpu.VMEM((TILES + 1, BT * COLS, BT * LANES), BF)
+    dense_ham = shape(BT + 1, BT * ROWS, BT * LANES)
+    dense_right = [pltpu.VMEM((BT + 1, BT * COLS, BT * LANES), BF)] * BT
     rounded = pltpu.VMEM((BT * ROWS, BT * COLS), BF)
-    sems = pltpu.SemaphoreType.DMA((TILES // BT,))
     code = pltpu.SMEM((TILES, LANES), jnp.int32)
-    wire = shape(COLS, WIRE)
-
-    def gathered(piece):
-        tiles = gather(piece, y_first, False)
-        return tiles.reshape((TILES,) + tiles.shape[2:])
-
-    ham, codes, first_term, first_wire = call(
+    wire, wires = shape(COLS, WIRE), shape(8, 2, COLS, WIRE)
+    *ham, codes, first_term, first_wire = call(
         first_kernel,
-        [SMEM, SMEM, VMEM, VMEM],
-        (first_index, first_count, panel, other),
-        (shape(*ham_shape), shape(TILES, LANES, dtype=jnp.int32), half, wire),
-        [dense_ham, dense_right, rounded, pltpu.VMEM((2, TILES, LANES), jnp.int32), code, code, sems],
-        (HBM, VMEM, VMEM, VMEM),
-    )
+        [SMEM] * 2 + [VMEM] * 3,
+        (first_index, first_count, panel, swap(panel), dense_half),
+        (dense_ham,) * BT + (shape(TILES, LANES, dtype=jnp.int32), half, wire),
+        dense_right + [rounded, pltpu.VMEM((2, TILES, LANES), jnp.int32), code, code,
+                       pltpu.SemaphoreType.DMA((2,))],
+    )
+    pairs = call(lay_kernel, [VMEM] * 2, (first_wire, to_pair(first_wire, False)), wires)
     real_half, second_wire = call(
         second_kernel,
-        [SMEM, SMEM, SMEM, HBM, VMEM, VMEM],
-        (codes, second_index, second_count, ham, gathered(first_wire), dense_half),
+        [SMEM] * 3 + [VMEM] * 6,
+        (codes, second_index, second_count, *ham, spread(pairs, False), dense_half),
         (half, wire),
-        [dense_ham, dense_right, rounded, sems],
-    )
-    real_part = join(real_half)
-    imag_half = call(
+        dense_right + [rounded],
+    )
+    pairs = call(
+        lay_kernel,
+        [VMEM, VMEM, SMEM],
+        (second_wire, to_pair(second_wire, False), third_count),
+        wires,
+    )
+    halves = call(
         third_kernel,
-        [SMEM, SMEM, SMEM, HBM, VMEM, VMEM],
-        (codes, third_index, third_count, ham, gathered(second_wire), first_term),
-        half,
-        [dense_ham, dense_right, sems],
-    )
-    return real_part, join(imag_half)
-
-
-def join(part):
-    return call(join_kernel, [VMEM, VMEM], (part, swap(part)), shape(SIDE, SIDE, dtype=F32))
+        [SMEM] * 3 + [VMEM] * 7,
+        (codes, third_index, third_count, *ham, spread(pairs, False), first_term, real_half),
+        shape(2, BT * ROWS, BT * COLS, dtype=F32),
+        dense_right,
+    )
+    whole = shape(SIDE, SIDE, dtype=F32)
+    return call(join_kernel, [VMEM] * 2, (halves, swap(halves)), (whole, whole))
 
 
 def solution(mesh):

time: 165 us -> 143 us (0.87)
  blocking collectives: 41.6 us -> 78.7 us
  waiting for transfers between devices: 40 us -> 13.5 us
  starting transfers between devices: 36.1 us -> 24.5 us
  Pallas kernels: 31 us -> 20.6 us
  local copies, waits for them, and re-layouts: 11.1 us -> 1.45 us
    all_to_all x1 -> x3, blocking collectives: 41.6 us -> 78.7 us  [spread(): tiles = lax.all_to_all(pairs, AXES, 0, 0, axis_index_groups=groups(both))]
    all_to_all x2 -> x0, waiting for transfers between devices: 23.9 us -> none  [gather(): lax.all_to_all(jnp.broadcast_to(pair, (8,) + pair.shape), AXES, 0, 0, axi...]
    pallas_call x7 -> x10, Pallas kernels: 31 us -> 20.6 us  [call(): pl.pallas_call(kernel, out_shape=out_shape, in_specs=in_specs, out_specs=...]
    unnamed x16 -> x12, local copies, waits for them, and re-layouts: 8.59 us -> 0.95 us
    all_to_all x2 -> x0, starting transfers between devices: 7.58 us -> none  [gather(): lax.all_to_all(jnp.broadcast_to(pair, (8,) + pair.shape), AXES, 0, 0, axi...]
    ppermute x3 -> x2, starting transfers between devices: 12.1 us -> 8.11 us  [swap(): return lax.ppermute(values, 'layer', [(0, 1), (1, 0)])]
    broadcast_in_dim x3 -> x0, local copies, waits for them, and re-layouts: 2.46 us -> none  [gather(): jnp.broadcast_to(pair, (8,) + pair.shape)]
    ppermute x3, waiting for transfers between devices: 11.6 us -> 9.15 us  [to_pair(): return lax.ppermute(piece, AXES, pair_route(both))]
  transfers between devices with their start and end apart: 8 -> 5, of which waited for: 6 -> 5; matrix products, arithmetic and copies ran while one was open for 0% -> 0% of each run, Pallas kernels for 6% -> 1%
where the time goes in v5:
time: 143 us
  blocking collectives  78.7 us (55%)
  starting transfers between devices  24.5 us (17%)
  Pallas kernels  20.6 us (14%)
  waiting for transfers between devices  13.5 us (9%)
  between operations  4.04 us (3%)
  local copies, waits for them, and re-layouts  1.45 us (1%)
    all_to_all x3, blocking collectives, spread(): tiles = lax.all_to_all(pairs, AXES, 0, 0, axis_index_groups=groups(both))  78.7 us
    pallas_call x10, Pallas kernels, call(): pl.pallas_call(kernel, out_shape=out_shape, in_specs=in_specs, out_specs=...  20.6 us
    ppermute x3, starting transfers between devices, to_pair(): return lax.ppermute(piece, AXES, pair_route(both))  16.3 us
    ppermute x3, waiting for transfers between devices, to_pair(): return lax.ppermute(piece, AXES, pair_route(both))  9.15 us
    ppermute x2, starting transfers between devices, swap(): return lax.ppermute(values, 'layer', [(0, 1), (1, 0)])  8.11 us
    ppermute x2, waiting for transfers between devices, swap(): return lax.ppermute(values, 'layer', [(0, 1), (1, 0)])  4.34 us
  transfers between devices with their start and end apart: 5, of which 5 were waited for; matrix products, arithmetic and copies ran while one was open for 0% of the time, Pallas kernels for 1%

profile of v5, /device:TPU:1, one launch (start us, length us, event | category | flops | bytes accessed | tf_op | source)
XLA Modules:
  0.0 142.7 jit_solution(16596875011959203726)
XLA Ops:
  3.2 1.8 %shard_map.131.piece_ref = bf16[96,768]{1,0:T(8,128)(2,1)} custom-call(s32[2,1,8]{2,1,0:T(1,128)} %hidx_hbm.1, s32[1,1]{1,0:T(1,128)S(6)} %copy.18.hcnt_ref, s32[2,1,8]{2,1,0:T(1,128)} %didx_ref.1, s32[1,1]{1,0:T(1,128)S(6)} %copy.19.dcnt_ref, s32[2,1,8]{2,1,0:T(1,128)} %index_ref.3, s32[1,1]{1,0:T(1,128)S(6)} %copy.20.fcnt_ref.count_ref, ...), custom_call_target="tpu_custom_call" | custom-call | tf_op jit(solution)/shard_map/pallas_call | solution.py:268
  5.0 8.3 %collective-permute-start = (bf16[96,768]{1,0:T(8,128)(2,1)}, bf16[96,768]{1,0:T(8,128)(2,1)S(1)}, u32[]{:S(2)}, u32[]{:S(2)}) collective-permute-start(bf16[96,768]{1,0:T(8,128)(2,1)} %shard_map.131.piece_ref), channel_id=1, source_target_pairs={{0,64},{1,3},{2,66},{3,1},{4,68},{5,7},{6,70},{7,5},{8,72},{9,11},... | collective-permute-start | bytes 442376 | tf_op jit(solution)/shard_map/ppermute | solution.py:308
  13.3 0.0 copy-start
  13.3 0.9 copy-done
  14.2 0.1 shard_map.132.pairs_ref
  14.3 1.9 %collective-permute-done.far_ref = bf16[96,768]{1,0:T(8,128)(2,1)S(1)} collective-permute-done((bf16[96,768]{1,0:T(8,128)(2,1)}, bf16[96,768]{1,0:T(8,128)(2,1)S(1)}, u32[]{:S(2)}, u32[]{:S(2)}) %collective-permute-start) | collective-permute-done | bytes 147488 | tf_op jit(solution)/shard_map/ppermute | solution.py:308
  16.2 0.1 shard_map.133
  16.3 0.0 copy-start.1
  16.3 0.0 copy-start.2
  16.3 0.0 copy-start.3
  16.3 41.7 %all_to_all.15 = bf16[8,2,96,768]{3,2,1,0:T(8,128)(2,1)S(1)} all-to-all(bf16[8,2,96,768]{3,2,1,0:T(8,128)(2,1)S(1)} %shard_map.133), channel_id=1, replica_groups={{0,32,128,160,256,288,384,416},{1,5,9,13,17,21,25,29},{2,34,130,162,258..., dimensions={0} | all-to-all | bytes 4718592 | tf_op jit(solution)/shard_map/all_to_all | solution.py:312
  58.0 1.9 %collective-permute-start.1 = (bf16[16,96,768]{2,1,0:T(8,128)(2,1)S(1)}, bf16[16,96,768]{2,1,0:T(8,128)(2,1)S(1)}, u32[]{:S(2)}, u32[]{:S(2)}) collective-permute-start(bf16[16,96,768]{2,1,0:T(8,128)(2,1)S(1)} %bitcast.3), channel_id=1, source_target_pairs={{0,1},{1,0},{2,3},{3,2},{4,5},{5,4},{6,7},{7,6},{8,9},{9,8},{10,11... | collective-permute-start | bytes 7077896 | tf_op jit(solution)/shard_map/ppermute | solution.py:317
  60.0 0.0 copy-done.1
  60.0 0.0 copy-done.2
  60.0 1.7 %shard_map.134.dense_ref = f32[384,192]{1,0:T(8,128)S(1)} custom-call(s32[2,1,8]{2,1,0:T(1,128)S(1)} %copy-done.2, s32[1,1]{1,0:T(1,128)S(6)} %copy.19.dcnt_ref, bf16[92,736]{1,0:T(8,128)(2,1)S(1)} %copy-done.1), custom_call_target="tpu_custom_call" | custom-call | tf_op jit(solution)/shard_map/pallas_call | solution.py:268
  61.7 2.7 %collective-permute-done.1.other_ref = bf16[16,96,768]{2,1,0:T(8,128)(2,1)S(1)} collective-permute-done((bf16[16,96,768]{2,1,0:T(8,128)(2,1)S(1)}, bf16[16,96,768]{2,1,0:T(8,128)(2,1)S(1)}, u32[]{:S(2)}, u32[]{:S(2)}) %collective-permute-start.1) | collective-permute-done | bytes 2359328 | tf_op jit(solution)/shard_map/ppermute | solution.py:317
  64.5 0.0 copy-done.3
  64.5 7.4 %shard_map.135 = (bf16[5,384,512]{2,1,0:T(8,128)(2,1)S(1)}, bf16[5,384,512]{2,1,0:T(8,128)(2,1)S(1)}, bf16[5,384,512]{2,1,0:T(8,128)(2,1)S(1)}, bf16[5,384,512]{...) custom-call(s32[2,1,8]{2,1,0:T(1,128)S(1)} %copy-done.3, ...), custom_call_target="tpu_custom_call" | custom-call | tf_op jit(solution)/shard_map/pallas_call | solution.py:268
  71.8 0.0 copy-start.4
  71.8 6.1 %collective-permute-start.2 = (bf16[48,768]{1,0:T(8,128)(2,1)S(1)}, bf16[48,768]{1,0:T(8,128)(2,1)S(1)}, u32[]{:S(2)}, u32[]{:S(2)}) collective-permute-start(bf16[48,768]{1,0:T(8,128)(2,1)S(1)} %get-tuple-element.16.piece_ref), channel_id=1, source_target_pairs={{0,64},{1,65},{2,66},{3,67},{4,68},{5,69},{6,70},{7,71},{8,72},{9,... | collective-permute-start | bytes 221192 | tf_op jit(solution)/shard_map/ppermute | solution.py:308
  78.0 3.8 %collective-permute-done.2.far_ref = bf16[48,768]{1,0:T(8,128)(2,1)S(1)} collective-permute-done((bf16[48,768]{1,0:T(8,128)(2,1)S(1)}, bf16[48,768]{1,0:T(8,128)(2,1)S(1)}, u32[]{:S(2)}, u32[]{:S(2)}) %collective-permute-start.2) | collective-permute-done | bytes 73760 | tf_op jit(solution)/shard_map/ppermute | solution.py:308
  81.8 0.1 shard_map.136
  81.9 20.1 %all_to_all.16 = bf16[8,2,48,768]{3,2,1,0:T(8,128)(2,1)S(1)} all-to-all(bf16[8,2,48,768]{3,2,1,0:T(8,128)(2,1)S(1)} %shard_map.136), channel_id=1, replica_groups={{0,32,128,160,256,288,384,416},{1,33,129,161,257,289,385,417},{2,34,130..., dimensions={0} | all-to-all | bytes 2359296 | tf_op jit(solution)/shard_map/all_to_all | solution.py:312
  102.0 0.0 copy-done.4
  102.0 4.0 %shard_map.137 = (f32[384,192]{1,0:T(8,128)S(1)}, bf16[48,768]{1,0:T(8,128)(2,1)S(1)}) custom-call(s32[16,128]{1,0:T(8,128)S(1)} %get-tuple-element.11.code_ref, s32[2,1,8]{2,1,0:T(1,128)S(1)} %copy-done.4, s32[1,1]{1,0:T(1,128)S(6)} %copy.21.scnt_ref.count_ref, bf16[5,384,512]{2,1,0:T(8,128)(2,1)S(1)} %get-tuple-element.12.h0, ...), custom_call_target="tpu_custom_call" | custom-call | tf_op jit(solution)/shard_map/pallas_call | solution.py:268
  106.1 0.0 copy-start.5
  106.1 1.9 %collective-permute-start.3 = (bf16[48,768]{1,0:T(8,128)(2,1)S(1)}, bf16[48,768]{1,0:T(8,128)(2,1)S(1)}, u32[]{:S(2)}, u32[]{:S(2)}) collective-permute-start(bf16[48,768]{1,0:T(8,128)(2,1)S(1)} %get-tuple-element.17.piece_ref), channel_id=1, source_target_pairs={{0,64},{1,65},{2,66},{3,67},{4,68},{5,69},{6,70},{7,71},{8,72},{9,... | collective-permute-start | bytes 221192 | tf_op jit(solution)/shard_map/ppermute | solution.py:308
  108.6 3.4 %collective-permute-done.3.far_ref = bf16[48,768]{1,0:T(8,128)(2,1)S(1)} collective-permute-done((bf16[48,768]{1,0:T(8,128)(2,1)S(1)}, bf16[48,768]{1,0:T(8,128)(2,1)S(1)}, u32[]{:S(2)}, u32[]{:S(2)}) %collective-permute-start.3) | collective-permute-done | bytes 73760 | tf_op jit(solution)/shard_map/ppermute | solution.py:308
  112.1 0.1 shard_map.138
  112.2 16.8 %all_to_all.17 = bf16[8,2,48,768]{3,2,1,0:T(8,128)(2,1)S(1)} all-to-all(bf16[8,2,48,768]{3,2,1,0:T(8,128)(2,1)S(1)} %shard_map.138), channel_id=1, replica_groups={{0,32,128,160,256,288,384,416},{1,33,129,161,257,289,385,417},{2,34,130..., dimensions={0} | all-to-all | bytes 2359296 | tf_op jit(solution)/shard_map/all_to_all | solution.py:312
  129.0 0.0 copy-done.5
  129.0 3.6 %shard_map.139.own_ref = f32[2,384,192]{2,1,0:T(8,128)S(1)} custom-call(s32[16,128]{1,0:T(8,128)S(1)} %get-tuple-element.11.code_ref, s32[2,1,8]{2,1,0:T(1,128)S(1)} %copy-done.5, s32[1,1]{1,0:T(1,128)S(6)} %copy.22.refs_0_.count_ref, bf16[5,384,512]{2,1,0:T(8,128)(2,1)S(1)} %get-tuple-element.12.h0, bf16[5,384,512]{2,1,0:T(8,128)(2,1)S(1)} %get-tuple-element.13.h1, ...), custom_call_target="tpu_custom_call" | custom-call | tf_op jit(solution)/shard_map/pallas_call | solution.py:268
  132.5 0.2 copy.15
  132.8 6.2 %collective-permute-start.4 = (f32[2,384,192]{1,2,0:T(8,128)S(1)}, f32[2,384,192]{1,2,0:T(8,128)S(1)}, u32[]{:S(2)}, u32[]{:S(2)}) collective-permute-start(f32[2,384,192]{1,2,0:T(8,128)S(1)} %copy.15), channel_id=1, source_target_pairs={{0,1},{1,0},{2,3},{3,2},{4,5},{5,4},{6,7},{7,6},{8,9},{9,8},{10,11... | collective-permute-start | bytes 1769480 | tf_op jit(solution)/shard_map/ppermute | solution.py:317
  139.0 1.6 %collective-permute-done.4 = f32[2,384,192]{1,2,0:T(8,128)S(1)} collective-permute-done((f32[2,384,192]{1,2,0:T(8,128)S(1)}, f32[2,384,192]{1,2,0:T(8,128)S(1)}, u32[]{:S(2)}, u32[]{:S(2)}) %collective-permute-start.4) | collective-permute-done | bytes 589856 | tf_op jit(solution)/shard_map/ppermute | solution.py:317
  140.6 0.3 copy.16.other_ref
  140.9 1.8 %shard_map.140 = (f32[368,368]{1,0:T(8,128)}, f32[368,368]{1,0:T(8,128)}) custom-call(f32[2,384,192]{2,1,0:T(8,128)S(1)} %shard_map.139.own_ref, f32[2,384,192]{2,1,0:T(8,128)S(1)} %copy.16.other_ref), custom_call_target="tpu_custom_call" | custom-call | tf_op jit(solution)/shard_map/pallas_call | solution.py:268
Async XLA Ops:
  5.0 11.2 %collective-permute-start = (bf16[96,768]{1,0:T(8,128)(2,1)}, bf16[96,768]{1,0:T(8,128)(2,1)S(1)}, u32[]{:S(2)}, u32[]{:S(2)}) collective-permute-start(bf16[96,768]{1,0:T(8,128)(2,1)} %shard_map.131.piece_ref), channel_id=1, source_target_pairs={{0,64},{1,3},{2,66},{3,1},{4,68},{5,7},{6,70},{7,5},{8,72},{9,11},... | collective-permute-start | bytes 442376 | tf_op jit(solution)/shard_map/ppermute | solution.py:308
  13.3 0.9 copy-start
  16.3 43.7 %copy-start.1 = (bf16[92,736]{1,0:T(8,128)(2,1)S(1)}, bf16[92,736]{1,0:T(8,128)(2,1)}, u32[]{:S(2)}) copy-start(bf16[92,736]{1,0:T(8,128)(2,1)} %dens_ref.1) | copy-start | bytes 406276
  16.3 43.7 %copy-start.2 = (s32[2,1,8]{2,1,0:T(1,128)S(1)}, s32[2,1,8]{2,1,0:T(1,128)}, u32[]{:S(2)}) copy-start(s32[2,1,8]{2,1,0:T(1,128)} %didx_ref.1) | copy-start | bytes 196
  16.3 48.1 %copy-start.3 = (s32[2,1,8]{2,1,0:T(1,128)S(1)}, s32[2,1,8]{2,1,0:T(1,128)}, u32[]{:S(2)}) copy-start(s32[2,1,8]{2,1,0:T(1,128)} %index_ref.3) | copy-start | bytes 196
  58.0 6.4 %collective-permute-start.1 = (bf16[16,96,768]{2,1,0:T(8,128)(2,1)S(1)}, bf16[16,96,768]{2,1,0:T(8,128)(2,1)S(1)}, u32[]{:S(2)}, u32[]{:S(2)}) collective-permute-start(bf16[16,96,768]{2,1,0:T(8,128)(2,1)S(1)} %bitcast.3), channel_id=1, source_target_pairs={{0,1},{1,0},{2,3},{3,2},{4,5},{5,4},{6,7},{7,6},{8,9},{9,8},{10,11... | collective-permute-start | bytes 7077896 | tf_op jit(solution)/shard_map/ppermute | solution.py:317
  71.8 30.2 %copy-start.4 = (s32[2,1,8]{2,1,0:T(1,128)S(1)}, s32[2,1,8]{2,1,0:T(1,128)}, u32[]{:S(2)}) copy-start(s32[2,1,8]{2,1,0:T(1,128)} %index_ref.4) | copy-start | bytes 196
  71.8 10.0 %collective-permute-start.2 = (bf16[48,768]{1,0:T(8,128)(2,1)S(1)}, bf16[48,768]{1,0:T(8,128)(2,1)S(1)}, u32[]{:S(2)}, u32[]{:S(2)}) collective-permute-start(bf16[48,768]{1,0:T(8,128)(2,1)S(1)} %get-tuple-element.16.piece_ref), channel_id=1, source_target_pairs={{0,64},{1,65},{2,66},{3,67},{4,68},{5,69},{6,70},{7,71},{8,72},{9,... | collective-permute-start | bytes 221192 | tf_op jit(solution)/shard_map/ppermute | solution.py:308
  106.1 22.9 %copy-start.5 = (s32[2,1,8]{2,1,0:T(1,128)S(1)}, s32[2,1,8]{2,1,0:T(1,128)}, u32[]{:S(2)}) copy-start(s32[2,1,8]{2,1,0:T(1,128)} %index_ref.5) | copy-start | bytes 196
  106.1 6.0 %collective-permute-start.3 = (bf16[48,768]{1,0:T(8,128)(2,1)S(1)}, bf16[48,768]{1,0:T(8,128)(2,1)S(1)}, u32[]{:S(2)}, u32[]{:S(2)}) collective-permute-start(bf16[48,768]{1,0:T(8,128)(2,1)S(1)} %get-tuple-element.17.piece_ref), channel_id=1, source_target_pairs={{0,64},{1,65},{2,66},{3,67},{4,68},{5,69},{6,70},{7,71},{8,72},{9,... | collective-permute-start | bytes 221192 | tf_op jit(solution)/shard_map/ppermute | solution.py:308
  132.8 7.8 %collective-permute-start.4 = (f32[2,384,192]{1,2,0:T(8,128)S(1)}, f32[2,384,192]{1,2,0:T(8,128)S(1)}, u32[]{:S(2)}, u32[]{:S(2)}) collective-permute-start(f32[2,384,192]{1,2,0:T(8,128)S(1)} %copy.15), channel_id=1, source_target_pairs={{0,1},{1,0},{2,3},{3,2},{4,5},{5,4},{6,7},{7,6},{8,9},{9,8},{10,11... | collective-permute-start | bytes 1769480 | tf_op jit(solution)/shard_map/ppermute | solution.py:317

commit v6 on v5

--- a/solution.py
+++ b/solution.py
@@ -86,7 +86,8 @@
         out_ref[:, TAIL:] = noted(tail, (hidx_ref, hcnt_ref))
 
 
-def dense_kernel(didx_ref, dcnt_ref, dens_ref, dense_ref):
+def dense_kernel(didx_ref, dcnt_ref, dens_ref, after_ref, dense_ref):
+    del after_ref
     layer = lax.axis_index("layer")
     dens = dens_ref[...]
     dense_ref[...] = jnp.zeros_like(dense_ref)
@@ -173,36 +174,57 @@
     return [code_of(index_ref, count_ref, s) for s in range(CAP)]
 
 
-def first_kernel(index_ref, count_ref, own_ref, other_ref, dense_ref, *refs):
-    del dense_ref
-    ham_refs, (code_out, term_ref, out_ref), right_refs = refs[0:4], refs[4:7], refs[7:11]
-    rounded_ref, note_ref, hcode_ref, dcode_ref, sems = refs[11:]
+def read_codes(panel_ref, note_ref, code_ref, sem):
+    for k in range(TILES):
+        note_ref[k:k + 1, :] = panel_ref[k, 0:16, TAIL:][0:1].astype(F32).astype(jnp.int32)
+    copy = pltpu.make_async_copy(note_ref, code_ref, sem)
+    copy.start()
+    copy.wait()
+
+
+def local_kernel(panel_ref, *refs):
+    ham_refs, right_refs, (own_note, note_ref, code_ref, sem) = refs[0:4], refs[4:8], refs[8:]
     layer = lax.axis_index("layer")
-    for k in range(TILES):
-        own = own_ref[k, 0:16, TAIL:][0:1].astype(F32).astype(jnp.int32)
-        other = other_ref[k, 0:16, TAIL:][0:1].astype(F32).astype(jnp.int32)
-        note_ref[0, k:k + 1, :] = jnp.where(layer == 0, own, other)
-        note_ref[1, k:k + 1, :] = jnp.where(layer == 0, other, own)
-    code_out[...] = note_ref[0]
-    dens_codes = pltpu.make_async_copy(note_ref.at[0], dcode_ref, sems.at[0])
-    ham_codes = pltpu.make_async_copy(note_ref.at[1], hcode_ref, sems.at[1])
-    dens_codes.start()
-    ham_codes.start()
-    dens_codes.wait()
-    ham_codes.wait()
-
-    def unpack(ham_from, dens_from, first_row):
+    read_codes(panel_ref, note_ref, code_ref, sem)
+    own_note[...] = note_ref[...]
+
+    @pl.when(layer == 0)
+    def _():
         for g in range(BT):
-            unpack_right(dcode_ref, 0, g, dens_from, right_refs[g], first_row)
-            unpack_ham(hcode_ref, g, ham_from, ham_refs[g])
-
-    pl.when(layer == 0)(lambda: unpack(other_ref, own_ref, 0))
-    pl.when(layer == 1)(lambda: unpack(own_ref, other_ref, COLS))
-    total = jnp.zeros((BT * ROWS, BT * COLS), F32)
-    for g in range(BT):
-        total = multiply(total, ham_refs[g], right_refs[g])
+            unpack_right(code_ref, 0, g, panel_ref, right_refs[g])
+
+    @pl.when(layer == 1)
+    def _():
+        for g in range(BT):
+            unpack_ham(code_ref, g, panel_ref, ham_refs[g])
+
+
+def first_kernel(index_ref, count_ref, other_ref, own_note, *refs):
+    ham_refs, right_refs, (code_out, term_ref, out_ref) = refs[8:12], refs[12:16], refs[16:19]
+    total_ref, rounded_ref, note_ref, code_ref, sem = refs[19:]
+    layer = lax.axis_index("layer")
+    read_codes(other_ref, note_ref, code_ref, sem)
+    code_out[...] = jnp.where(layer == 0, own_note[...], note_ref[...])
+
+    def pipelined(unpack):
+        total = jnp.zeros((BT * ROWS, BT * COLS), F32)
+        unpack(0)
+        for g in range(BT):
+            total = multiply(total, ham_refs[g], right_refs[g])
+            if g + 1 < BT:
+                unpack(g + 1)
+        total_ref[...] = total
+
+    @pl.when(layer == 0)
+    def _():
+        pipelined(lambda g: unpack_ham(code_ref, g, other_ref, ham_refs[g]))
+
+    @pl.when(layer == 1)
+    def _():
+        pipelined(lambda g: unpack_right(code_ref, 0, g, other_ref, right_refs[g], COLS))
+
     codes = all_codes(index_ref, count_ref)
-    term = keep(codes, total)
+    term = keep(codes, total_ref[...])
     term_ref[...] = term
     pack(codes, term, rounded_ref, out_ref)
 
@@ -218,15 +240,25 @@
 def third_kernel(code_ref, index_ref, count_ref, h0, h1, h2, h3, wire_ref, first_ref, real_ref,
                  halves_ref, r0, r1, r2, r3):
     codes = all_codes(index_ref, count_ref)
-    halves_ref[0] = real_ref[...]
     term = keep(codes, product((h0, h1, h2, h3), code_ref, 2, wire_ref, (r0, r1, r2, r3)))
-    halves_ref[1] = term / 6.0 - first_ref[...]
+    rows = BT * ROWS
+    real, imag = real_ref[...], term / 6.0 - first_ref[...]
+    halves_ref[0:rows] = real[:, 0:LANES]
+    halves_ref[rows:2 * rows] = imag[:, 0:LANES]
+    halves_ref[2 * rows:3 * rows] = jnp.concatenate([real[:, LANES:], imag[:, LANES:]], axis=1)
 
 
 def join_kernel(own_ref, other_ref, *out_refs):
     swap = lax.axis_index("layer") == 1
+    rows, rest = BT * ROWS, BT * COLS - LANES
     for n, out_ref in enumerate(out_refs):
-        own, other = own_ref[n], other_ref[n]
+        own, other = (
+            jnp.concatenate(
+                [ref[n * rows:(n + 1) * rows], ref[2 * rows:3 * rows][:, n * rest:(n + 1) * rest]],
+                axis=1,
+            )
+            for ref in (own_ref, other_ref)
+        )
         low, high = jnp.where(swap, other, own), jnp.where(swap, own, other)
         pieces = []
         for j in range(BT):
@@ -330,30 +362,40 @@
         [index] * 4 + [packed, packed, pltpu.SemaphoreType.DMA((6,))],
         vmem=62900000,
     )
+    half = shape(BT * ROWS, BT * COLS, dtype=F32)
     pairs = call(own_kernel, [VMEM], (payload,), shape(8, 2, ROWS, WIRE))
     pairs = call(
         far_kernel, [VMEM] * 2, (to_pair(payload, True), pairs), shape(8, 2, ROWS, WIRE),
         alias={1: 0},
     )
     panel = spread(pairs, True)
-    half = shape(BT * ROWS, BT * COLS, dtype=F32)
-    dense_half = call(
-        dense_kernel, [SMEM, SMEM, VMEM], (dens_index, dens_count, dens_blocks), half
-    )
     dense_ham = shape(BT + 1, BT * ROWS, BT * LANES)
     dense_right = [pltpu.VMEM((BT + 1, BT * COLS, BT * LANES), BF)] * BT
     rounded = pltpu.VMEM((BT * ROWS, BT * COLS), BF)
     code = pltpu.SMEM((TILES, LANES), jnp.int32)
     wire, wires = shape(COLS, WIRE), shape(8, 2, COLS, WIRE)
-    *ham, codes, first_term, first_wire = call(
+    note = shape(TILES, LANES, dtype=jnp.int32)
+    reading = [pltpu.VMEM((TILES, LANES), jnp.int32), code, pltpu.SemaphoreType.DMA]
+    made = (dense_ham,) * BT + (shape(BT + 1, BT * COLS, BT * LANES),) * BT
+    *unpacked, own_note = call(local_kernel, [VMEM], (panel,), made + (note,), reading)
+    out = call(
         first_kernel,
-        [SMEM] * 2 + [VMEM] * 3,
-        (first_index, first_count, panel, swap(panel), dense_half),
-        (dense_ham,) * BT + (shape(TILES, LANES, dtype=jnp.int32), half, wire),
-        dense_right + [rounded, pltpu.VMEM((2, TILES, LANES), jnp.int32), code, code,
-                       pltpu.SemaphoreType.DMA((2,))],
-    )
-    pairs = call(lay_kernel, [VMEM] * 2, (first_wire, to_pair(first_wire, False)), wires)
+        [SMEM] * 2 + [VMEM] * 10,
+        (first_index, first_count, swap(panel), own_note, *unpacked),
+        made + (note, half, wire),
+        [pltpu.VMEM((BT * ROWS, BT * COLS), F32), rounded] + reading,
+        alias={4 + n: n for n in range(8)},
+    )
+    ham, (codes, first_term, first_wire) = out[0:4], out[8:]
+    dense_half = call(
+        dense_kernel, [SMEM, SMEM, VMEM, VMEM], (dens_index, dens_count, dens_blocks, codes), half
+    )
+    pairs = call(
+        lay_kernel,
+        [VMEM] * 3,
+        (first_wire, to_pair(first_wire, False), dense_half),
+        wires,
+    )
     real_half, second_wire = call(
         second_kernel,
         [SMEM] * 3 + [VMEM] * 6,
@@ -371,7 +413,7 @@
         third_kernel,
         [SMEM] * 3 + [VMEM] * 7,
         (codes, third_index, third_count, *ham, spread(pairs, False), first_term, real_half),
-        shape(2, BT * ROWS, BT * COLS, dtype=F32),
+        shape(3 * BT * ROWS, LANES, dtype=F32),
         dense_right,
     )
     whole = shape(SIDE, SIDE, dtype=F32)

time: 143 us -> 140 us (0.979)
  waiting for transfers between devices: 13.5 us -> 10.6 us
    ppermute x3, waiting for transfers between devices: 9.15 us -> 7.55 us  [to_pair(): return lax.ppermute(piece, AXES, pair_route(both))]
    pallas_call x10 -> x11, Pallas kernels: 20.6 us -> 21.2 us  [call(): pl.pallas_call(kernel, out_shape=out_shape, in_specs=in_specs, out_specs=...]
  transfers between devices with their start and end apart: 5 -> 5, of which waited for: 5 -> 5; matrix products, arithmetic and copies ran while one was open for 0% -> 0% of each run, Pallas kernels for 1% -> 3%
where the time goes in v6:
time: 140 us
  blocking collectives  78.2 us (56%)
  starting transfers between devices  24.7 us (18%)
  Pallas kernels  21.2 us (15%)
  waiting for transfers between devices  10.6 us (8%)
  between operations  4 us (3%)
    all_to_all x3, blocking collectives, spread(): tiles = lax.all_to_all(pairs, AXES, 0, 0, axis_index_groups=groups(both))  78.2 us
    pallas_call x11, Pallas kernels, call(): pl.pallas_call(kernel, out_shape=out_shape, in_specs=in_specs, out_specs=...  21.2 us
    ppermute x3, starting transfers between devices, to_pair(): return lax.ppermute(piece, AXES, pair_route(both))  16.5 us
    ppermute x2, starting transfers between devices, swap(): return lax.ppermute(values, 'layer', [(0, 1), (1, 0)])  8.15 us
    ppermute x3, waiting for transfers between devices, to_pair(): return lax.ppermute(piece, AXES, pair_route(both))  7.55 us
    ppermute x2, waiting for transfers between devices, swap(): return lax.ppermute(values, 'layer', [(0, 1), (1, 0)])  3.08 us
  transfers between devices with their start and end apart: 5, of which 5 were waited for; matrix products, arithmetic and copies ran while one was open for 0% of the time, Pallas kernels for 3%

profile of v6, /device:TPU:1, one launch (start us, length us, event | category | flops | bytes accessed | tf_op | source)
XLA Modules:
  0.0 139.6 jit_solution(6777216194807323125)
XLA Ops:
  3.2 1.8 %shard_map.131.piece_ref = bf16[96,768]{1,0:T(8,128)(2,1)} custom-call(s32[2,1,8]{2,1,0:T(1,128)} %hidx_hbm.1, s32[1,1]{1,0:T(1,128)S(6)} %copy.32.hcnt_ref, s32[2,1,8]{2,1,0:T(1,128)} %didx_ref.1, s32[1,1]{1,0:T(1,128)S(6)} %copy.33.dcnt_ref, s32[2,1,8]{2,1,0:T(1,128)} %index_ref.3, s32[1,1]{1,0:T(1,128)S(6)} %copy.34.fcnt_ref.count_ref, ...), custom_call_target="tpu_custom_call" | custom-call | tf_op jit(solution)/shard_map/pallas_call | solution.py:300
  5.0 8.3 %collective-permute-start = (bf16[96,768]{1,0:T(8,128)(2,1)}, bf16[96,768]{1,0:T(8,128)(2,1)S(1)}, u32[]{:S(2)}, u32[]{:S(2)}) collective-permute-start(bf16[96,768]{1,0:T(8,128)(2,1)} %shard_map.131.piece_ref), channel_id=1, source_target_pairs={{0,64},{1,3},{2,66},{3,1},{4,68},{5,7},{6,70},{7,5},{8,72},{9,11},... | collective-permute-start | bytes 442376 | tf_op jit(solution)/shard_map/ppermute | solution.py:340
  13.3 0.0 copy-start
  13.3 0.9 copy-done
  14.2 0.1 shard_map.132.pairs_ref
  14.3 1.9 %collective-permute-done.far_ref = bf16[96,768]{1,0:T(8,128)(2,1)S(1)} collective-permute-done((bf16[96,768]{1,0:T(8,128)(2,1)}, bf16[96,768]{1,0:T(8,128)(2,1)S(1)}, u32[]{:S(2)}, u32[]{:S(2)}) %collective-permute-start) | collective-permute-done | bytes 147488 | tf_op jit(solution)/shard_map/ppermute | solution.py:340
  16.2 0.1 shard_map.133
  16.3 41.6 %all_to_all.15 = bf16[8,2,96,768]{3,2,1,0:T(8,128)(2,1)S(1)} all-to-all(bf16[8,2,96,768]{3,2,1,0:T(8,128)(2,1)S(1)} %shard_map.133), channel_id=1, replica_groups={{0,32,128,160,256,288,384,416},{1,5,9,13,17,21,25,29},{2,34,130,162,258..., dimensions={0} | all-to-all | bytes 4718592 | tf_op jit(solution)/shard_map/all_to_all | solution.py:344
  57.9 0.0 copy-start.2
  57.9 2.0 %collective-permute-start.1 = (bf16[16,96,768]{2,1,0:T(8,128)(2,1)S(1)}, bf16[16,96,768]{2,1,0:T(8,128)(2,1)S(1)}, u32[]{:S(2)}, u32[]{:S(2)}) collective-permute-start(bf16[16,96,768]{2,1,0:T(8,128)(2,1)S(1)} %bitcast.3), channel_id=1, source_target_pairs={{0,1},{1,0},{2,3},{3,2},{4,5},{5,4},{6,7},{7,6},{8,9},{9,8},{10,11... | collective-permute-start | bytes 7077896 | tf_op jit(solution)/shard_map/ppermute | solution.py:349
  59.9 3.0 %shard_map.134 = (bf16[5,384,512]{2,1,0:T(8,128)(2,1)S(1)}, bf16[5,384,512]{2,1,0:T(8,128)(2,1)S(1)}, bf16[5,384,512]{2,1,0:T(8,128)(2,1)S(1)}, bf16[5,384,512]{...) custom-call(bf16[16,96,768]{2,1,0:T(8,128)(2,1)S(1)} %bitcast.4), custom_call_target="tpu_custom_call" | custom-call | tf_op jit(solution)/shard_map/pallas_call | solution.py:300
  62.9 1.5 %collective-permute-done.1.other_ref = bf16[16,96,768]{2,1,0:T(8,128)(2,1)S(1)} collective-permute-done((bf16[16,96,768]{2,1,0:T(8,128)(2,1)S(1)}, bf16[16,96,768]{2,1,0:T(8,128)(2,1)S(1)}, u32[]{:S(2)}, u32[]{:S(2)}) %collective-permute-start.1) | collective-permute-done | bytes 2359328 | tf_op jit(solution)/shard_map/ppermute | solution.py:349
  64.4 0.0 copy-done.2
  64.4 0.0 copy-start.1
  64.4 0.0 copy-start.3
  64.4 4.8 %shard_map.135 = (bf16[5,384,512]{2,1,0:T(8,128)(2,1)S(1)}, bf16[5,384,512]{2,1,0:T(8,128)(2,1)S(1)}, bf16[5,384,512]{2,1,0:T(8,128)(2,1)S(1)}, bf16[5,384,512]{...) custom-call(s32[2,1,8]{2,1,0:T(1,128)S(1)} %copy-done.2, ...), custom_call_target="tpu_custom_call", output_to_operand_aliasing={{0}: (4, {}), {1}: (5, {}), {2}: (6, {}), {3}: (7, {}), {4}... | custom-call | tf_op jit(solution)/shard_map/pallas_call | solution.py:300
  69.2 6.3 %collective-permute-start.2 = (bf16[48,768]{1,0:T(8,128)(2,1)S(1)}, bf16[48,768]{1,0:T(8,128)(2,1)S(1)}, u32[]{:S(2)}, u32[]{:S(2)}) collective-permute-start(bf16[48,768]{1,0:T(8,128)(2,1)S(1)} %get-tuple-element.34.piece_ref), channel_id=1, source_target_pairs={{0,64},{1,65},{2,66},{3,67},{4,68},{5,69},{6,70},{7,71},{8,72},{9,... | collective-permute-start | bytes 221192 | tf_op jit(solution)/shard_map/ppermute | solution.py:340
  75.5 0.0 copy-done.1
  75.5 0.0 copy-done.3
  75.5 1.7 %shard_map.136.refs_0_.dense_ref = f32[384,192]{1,0:T(8,128)S(1)} custom-call(s32[2,1,8]{2,1,0:T(1,128)S(1)} %copy-done.3, s32[1,1]{1,0:T(1,128)S(6)} %copy.33.dcnt_ref, bf16[92,736]{1,0:T(8,128)(2,1)S(1)} %copy-done.1, s32[16,128]{1,0:T(8,128)S(1)} %get-tuple-element.29.after_ref.code_ref), custom_call_target="tpu_custom_call" | custom-call | tf_op jit(solution)/shard_map/pallas_call | solution.py:300
  77.3 0.0 copy-start.4
  77.3 1.7 %collective-permute-done.2.far_ref = bf16[48,768]{1,0:T(8,128)(2,1)S(1)} collective-permute-done((bf16[48,768]{1,0:T(8,128)(2,1)S(1)}, bf16[48,768]{1,0:T(8,128)(2,1)S(1)}, u32[]{:S(2)}, u32[]{:S(2)}) %collective-permute-start.2) | collective-permute-done | bytes 73760 | tf_op jit(solution)/shard_map/ppermute | solution.py:340
  79.0 0.1 shard_map.137
  79.1 20.2 %all_to_all.16 = bf16[8,2,48,768]{3,2,1,0:T(8,128)(2,1)S(1)} all-to-all(bf16[8,2,48,768]{3,2,1,0:T(8,128)(2,1)S(1)} %shard_map.137), channel_id=1, replica_groups={{0,32,128,160,256,288,384,416},{1,33,129,161,257,289,385,417},{2,34,130..., dimensions={0} | all-to-all | bytes 2359296 | tf_op jit(solution)/shard_map/all_to_all | solution.py:344
  99.3 0.0 copy-done.4
  99.3 4.0 %shard_map.138 = (f32[384,192]{1,0:T(8,128)S(1)}, bf16[48,768]{1,0:T(8,128)(2,1)S(1)}) custom-call(s32[16,128]{1,0:T(8,128)S(1)} %get-tuple-element.29.after_ref.code_ref, s32[2,1,8]{2,1,0:T(1,128)S(1)} %copy-done.4, s32[1,1]{1,0:T(1,128)S(6)} %copy.35.scnt_ref.count_ref, bf16[5,384,512]{2,1,0:T(8,128)(2,1)S(1)} %get-tuple-element.30.h0, ...), custom_call_target="tpu_custom_call" | custom-call | tf_op jit(solution)/shard_map/pallas_call | solution.py:300
  103.3 0.0 copy-start.5
  103.3 1.9 %collective-permute-start.3 = (bf16[48,768]{1,0:T(8,128)(2,1)S(1)}, bf16[48,768]{1,0:T(8,128)(2,1)S(1)}, u32[]{:S(2)}, u32[]{:S(2)}) collective-permute-start(bf16[48,768]{1,0:T(8,128)(2,1)S(1)} %get-tuple-element.35.piece_ref), channel_id=1, source_target_pairs={{0,64},{1,65},{2,66},{3,67},{4,68},{5,69},{6,70},{7,71},{8,72},{9,... | collective-permute-start | bytes 221192 | tf_op jit(solution)/shard_map/ppermute | solution.py:340
  105.9 4.0 %collective-permute-done.3.far_ref = bf16[48,768]{1,0:T(8,128)(2,1)S(1)} collective-permute-done((bf16[48,768]{1,0:T(8,128)(2,1)S(1)}, bf16[48,768]{1,0:T(8,128)(2,1)S(1)}, u32[]{:S(2)}, u32[]{:S(2)}) %collective-permute-start.3) | collective-permute-done | bytes 73760 | tf_op jit(solution)/shard_map/ppermute | solution.py:340
  109.9 0.1 shard_map.139
  110.0 16.4 %all_to_all.17 = bf16[8,2,48,768]{3,2,1,0:T(8,128)(2,1)S(1)} all-to-all(bf16[8,2,48,768]{3,2,1,0:T(8,128)(2,1)S(1)} %shard_map.139), channel_id=1, replica_groups={{0,32,128,160,256,288,384,416},{1,33,129,161,257,289,385,417},{2,34,130..., dimensions={0} | all-to-all | bytes 2359296 | tf_op jit(solution)/shard_map/all_to_all | solution.py:344
  126.3 0.0 copy-done.5
  126.3 3.6 %shard_map.140.own_ref = f32[1152,128]{1,0:T(8,128)S(1)} custom-call(s32[16,128]{1,0:T(8,128)S(1)} %get-tuple-element.29.after_ref.code_ref, s32[2,1,8]{2,1,0:T(1,128)S(1)} %copy-done.5, s32[1,1]{1,0:T(1,128)S(6)} %copy.36.refs_0_.count_ref, bf16[5,384,512]{2,1,0:T(8,128)(2,1)S(1)} %get-tuple-element.30.h0, bf16[5,384,512]{2,1,0:T(8,128)(2,1)S(1)} %get-tuple-element.31.h1, ...), custom_call_target="tpu_custom_call" | custom-call | tf_op jit(solution)/shard_map/pallas_call | solution.py:300
  129.9 6.1 %collective-permute-start.4 = (f32[1152,128]{1,0:T(8,128)S(1)}, f32[1152,128]{1,0:T(8,128)S(1)}, u32[]{:S(2)}, u32[]{:S(2)}) collective-permute-start(f32[1152,128]{1,0:T(8,128)S(1)} %shard_map.140.own_ref), channel_id=1, source_target_pairs={{0,1},{1,0},{2,3},{3,2},{4,5},{5,4},{6,7},{7,6},{8,9},{9,8},{10,11... | collective-permute-start | bytes 1769480 | tf_op jit(solution)/shard_map/ppermute | solution.py:349
  136.1 1.6 %collective-permute-done.4.other_ref = f32[1152,128]{1,0:T(8,128)S(1)} collective-permute-done((f32[1152,128]{1,0:T(8,128)S(1)}, f32[1152,128]{1,0:T(8,128)S(1)}, u32[]{:S(2)}, u32[]{:S(2)}) %collective-permute-start.4) | collective-permute-done | bytes 589856 | tf_op jit(solution)/shard_map/ppermute | solution.py:349
  137.7 1.9 %shard_map.141 = (f32[368,368]{1,0:T(8,128)}, f32[368,368]{1,0:T(8,128)}) custom-call(f32[1152,128]{1,0:T(8,128)S(1)} %shard_map.140.own_ref, f32[1152,128]{1,0:T(8,128)S(1)} %collective-permute-done.4.other_ref), custom_call_target="tpu_custom_call" | custom-call | tf_op jit(solution)/shard_map/pallas_call | solution.py:300
Async XLA Ops:
  5.0 11.2 %collective-permute-start = (bf16[96,768]{1,0:T(8,128)(2,1)}, bf16[96,768]{1,0:T(8,128)(2,1)S(1)}, u32[]{:S(2)}, u32[]{:S(2)}) collective-permute-start(bf16[96,768]{1,0:T(8,128)(2,1)} %shard_map.131.piece_ref), channel_id=1, source_target_pairs={{0,64},{1,3},{2,66},{3,1},{4,68},{5,7},{6,70},{7,5},{8,72},{9,11},... | collective-permute-start | bytes 442376 | tf_op jit(solution)/shard_map/ppermute | solution.py:340
  13.3 0.9 copy-start
  57.9 6.6 %copy-start.2 = (s32[2,1,8]{2,1,0:T(1,128)S(1)}, s32[2,1,8]{2,1,0:T(1,128)}, u32[]{:S(2)}) copy-start(s32[2,1,8]{2,1,0:T(1,128)} %index_ref.3) | copy-start | bytes 196
  57.9 6.5 %collective-permute-start.1 = (bf16[16,96,768]{2,1,0:T(8,128)(2,1)S(1)}, bf16[16,96,768]{2,1,0:T(8,128)(2,1)S(1)}, u32[]{:S(2)}, u32[]{:S(2)}) collective-permute-start(bf16[16,96,768]{2,1,0:T(8,128)(2,1)S(1)} %bitcast.3), channel_id=1, source_target_pairs={{0,1},{1,0},{2,3},{3,2},{4,5},{5,4},{6,7},{7,6},{8,9},{9,8},{10,11... | collective-permute-start | bytes 7077896 | tf_op jit(solution)/shard_map/ppermute | solution.py:349
  64.4 11.1 %copy-start.1 = (bf16[92,736]{1,0:T(8,128)(2,1)S(1)}, bf16[92,736]{1,0:T(8,128)(2,1)}, u32[]{:S(2)}) copy-start(bf16[92,736]{1,0:T(8,128)(2,1)} %dens_ref.1) | copy-start | bytes 406276
  64.4 11.1 %copy-start.3 = (s32[2,1,8]{2,1,0:T(1,128)S(1)}, s32[2,1,8]{2,1,0:T(1,128)}, u32[]{:S(2)}) copy-start(s32[2,1,8]{2,1,0:T(1,128)} %didx_ref.1) | copy-start | bytes 196
  69.2 9.8 %collective-permute-start.2 = (bf16[48,768]{1,0:T(8,128)(2,1)S(1)}, bf16[48,768]{1,0:T(8,128)(2,1)S(1)}, u32[]{:S(2)}, u32[]{:S(2)}) collective-permute-start(bf16[48,768]{1,0:T(8,128)(2,1)S(1)} %get-tuple-element.34.piece_ref), channel_id=1, source_target_pairs={{0,64},{1,65},{2,66},{3,67},{4,68},{5,69},{6,70},{7,71},{8,72},{9,... | collective-permute-start | bytes 221192 | tf_op jit(solution)/shard_map/ppermute | solution.py:340
  77.3 22.0 %copy-start.4 = (s32[2,1,8]{2,1,0:T(1,128)S(1)}, s32[2,1,8]{2,1,0:T(1,128)}, u32[]{:S(2)}) copy-start(s32[2,1,8]{2,1,0:T(1,128)} %index_ref.4) | copy-start | bytes 196
  103.3 23.0 %copy-start.5 = (s32[2,1,8]{2,1,0:T(1,128)S(1)}, s32[2,1,8]{2,1,0:T(1,128)}, u32[]{:S(2)}) copy-start(s32[2,1,8]{2,1,0:T(1,128)} %index_ref.5) | copy-start | bytes 196
  103.3 6.5 %collective-permute-start.3 = (bf16[48,768]{1,0:T(8,128)(2,1)S(1)}, bf16[48,768]{1,0:T(8,128)(2,1)S(1)}, u32[]{:S(2)}, u32[]{:S(2)}) collective-permute-start(bf16[48,768]{1,0:T(8,128)(2,1)S(1)} %get-tuple-element.35.piece_ref), channel_id=1, source_target_pairs={{0,64},{1,65},{2,66},{3,67},{4,68},{5,69},{6,70},{7,71},{8,72},{9,... | collective-permute-start | bytes 221192 | tf_op jit(solution)/shard_map/ppermute | solution.py:340
  129.9 7.7 %collective-permute-start.4 = (f32[1152,128]{1,0:T(8,128)S(1)}, f32[1152,128]{1,0:T(8,128)S(1)}, u32[]{:S(2)}, u32[]{:S(2)}) collective-permute-start(f32[1152,128]{1,0:T(8,128)S(1)} %shard_map.140.own_ref), channel_id=1, source_target_pairs={{0,1},{1,0},{2,3},{3,2},{4,5},{5,4},{6,7},{7,6},{8,9},{9,8},{10,11... | collective-permute-start | bytes 1769480 | tf_op jit(solution)/shard_map/ppermute | solution.py:349

commit v7 on v6

--- a/solution.py
+++ b/solution.py
@@ -107,7 +107,6 @@
 
 
 def unpack_ham(code_ref, g, from_ref, ham_ref):
-    ham_ref[...] = jnp.zeros_like(ham_ref)
     for t in range(BT):
         wire = from_ref[g * BT + t]
         for s in range(CAP):
@@ -119,17 +118,24 @@
             ham_ref[where, rows, lanes] = wire[:, s * BLK:(s + 1) * BLK]
 
 
-def unpack_right(code_ref, which, g, wire_ref, right_ref, first_row=0):
-    right_ref[...] = jnp.zeros_like(right_ref)
-    for t in range(BT):
-        wire = wire_ref[g * BT + t, pl.ds(first_row, COLS), :]
+def unpack_right(code_ref, which, wire_ref, order, right_ref, first_row=0):
+    for t, n in enumerate(order):
+        wire = wire_ref[n, pl.ds(first_row, COLS), :]
         for s in range(CAP):
-            code = code_ref[g * BT + t, META - TAIL + which * CAP + s]
+            code = code_ref[n, META - TAIL + which * CAP + s]
             at = jnp.maximum(code, 0)
-            where = jnp.where(code >= 0, t % 2 * 2 + t // 2, BT)
+            where = jnp.where(code >= 0, t, BT)
             rows = pl.ds(pl.multiple_of((at % BT) * COLS, 16), COLS)
             lanes = pl.ds(pl.multiple_of((at // BT) * LANES, LANES), BLK)
             right_ref[where, rows, lanes] = wire[:, s * BLK:(s + 1) * BLK]
+
+
+def dens_order(g):
+    return [g // 2 * 8 + y_lo * 2 + g % 2 for y_lo in range(BT)]
+
+
+def term_order(g):
+    return [g * BT + y_lo % 2 * 2 + y_lo // 2 for y_lo in range(BT)]
 
 
 def multiply(total, ham_ref, right_ref):
@@ -140,11 +146,13 @@
 
 def product(ham_refs, code_ref, which, wire_ref, right_refs):
     total = jnp.zeros((BT * ROWS, BT * COLS), F32)
-    unpack_right(code_ref, which, 0, wire_ref, right_refs[0])
+    right_refs[0][...] = jnp.zeros_like(right_refs[0])
+    unpack_right(code_ref, which, wire_ref, term_order(0), right_refs[0])
     for g in range(BT):
         total = multiply(total, ham_refs[g], right_refs[g])
         if g + 1 < BT:
-            unpack_right(code_ref, which, g + 1, wire_ref, right_refs[g + 1])
+            right_refs[g + 1][...] = jnp.zeros_like(right_refs[g + 1])
+            unpack_right(code_ref, which, wire_ref, term_order(g + 1), right_refs[g + 1])
     return total
 
 
@@ -187,11 +195,13 @@
     layer = lax.axis_index("layer")
     read_codes(panel_ref, note_ref, code_ref, sem)
     own_note[...] = note_ref[...]
+    for ref in (*ham_refs, *right_refs):
+        ref[...] = jnp.zeros_like(ref)
 
     @pl.when(layer == 0)
     def _():
         for g in range(BT):
-            unpack_right(code_ref, 0, g, panel_ref, right_refs[g])
+            unpack_right(code_ref, 0, panel_ref, dens_order(g), right_refs[g])
 
     @pl.when(layer == 1)
     def _():
@@ -204,7 +214,9 @@
     total_ref, rounded_ref, note_ref, code_ref, sem = refs[19:]
     layer = lax.axis_index("layer")
     read_codes(other_ref, note_ref, code_ref, sem)
-    code_out[...] = jnp.where(layer == 0, own_note[...], note_ref[...])
+    for g in range(BT):
+        for n, to in zip(dens_order(g), term_order(g)):
+            code_out[to:to + 1, :] = jnp.where(layer == 0, own_note[n:n + 1, :], note_ref[n:n + 1, :])
 
     def pipelined(unpack):
         total = jnp.zeros((BT * ROWS, BT * COLS), F32)
@@ -221,7 +233,7 @@
 
     @pl.when(layer == 1)
     def _():
-        pipelined(lambda g: unpack_right(code_ref, 0, g, other_ref, right_refs[g], COLS))
+        pipelined(lambda g: unpack_right(code_ref, 0, other_ref, dens_order(g), right_refs[g], COLS))
 
     codes = all_codes(index_ref, count_ref)
     term = keep(codes, total_ref[...])
@@ -248,31 +260,44 @@
     halves_ref[2 * rows:3 * rows] = jnp.concatenate([real[:, LANES:], imag[:, LANES:]], axis=1)
 
 
-def join_kernel(own_ref, other_ref, *out_refs):
-    swap = lax.axis_index("layer") == 1
+def put_half(from_ref, n, layer, out_ref, add):
     rows, rest = BT * ROWS, BT * COLS - LANES
-    for n, out_ref in enumerate(out_refs):
-        own, other = (
-            jnp.concatenate(
-                [ref[n * rows:(n + 1) * rows], ref[2 * rows:3 * rows][:, n * rest:(n + 1) * rest]],
-                axis=1,
-            )
-            for ref in (own_ref, other_ref)
-        )
-        low, high = jnp.where(swap, other, own), jnp.where(swap, own, other)
-        pieces = []
-        for j in range(BT):
-            pieces += [low[:, j * COLS:j * COLS + HALF], high[:, j * COLS:j * COLS + HALF]]
-        whole = jnp.concatenate(pieces, axis=1)
-        for i in range(BT):
-            out_ref[i * BLK:(i + 1) * BLK, :] = whole[i * ROWS:i * ROWS + BLK, :]
+    half = jnp.concatenate(
+        [from_ref[n * rows:(n + 1) * rows], from_ref[2 * rows:3 * rows][:, n * rest:(n + 1) * rest]],
+        axis=1,
+    )
+    gap = jnp.zeros((rows, HALF), F32)
+    pieces = []
+    for j in range(BT):
+        piece = half[:, j * COLS:j * COLS + HALF]
+        pieces += [gap, piece] if layer else [piece, gap]
+    whole = jnp.concatenate(pieces, axis=1)
+    for i in range(BT):
+        to = slice(i * BLK, (i + 1) * BLK)
+        block = whole[i * ROWS:i * ROWS + BLK, :]
+        out_ref[to, :] = add[to, :] + block if add is not None else block
+
+
+def own_half_kernel(own_ref, *out_refs):
+    for layer in range(2):
+        @pl.when(lax.axis_index("layer") == layer)
+        def _(layer=layer):
+            for n, out_ref in enumerate(out_refs):
+                put_half(own_ref, n, layer, out_ref, None)
+
+
+def other_half_kernel(other_ref, real_ref, imag_ref, *out_refs):
+    for layer in range(2):
+        @pl.when(lax.axis_index("layer") == layer)
+        def _(layer=layer):
+            for n, out_ref in enumerate(out_refs):
+                put_half(other_ref, n, 1 - layer, out_ref, (real_ref, imag_ref)[n])
 
 
 def own_place(by_layer):
-    high = lax.axis_index("y_lo") // 2
     if by_layer:
-        high = jnp.where(lax.axis_index("layer") == 0, high, lax.axis_index("y_hi"))
-    return high
+        return jnp.where(lax.axis_index("layer") == 0, lax.axis_index("x") % 2, lax.axis_index("y_hi"))
+    return lax.axis_index("y_lo") // 2
 
 
 def own_kernel(piece_ref, out_ref):
@@ -323,7 +348,9 @@
 def pair_route(both):
     route = []
     for x, y_lo, z, y_hi, layer in everywhere():
-        to = (x, y_lo, z, 1 - y_hi, layer) if both and layer else (x, y_lo ^ 2, z, y_hi, layer)
+        to = (x, y_lo ^ 2, z, y_hi, layer)
+        if both:
+            to = (x, y_lo, z, 1 - y_hi, layer) if layer else (x ^ 1, y_lo, z, y_hi, layer)
         route.append((place(x, y_lo, z, y_hi, layer), place(*to)))
     return route
 
@@ -331,7 +358,9 @@
 def groups(both):
     found = {}
     for x, y_lo, z, y_hi, layer in everywhere():
-        key = (layer, x, y_lo, y_hi) if both and layer else (layer, y_lo // 2, z, y_hi)
+        key = (layer, y_lo // 2, z, y_hi)
+        if both:
+            key = (layer, x, y_lo, y_hi) if layer else (layer, x % 2, z, y_hi)
         found.setdefault(key, []).append(place(x, y_lo, z, y_hi, layer))
     return sorted(found.values())
 
@@ -417,7 +446,8 @@
         dense_right,
     )
     whole = shape(SIDE, SIDE, dtype=F32)
-    return call(join_kernel, [VMEM] * 2, (halves, swap(halves)), (whole, whole))
+    own = call(own_half_kernel, [VMEM], (halves,), (whole, whole))
+    return call(other_half_kernel, [VMEM] * 3, (swap(halves), *own), (whole, whole))
 
 
 def solution(mesh):

time: 140 us -> 139 us (level)
    pallas_call x11 -> x12, Pallas kernels: 21.2 us -> 21.5 us  [call(): pl.pallas_call(kernel, out_shape=out_shape, in_specs=in_specs, out_specs=...]
  transfers between devices with their start and end apart: 5 -> 5, of which waited for: 5 -> 5; matrix products, arithmetic and copies ran while one was open for 0% -> 0% of each run, Pallas kernels for 3% -> 4%
where the time goes in v7:
time: 139 us; the launch traced here: 138 us
  blocking collectives  78.1 us (56%)
  starting transfers between devices  24 us (17%)
  Pallas kernels  21.5 us (15%)
  waiting for transfers between devices  9.81 us (7%)
  between operations  4.01 us (3%)
    all_to_all x3, blocking collectives, spread(): tiles = lax.all_to_all(pairs, AXES, 0, 0, axis_index_groups=groups(both))  78.1 us
    pallas_call x12, Pallas kernels, call(): pl.pallas_call(kernel, out_shape=out_shape, in_specs=in_specs, out_specs=...  21.5 us
    ppermute x3, starting transfers between devices, to_pair(): return lax.ppermute(piece, AXES, pair_route(both))  15.8 us
    ppermute x2, starting transfers between devices, swap(): return lax.ppermute(values, 'layer', [(0, 1), (1, 0)])  8.21 us
    ppermute x3, waiting for transfers between devices, to_pair(): return lax.ppermute(piece, AXES, pair_route(both))  7.69 us
  transfers between devices with their start and end apart: 5, of which 5 were waited for; matrix products, arithmetic and copies ran while one was open for 0% of the time, Pallas kernels for 4%

profile of v7, /device:TPU:1, one launch (start us, length us, event | category | flops | bytes accessed | tf_op | source)
XLA Modules:
  0.0 138.4 jit_solution(12674149964357826250)
XLA Ops:
  3.2 1.8 %shard_map.131.piece_ref = bf16[96,768]{1,0:T(8,128)(2,1)} custom-call(s32[2,1,8]{2,1,0:T(1,128)} %hidx_hbm.1, s32[1,1]{1,0:T(1,128)S(6)} %copy.32.hcnt_ref, s32[2,1,8]{2,1,0:T(1,128)} %didx_ref.1, s32[1,1]{1,0:T(1,128)S(6)} %copy.33.dcnt_ref, s32[2,1,8]{2,1,0:T(1,128)} %index_ref.3, s32[1,1]{1,0:T(1,128)S(6)} %copy.34.fcnt_ref.count_ref, ...), custom_call_target="tpu_custom_call" | custom-call | tf_op jit(solution)/shard_map/pallas_call | solution.py:325
  5.0 8.3 %collective-permute-start = (bf16[96,768]{1,0:T(8,128)(2,1)}, bf16[96,768]{1,0:T(8,128)(2,1)S(1)}, u32[]{:S(2)}, u32[]{:S(2)}) collective-permute-start(bf16[96,768]{1,0:T(8,128)(2,1)} %shard_map.131.piece_ref), channel_id=1, source_target_pairs={{0,128},{1,3},{2,130},{3,1},{4,132},{5,7},{6,134},{7,5},{8,136},{9... | collective-permute-start | bytes 442376 | tf_op jit(solution)/shard_map/ppermute | solution.py:369
  13.3 0.0 copy-start
  13.3 0.9 copy-done
  14.2 0.1 shard_map.132.pairs_ref
  14.3 1.8 %collective-permute-done.far_ref = bf16[96,768]{1,0:T(8,128)(2,1)S(1)} collective-permute-done((bf16[96,768]{1,0:T(8,128)(2,1)}, bf16[96,768]{1,0:T(8,128)(2,1)S(1)}, u32[]{:S(2)}, u32[]{:S(2)}) %collective-permute-start) | collective-permute-done | bytes 147488 | tf_op jit(solution)/shard_map/ppermute | solution.py:369
  16.1 0.1 shard_map.133
  16.2 41.6 %all_to_all.15 = bf16[8,2,96,768]{3,2,1,0:T(8,128)(2,1)S(1)} all-to-all(bf16[8,2,96,768]{3,2,1,0:T(8,128)(2,1)S(1)} %shard_map.133), channel_id=1, replica_groups={{0,32,64,96,256,288,320,352},{1,5,9,13,17,21,25,29},{2,34,66,98,258,290..., dimensions={0} | all-to-all | bytes 4718592 | tf_op jit(solution)/shard_map/all_to_all | solution.py:373
  57.9 0.0 copy-start.2
  57.9 2.0 %collective-permute-start.1 = (bf16[16,96,768]{2,1,0:T(8,128)(2,1)S(1)}, bf16[16,96,768]{2,1,0:T(8,128)(2,1)S(1)}, u32[]{:S(2)}, u32[]{:S(2)}) collective-permute-start(bf16[16,96,768]{2,1,0:T(8,128)(2,1)S(1)} %bitcast.3), channel_id=1, source_target_pairs={{0,1},{1,0},{2,3},{3,2},{4,5},{5,4},{6,7},{7,6},{8,9},{9,8},{10,11... | collective-permute-start | bytes 7077896 | tf_op jit(solution)/shard_map/ppermute | solution.py:378
  59.9 3.3 %shard_map.134 = (bf16[5,384,512]{2,1,0:T(8,128)(2,1)S(1)}, bf16[5,384,512]{2,1,0:T(8,128)(2,1)S(1)}, bf16[5,384,512]{2,1,0:T(8,128)(2,1)S(1)}, bf16[5,384,512]{...) custom-call(bf16[16,96,768]{2,1,0:T(8,128)(2,1)S(1)} %bitcast.4), custom_call_target="tpu_custom_call" | custom-call | tf_op jit(solution)/shard_map/pallas_call | solution.py:325
  63.2 1.2 collective-permute-done.1.other_ref
  64.4 0.0 copy-done.2
  64.4 0.0 copy-start.1
  64.4 0.0 copy-start.3
  64.4 4.6 %shard_map.135 = (bf16[5,384,512]{2,1,0:T(8,128)(2,1)S(1)}, bf16[5,384,512]{2,1,0:T(8,128)(2,1)S(1)}, bf16[5,384,512]{2,1,0:T(8,128)(2,1)S(1)}, bf16[5,384,512]{...) custom-call(s32[2,1,8]{2,1,0:T(1,128)S(1)} %copy-done.2, ...), custom_call_target="tpu_custom_call", output_to_operand_aliasing={{0}: (4, {}), {1}: (5, {}), {2}: (6, {}), {3}: (7, {}), {4}... | custom-call | tf_op jit(solution)/shard_map/pallas_call | solution.py:325
  69.0 5.6 %collective-permute-start.2 = (bf16[48,768]{1,0:T(8,128)(2,1)S(1)}, bf16[48,768]{1,0:T(8,128)(2,1)S(1)}, u32[]{:S(2)}, u32[]{:S(2)}) collective-permute-start(bf16[48,768]{1,0:T(8,128)(2,1)S(1)} %get-tuple-element.36.piece_ref), channel_id=1, source_target_pairs={{0,64},{1,65},{2,66},{3,67},{4,68},{5,69},{6,70},{7,71},{8,72},{9,... | collective-permute-start | bytes 221192 | tf_op jit(solution)/shard_map/ppermute | solution.py:369
  74.6 0.0 copy-done.1
  74.6 0.0 copy-done.3
  74.6 1.7 %shard_map.136.refs_0_.dense_ref = f32[384,192]{1,0:T(8,128)S(1)} custom-call(s32[2,1,8]{2,1,0:T(1,128)S(1)} %copy-done.3, s32[1,1]{1,0:T(1,128)S(6)} %copy.33.dcnt_ref, bf16[92,736]{1,0:T(8,128)(2,1)S(1)} %copy-done.1, s32[16,128]{1,0:T(8,128)S(1)} %get-tuple-element.31.after_ref.code_ref), custom_call_target="tpu_custom_call" | custom-call | tf_op jit(solution)/shard_map/pallas_call | solution.py:325
  76.3 0.0 copy-start.4
  76.3 1.9 %collective-permute-done.2.far_ref = bf16[48,768]{1,0:T(8,128)(2,1)S(1)} collective-permute-done((bf16[48,768]{1,0:T(8,128)(2,1)S(1)}, bf16[48,768]{1,0:T(8,128)(2,1)S(1)}, u32[]{:S(2)}, u32[]{:S(2)}) %collective-permute-start.2) | collective-permute-done | bytes 73760 | tf_op jit(solution)/shard_map/ppermute | solution.py:369
  78.2 0.1 shard_map.137
  78.3 20.2 %all_to_all.16 = bf16[8,2,48,768]{3,2,1,0:T(8,128)(2,1)S(1)} all-to-all(bf16[8,2,48,768]{3,2,1,0:T(8,128)(2,1)S(1)} %shard_map.137), channel_id=1, replica_groups={{0,32,128,160,256,288,384,416},{1,33,129,161,257,289,385,417},{2,34,130..., dimensions={0} | all-to-all | bytes 2359296 | tf_op jit(solution)/shard_map/all_to_all | solution.py:373
  98.5 0.0 copy-done.4
  98.5 4.0 %shard_map.138 = (f32[384,192]{1,0:T(8,128)S(1)}, bf16[48,768]{1,0:T(8,128)(2,1)S(1)}) custom-call(s32[16,128]{1,0:T(8,128)S(1)} %get-tuple-element.31.after_ref.code_ref, s32[2,1,8]{2,1,0:T(1,128)S(1)} %copy-done.4, s32[1,1]{1,0:T(1,128)S(6)} %copy.35.scnt_ref.count_ref, bf16[5,384,512]{2,1,0:T(8,128)(2,1)S(1)} %get-tuple-element.32.h0, ...), custom_call_target="tpu_custom_call" | custom-call | tf_op jit(solution)/shard_map/pallas_call | solution.py:325
  102.5 0.0 copy-start.5
  102.5 1.9 %collective-permute-start.3 = (bf16[48,768]{1,0:T(8,128)(2,1)S(1)}, bf16[48,768]{1,0:T(8,128)(2,1)S(1)}, u32[]{:S(2)}, u32[]{:S(2)}) collective-permute-start(bf16[48,768]{1,0:T(8,128)(2,1)S(1)} %get-tuple-element.37.piece_ref), channel_id=1, source_target_pairs={{0,64},{1,65},{2,66},{3,67},{4,68},{5,69},{6,70},{7,71},{8,72},{9,... | collective-permute-start | bytes 221192 | tf_op jit(solution)/shard_map/ppermute | solution.py:369
  105.1 4.0 %collective-permute-done.3.far_ref = bf16[48,768]{1,0:T(8,128)(2,1)S(1)} collective-permute-done((bf16[48,768]{1,0:T(8,128)(2,1)S(1)}, bf16[48,768]{1,0:T(8,128)(2,1)S(1)}, u32[]{:S(2)}, u32[]{:S(2)}) %collective-permute-start.3) | collective-permute-done | bytes 73760 | tf_op jit(solution)/shard_map/ppermute | solution.py:369
  109.1 0.1 shard_map.139
  109.1 16.3 %all_to_all.17 = bf16[8,2,48,768]{3,2,1,0:T(8,128)(2,1)S(1)} all-to-all(bf16[8,2,48,768]{3,2,1,0:T(8,128)(2,1)S(1)} %shard_map.139), channel_id=1, replica_groups={{0,32,128,160,256,288,384,416},{1,33,129,161,257,289,385,417},{2,34,130..., dimensions={0} | all-to-all | bytes 2359296 | tf_op jit(solution)/shard_map/all_to_all | solution.py:373
  125.5 0.0 copy-done.5
  125.5 3.6 %shard_map.140.own_ref = f32[1152,128]{1,0:T(8,128)S(1)} custom-call(s32[16,128]{1,0:T(8,128)S(1)} %get-tuple-element.31.after_ref.code_ref, s32[2,1,8]{2,1,0:T(1,128)S(1)} %copy-done.5, s32[1,1]{1,0:T(1,128)S(6)} %copy.36.refs_0_.count_ref, bf16[5,384,512]{2,1,0:T(8,128)(2,1)S(1)} %get-tuple-element.32.h0, bf16[5,384,512]{2,1,0:T(8,128)(2,1)S(1)} %get-tuple-element.33.h1, ...), custom_call_target="tpu_custom_call" | custom-call | tf_op jit(solution)/shard_map/pallas_call | solution.py:325
  129.1 6.2 %collective-permute-start.4 = (f32[1152,128]{1,0:T(8,128)S(1)}, f32[1152,128]{1,0:T(8,128)S(1)}, u32[]{:S(2)}, u32[]{:S(2)}) collective-permute-start(f32[1152,128]{1,0:T(8,128)S(1)} %shard_map.140.own_ref), channel_id=1, source_target_pairs={{0,1},{1,0},{2,3},{3,2},{4,5},{5,4},{6,7},{7,6},{8,9},{9,8},{10,11... | collective-permute-start | bytes 1769480 | tf_op jit(solution)/shard_map/ppermute | solution.py:378
  135.2 0.6 shard_map.141
  135.9 1.0 collective-permute-done.4.other_ref
  136.8 1.5 %shard_map.142 = (f32[368,368]{1,0:T(8,128)}, f32[368,368]{1,0:T(8,128)}) custom-call(f32[1152,128]{1,0:T(8,128)S(1)} %collective-permute-done.4.other_ref, f32[368,368]{1,0:T(8,128)S(1)} %get-tuple-element.40.real_ref, f32[368,368]{1,0:T(8,128)S(1)} %get-tuple-element.41.imag_ref), custom_call_target="tpu_custom_call" | custom-call | tf_op jit(solution)/shard_map/pallas_call | solution.py:325
Async XLA Ops:
  5.0 11.1 %collective-permute-start = (bf16[96,768]{1,0:T(8,128)(2,1)}, bf16[96,768]{1,0:T(8,128)(2,1)S(1)}, u32[]{:S(2)}, u32[]{:S(2)}) collective-permute-start(bf16[96,768]{1,0:T(8,128)(2,1)} %shard_map.131.piece_ref), channel_id=1, source_target_pairs={{0,128},{1,3},{2,130},{3,1},{4,132},{5,7},{6,134},{7,5},{8,136},{9... | collective-permute-start | bytes 442376 | tf_op jit(solution)/shard_map/ppermute | solution.py:369
  13.3 0.9 copy-start
  57.9 6.6 %copy-start.2 = (s32[2,1,8]{2,1,0:T(1,128)S(1)}, s32[2,1,8]{2,1,0:T(1,128)}, u32[]{:S(2)}) copy-start(s32[2,1,8]{2,1,0:T(1,128)} %index_ref.3) | copy-start | bytes 196
  57.9 6.5 %collective-permute-start.1 = (bf16[16,96,768]{2,1,0:T(8,128)(2,1)S(1)}, bf16[16,96,768]{2,1,0:T(8,128)(2,1)S(1)}, u32[]{:S(2)}, u32[]{:S(2)}) collective-permute-start(bf16[16,96,768]{2,1,0:T(8,128)(2,1)S(1)} %bitcast.3), channel_id=1, source_target_pairs={{0,1},{1,0},{2,3},{3,2},{4,5},{5,4},{6,7},{7,6},{8,9},{9,8},{10,11... | collective-permute-start | bytes 7077896 | tf_op jit(solution)/shard_map/ppermute | solution.py:378
  64.4 10.2 %copy-start.1 = (bf16[92,736]{1,0:T(8,128)(2,1)S(1)}, bf16[92,736]{1,0:T(8,128)(2,1)}, u32[]{:S(2)}) copy-start(bf16[92,736]{1,0:T(8,128)(2,1)} %dens_ref.1) | copy-start | bytes 406276
  64.4 10.2 %copy-start.3 = (s32[2,1,8]{2,1,0:T(1,128)S(1)}, s32[2,1,8]{2,1,0:T(1,128)}, u32[]{:S(2)}) copy-start(s32[2,1,8]{2,1,0:T(1,128)} %didx_ref.1) | copy-start | bytes 196
  69.0 9.3 %collective-permute-start.2 = (bf16[48,768]{1,0:T(8,128)(2,1)S(1)}, bf16[48,768]{1,0:T(8,128)(2,1)S(1)}, u32[]{:S(2)}, u32[]{:S(2)}) collective-permute-start(bf16[48,768]{1,0:T(8,128)(2,1)S(1)} %get-tuple-element.36.piece_ref), channel_id=1, source_target_pairs={{0,64},{1,65},{2,66},{3,67},{4,68},{5,69},{6,70},{7,71},{8,72},{9,... | collective-permute-start | bytes 221192 | tf_op jit(solution)/shard_map/ppermute | solution.py:369
  76.3 22.2 %copy-start.4 = (s32[2,1,8]{2,1,0:T(1,128)S(1)}, s32[2,1,8]{2,1,0:T(1,128)}, u32[]{:S(2)}) copy-start(s32[2,1,8]{2,1,0:T(1,128)} %index_ref.4) | copy-start | bytes 196
  102.5 23.0 %copy-start.5 = (s32[2,1,8]{2,1,0:T(1,128)S(1)}, s32[2,1,8]{2,1,0:T(1,128)}, u32[]{:S(2)}) copy-start(s32[2,1,8]{2,1,0:T(1,128)} %index_ref.5) | copy-start | bytes 196
  102.5 6.5 %collective-permute-start.3 = (bf16[48,768]{1,0:T(8,128)(2,1)S(1)}, bf16[48,768]{1,0:T(8,128)(2,1)S(1)}, u32[]{:S(2)}, u32[]{:S(2)}) collective-permute-start(bf16[48,768]{1,0:T(8,128)(2,1)S(1)} %get-tuple-element.37.piece_ref), channel_id=1, source_target_pairs={{0,64},{1,65},{2,66},{3,67},{4,68},{5,69},{6,70},{7,71},{8,72},{9,... | collective-permute-start | bytes 221192 | tf_op jit(solution)/shard_map/ppermute | solution.py:369
  129.1 7.8 %collective-permute-start.4 = (f32[1152,128]{1,0:T(8,128)S(1)}, f32[1152,128]{1,0:T(8,128)S(1)}, u32[]{:S(2)}, u32[]{:S(2)}) collective-permute-start(f32[1152,128]{1,0:T(8,128)S(1)} %shard_map.140.own_ref), channel_id=1, source_target_pairs={{0,1},{1,0},{2,3},{3,2},{4,5},{5,4},{6,7},{7,6},{8,9},{9,8},{10,11... | collective-permute-start | bytes 1769480 | tf_op jit(solution)/shard_map/ppermute | solution.py:378

commit v8 on v7

--- a/solution.py
+++ b/solution.py
@@ -17,6 +17,8 @@
 SIDE = BT * BLK
 WIRE = 768
 META = 736
+CODES = 464
+WROWS = WIRE // LANES * BLK
 TAIL = WIRE - LANES
 TILES = 16
 AXES = ("x", "y_lo", "z", "y_hi", "layer")
@@ -52,38 +54,30 @@
     for one in copies:
         one.wait()
     layer = lax.axis_index("layer")
-    lane = lax.broadcasted_iota(jnp.int32, (ROWS, LANES), 1) - (META - TAIL)
-
-    def noted(tail, *lists):
+    lane = lax.broadcasted_iota(jnp.int32, (BLK, LANES), 1) - (META - TAIL)
+
+    def store(wire, *lists):
+        tail = wire[:, TAIL:]
         for n, (index_ref, count_ref) in enumerate(lists):
             for s in range(CAP):
-                code = code_of(index_ref, count_ref, s).astype(F32)
-                tail = jnp.where(lane == n * CAP + s, code, tail)
-        return tail.astype(BF)
+                tail = jnp.where(lane == n * CAP + s, code_of(index_ref, count_ref, s).astype(F32), tail)
+        for t in range(TAIL // LANES):
+            out_ref[t * BLK:(t + 1) * BLK, :] = wire[:, t * LANES:(t + 1) * LANES].astype(BF)
+        out_ref[WROWS - BLK:, :] = tail.astype(BF)
 
     @pl.when(layer == 0)
     def _():
         dens = dens_ref[...]
-        r = lax.broadcasted_iota(jnp.int32, (2 * COLS, META), 0)
-        x = lax.broadcasted_iota(jnp.int32, (2 * COLS, META), 1)
-        q = r % COLS
-        pieces = []
-        for s in range(CAP):
-            pick = (x == q + (r // COLS) * HALF + s * BLK) & (q < HALF)
-            pieces.append(dot_nt(jnp.where(pick, 1.0, 0.0).astype(BF), dens))
-        pieces.append(jnp.zeros((2 * COLS, WIRE - META), F32))
-        wire = jnp.concatenate(pieces, axis=1)
-        out_ref[:, 0:TAIL] = wire[:, 0:TAIL].astype(BF)
-        out_ref[:, TAIL:] = noted(
-            wire[:, TAIL:], (didx_ref, dcnt_ref), (fidx_ref, fcnt_ref), (sidx_ref, scnt_ref)
+        pieces = [dot_nt(one_hot((BLK, META), s * BLK, BLK), dens) for s in range(CAP)]
+        store(
+            jnp.concatenate(pieces + [jnp.zeros((BLK, WIRE - META), F32)], axis=1),
+            (didx_ref, dcnt_ref), (fidx_ref, fcnt_ref), (sidx_ref, scnt_ref),
         )
 
     @pl.when(layer == 1)
     def _():
-        out_ref[...] = jnp.zeros_like(out_ref)
-        out_ref[0:BLK, 0:META] = ham_ref[...]
-        tail = out_ref[:, TAIL:].astype(F32)
-        out_ref[:, TAIL:] = noted(tail, (hidx_ref, hcnt_ref))
+        wire = jnp.concatenate([ham_ref[...].astype(F32), jnp.zeros((BLK, WIRE - META), F32)], axis=1)
+        store(wire, (hidx_ref, hcnt_ref))
 
 
 def dense_kernel(didx_ref, dcnt_ref, dens_ref, after_ref, dense_ref):
@@ -106,16 +100,33 @@
         dense_ref[rows, :] = dense_ref[rows, :] + block
 
 
+def piece_rows(from_ref, n, first, rows):
+    at = [t * BLK + first for t in range(WIRE // LANES)]
+    return jnp.concatenate([from_ref[n, row:row + rows, :] for row in at], axis=1)
+
+
 def unpack_ham(code_ref, g, from_ref, ham_ref):
     for t in range(BT):
-        wire = from_ref[g * BT + t]
+        wire = piece_rows(from_ref, g * BT + t, 0, BLK)
         for s in range(CAP):
             code = code_ref[g * BT + t, META - TAIL + s]
             at = jnp.maximum(code, 0)
             where = jnp.where(code >= 0, t, BT)
-            rows = pl.ds(pl.multiple_of((at // BT) * ROWS, 16), ROWS)
+            rows = pl.ds(pl.multiple_of((at // BT) * ROWS, 16), BLK)
             lanes = pl.ds(pl.multiple_of((at % BT) * LANES, LANES), BLK)
             ham_ref[where, rows, lanes] = wire[:, s * BLK:(s + 1) * BLK]
+
+
+def unpack_dens(code_ref, g, from_ref, half, right_ref):
+    for t, n in enumerate(dens_order(g)):
+        wire = piece_rows(from_ref, n, half * HALF, HALF)
+        for s in range(CAP):
+            code = code_ref[n, META - TAIL + s]
+            at = jnp.maximum(code, 0)
+            where = jnp.where(code >= 0, t, BT)
+            rows = pl.ds(pl.multiple_of((at % BT) * COLS, 16), HALF)
+            lanes = pl.ds(pl.multiple_of((at // BT) * LANES, LANES), BLK)
+            right_ref[where, rows, lanes] = wire[:, s * BLK:(s + 1) * BLK]
 
 
 def unpack_right(code_ref, which, wire_ref, order, right_ref, first_row=0):
@@ -184,7 +195,7 @@
 
 def read_codes(panel_ref, note_ref, code_ref, sem):
     for k in range(TILES):
-        note_ref[k:k + 1, :] = panel_ref[k, 0:16, TAIL:][0:1].astype(F32).astype(jnp.int32)
+        note_ref[k:k + 1, :] = panel_ref[k, CODES:CODES + 16, :][0:1].astype(F32).astype(jnp.int32)
     copy = pltpu.make_async_copy(note_ref, code_ref, sem)
     copy.start()
     copy.wait()
@@ -201,7 +212,7 @@
     @pl.when(layer == 0)
     def _():
         for g in range(BT):
-            unpack_right(code_ref, 0, panel_ref, dens_order(g), right_refs[g])
+            unpack_dens(code_ref, g, panel_ref, 0, right_refs[g])
 
     @pl.when(layer == 1)
     def _():
@@ -233,7 +244,7 @@
 
     @pl.when(layer == 1)
     def _():
-        pipelined(lambda g: unpack_right(code_ref, 0, other_ref, dens_order(g), right_refs[g], COLS))
+        pipelined(lambda g: unpack_dens(code_ref, g, other_ref, 1, right_refs[g]))
 
     codes = all_codes(index_ref, count_ref)
     term = keep(codes, total_ref[...])
@@ -387,14 +398,14 @@
         [HBM, SMEM] * 4 + [HBM, HBM],
         (ham_index, ham_count, dens_index, dens_count, first_index, first_count, second_index,
          second_count, ham_blocks, dens_blocks),
-        shape(ROWS, WIRE),
+        shape(WROWS, LANES),
         [index] * 4 + [packed, packed, pltpu.SemaphoreType.DMA((6,))],
         vmem=62900000,
     )
     half = shape(BT * ROWS, BT * COLS, dtype=F32)
-    pairs = call(own_kernel, [VMEM], (payload,), shape(8, 2, ROWS, WIRE))
+    pairs = call(own_kernel, [VMEM], (payload,), shape(8, 2, WROWS, LANES))
     pairs = call(
-        far_kernel, [VMEM] * 2, (to_pair(payload, True), pairs), shape(8, 2, ROWS, WIRE),
+        far_kernel, [VMEM] * 2, (to_pair(payload, True), pairs), shape(8, 2, WROWS, LANES),
         alias={1: 0},
     )
     panel = spread(pairs, True)

time: 139 us -> 138 us (level)
  no operation moved by 1% of the time
where the time goes in v8:
time: 138 us; the launch traced here: 137 us
  blocking collectives  77.5 us (56%)
  starting transfers between devices  24 us (17%)
  Pallas kernels  21.3 us (15%)
  waiting for transfers between devices  9.65 us (7%)
  between operations  4.01 us (3%)
    all_to_all x3, blocking collectives, spread(): tiles = lax.all_to_all(pairs, AXES, 0, 0, axis_index_groups=groups(both))  77.5 us
    pallas_call x12, Pallas kernels, call(): pl.pallas_call(kernel, out_shape=out_shape, in_specs=in_specs, out_specs=...  21.3 us
    ppermute x3, starting transfers between devices, to_pair(): return lax.ppermute(piece, AXES, pair_route(both))  15.7 us
    ppermute x2, starting transfers between devices, swap(): return lax.ppermute(values, 'layer', [(0, 1), (1, 0)])  8.27 us
    ppermute x3, waiting for transfers between devices, to_pair(): return lax.ppermute(piece, AXES, pair_route(both))  7.26 us
  transfers between devices with their start and end apart: 5, of which 5 were waited for; matrix products, arithmetic and copies ran while one was open for 0% of the time, Pallas kernels for 4%

profile of v8, /device:TPU:1, one launch (start us, length us, event | category | flops | bytes accessed | tf_op | source)
XLA Modules:
  0.0 137.4 jit_solution(8710462412714086734)
XLA Ops:
  3.2 1.8 %shard_map.131.piece_ref = bf16[552,128]{1,0:T(8,128)(2,1)} custom-call(s32[2,1,8]{2,1,0:T(1,128)} %hidx_hbm.1, s32[1,1]{1,0:T(1,128)S(6)} %copy.32.hcnt_ref, s32[2,1,8]{2,1,0:T(1,128)} %didx_ref.1, s32[1,1]{1,0:T(1,128)S(6)} %copy.33.dcnt_ref, s32[2,1,8]{2,1,0:T(1,128)} %index_ref.3, s32[1,1]{1,0:T(1,128)S(6)} %copy.34.fcnt_ref.count_ref, ...), custom_call_target="tpu_custom_call" | custom-call | tf_op jit(solution)/shard_map/pallas_call | solution.py:336
  5.0 8.3 %collective-permute-start = (bf16[552,128]{1,0:T(8,128)(2,1)}, bf16[552,128]{1,0:T(8,128)(2,1)S(1)}, u32[]{:S(2)}, u32[]{:S(2)}) collective-permute-start(bf16[552,128]{1,0:T(8,128)(2,1)} %shard_map.131.piece_ref), channel_id=1, source_target_pairs={{0,128},{1,3},{2,130},{3,1},{4,132},{5,7},{6,134},{7,5},{8,136},{9... | collective-permute-start | bytes 423944 | tf_op jit(solution)/shard_map/ppermute | solution.py:380
  13.3 0.0 copy-start.1
  13.3 0.9 copy-done.1
  14.2 0.2 shard_map.132.pairs_ref
  14.4 1.7 %collective-permute-done.far_ref = bf16[552,128]{1,0:T(8,128)(2,1)S(1)} collective-permute-done((bf16[552,128]{1,0:T(8,128)(2,1)}, bf16[552,128]{1,0:T(8,128)(2,1)S(1)}, u32[]{:S(2)}, u32[]{:S(2)}) %collective-permute-start) | collective-permute-done | bytes 141344 | tf_op jit(solution)/shard_map/ppermute | solution.py:380
  16.1 0.2 shard_map.133
  16.2 40.6 %all_to_all.15 = bf16[8,2,552,128]{3,2,1,0:T(8,128)(2,1)S(1)} all-to-all(bf16[8,2,552,128]{3,2,1,0:T(8,128)(2,1)S(1)} %shard_map.133), channel_id=1, replica_groups={{0,32,64,96,256,288,320,352},{1,5,9,13,17,21,25,29},{2,34,66,98,258,290..., dimensions={0} | all-to-all | bytes 4521984 | tf_op jit(solution)/shard_map/all_to_all | solution.py:384
  56.8 0.0 copy-start.2
  56.8 2.0 %collective-permute-start.1 = (bf16[16,552,128]{2,1,0:T(8,128)(2,1)S(1)}, bf16[16,552,128]{2,1,0:T(8,128)(2,1)S(1)}, u32[]{:S(2)}, u32[]{:S(2)}) collective-permute-start(bf16[16,552,128]{2,1,0:T(8,128)(2,1)S(1)} %bitcast.3), channel_id=1, source_target_pairs={{0,1},{1,0},{2,3},{3,2},{4,5},{5,4},{6,7},{7,6},{8,9},{9,8},{10,11... | collective-permute-start | bytes 6782984 | tf_op jit(solution)/shard_map/ppermute | solution.py:389
  58.9 2.9 %shard_map.134 = (bf16[5,384,512]{2,1,0:T(8,128)(2,1)S(1)}, bf16[5,384,512]{2,1,0:T(8,128)(2,1)S(1)}, bf16[5,384,512]{2,1,0:T(8,128)(2,1)S(1)}, bf16[5,384,512]{...) custom-call(bf16[16,552,128]{2,1,0:T(8,128)(2,1)S(1)} %bitcast.4), custom_call_target="tpu_custom_call" | custom-call | tf_op jit(solution)/shard_map/pallas_call | solution.py:336
  61.8 1.4 %collective-permute-done.1.other_ref = bf16[16,552,128]{2,1,0:T(8,128)(2,1)S(1)} collective-permute-done((bf16[16,552,128]{2,1,0:T(8,128)(2,1)S(1)}, bf16[16,552,128]{2,1,0:T(8,128)(2,1)S(1)}, u32[]{:S(2)}, u32[]{:S(2)}) %collective-permute-start.1) | collective-permute-done | bytes 2261024 | tf_op jit(solution)/shard_map/ppermute | solution.py:389
  63.2 0.0 copy-done.2
  63.2 0.0 copy-start
  63.2 0.0 copy-start.3
  63.2 4.6 %shard_map.135 = (bf16[5,384,512]{2,1,0:T(8,128)(2,1)S(1)}, bf16[5,384,512]{2,1,0:T(8,128)(2,1)S(1)}, bf16[5,384,512]{2,1,0:T(8,128)(2,1)S(1)}, bf16[5,384,512]{...) custom-call(s32[2,1,8]{2,1,0:T(1,128)S(1)} %copy-done.2, ...), custom_call_target="tpu_custom_call", output_to_operand_aliasing={{0}: (4, {}), {1}: (5, {}), {2}: (6, {}), {3}: (7, {}), {4}... | custom-call | tf_op jit(solution)/shard_map/pallas_call | solution.py:336
  67.9 5.5 %collective-permute-start.2 = (bf16[48,768]{1,0:T(8,128)(2,1)S(1)}, bf16[48,768]{1,0:T(8,128)(2,1)S(1)}, u32[]{:S(2)}, u32[]{:S(2)}) collective-permute-start(bf16[48,768]{1,0:T(8,128)(2,1)S(1)} %get-tuple-element.36.piece_ref), channel_id=1, source_target_pairs={{0,64},{1,65},{2,66},{3,67},{4,68},{5,69},{6,70},{7,71},{8,72},{9,... | collective-permute-start | bytes 221192 | tf_op jit(solution)/shard_map/ppermute | solution.py:380
  73.4 0.0 copy-done
  73.4 0.0 copy-done.3
  73.4 1.7 %shard_map.136.refs_0_.dense_ref = f32[384,192]{1,0:T(8,128)S(1)} custom-call(s32[2,1,8]{2,1,0:T(1,128)S(1)} %copy-done.3, s32[1,1]{1,0:T(1,128)S(6)} %copy.33.dcnt_ref, bf16[92,736]{1,0:T(8,128)(2,1)S(1)} %copy-done, s32[16,128]{1,0:T(8,128)S(1)} %get-tuple-element.31.after_ref.code_ref), custom_call_target="tpu_custom_call" | custom-call | tf_op jit(solution)/shard_map/pallas_call | solution.py:336
  75.1 0.0 copy-start.4
  75.2 2.2 %collective-permute-done.2.far_ref = bf16[48,768]{1,0:T(8,128)(2,1)S(1)} collective-permute-done((bf16[48,768]{1,0:T(8,128)(2,1)S(1)}, bf16[48,768]{1,0:T(8,128)(2,1)S(1)}, u32[]{:S(2)}, u32[]{:S(2)}) %collective-permute-start.2) | collective-permute-done | bytes 73760 | tf_op jit(solution)/shard_map/ppermute | solution.py:380
  77.3 0.1 shard_map.137
  77.4 20.2 %all_to_all.16 = bf16[8,2,48,768]{3,2,1,0:T(8,128)(2,1)S(1)} all-to-all(bf16[8,2,48,768]{3,2,1,0:T(8,128)(2,1)S(1)} %shard_map.137), channel_id=1, replica_groups={{0,32,128,160,256,288,384,416},{1,33,129,161,257,289,385,417},{2,34,130..., dimensions={0} | all-to-all | bytes 2359296 | tf_op jit(solution)/shard_map/all_to_all | solution.py:384
  97.6 0.0 copy-done.4
  97.6 4.0 %shard_map.138 = (f32[384,192]{1,0:T(8,128)S(1)}, bf16[48,768]{1,0:T(8,128)(2,1)S(1)}) custom-call(s32[16,128]{1,0:T(8,128)S(1)} %get-tuple-element.31.after_ref.code_ref, s32[2,1,8]{2,1,0:T(1,128)S(1)} %copy-done.4, s32[1,1]{1,0:T(1,128)S(6)} %copy.35.scnt_ref.count_ref, bf16[5,384,512]{2,1,0:T(8,128)(2,1)S(1)} %get-tuple-element.32.h0, ...), custom_call_target="tpu_custom_call" | custom-call | tf_op jit(solution)/shard_map/pallas_call | solution.py:336
  101.6 0.0 copy-start.5
  101.6 1.9 %collective-permute-start.3 = (bf16[48,768]{1,0:T(8,128)(2,1)S(1)}, bf16[48,768]{1,0:T(8,128)(2,1)S(1)}, u32[]{:S(2)}, u32[]{:S(2)}) collective-permute-start(bf16[48,768]{1,0:T(8,128)(2,1)S(1)} %get-tuple-element.37.piece_ref), channel_id=1, source_target_pairs={{0,64},{1,65},{2,66},{3,67},{4,68},{5,69},{6,70},{7,71},{8,72},{9,... | collective-permute-start | bytes 221192 | tf_op jit(solution)/shard_map/ppermute | solution.py:380
  104.2 3.4 %collective-permute-done.3.far_ref = bf16[48,768]{1,0:T(8,128)(2,1)S(1)} collective-permute-done((bf16[48,768]{1,0:T(8,128)(2,1)S(1)}, bf16[48,768]{1,0:T(8,128)(2,1)S(1)}, u32[]{:S(2)}, u32[]{:S(2)}) %collective-permute-start.3) | collective-permute-done | bytes 73760 | tf_op jit(solution)/shard_map/ppermute | solution.py:380
  107.6 0.1 shard_map.139
  107.7 16.7 %all_to_all.17 = bf16[8,2,48,768]{3,2,1,0:T(8,128)(2,1)S(1)} all-to-all(bf16[8,2,48,768]{3,2,1,0:T(8,128)(2,1)S(1)} %shard_map.139), channel_id=1, replica_groups={{0,32,128,160,256,288,384,416},{1,33,129,161,257,289,385,417},{2,34,130..., dimensions={0} | all-to-all | bytes 2359296 | tf_op jit(solution)/shard_map/all_to_all | solution.py:384
  124.4 0.0 copy-done.5
  124.4 3.6 %shard_map.140.own_ref = f32[1152,128]{1,0:T(8,128)S(1)} custom-call(s32[16,128]{1,0:T(8,128)S(1)} %get-tuple-element.31.after_ref.code_ref, s32[2,1,8]{2,1,0:T(1,128)S(1)} %copy-done.5, s32[1,1]{1,0:T(1,128)S(6)} %copy.36.refs_0_.count_ref, bf16[5,384,512]{2,1,0:T(8,128)(2,1)S(1)} %get-tuple-element.32.h0, bf16[5,384,512]{2,1,0:T(8,128)(2,1)S(1)} %get-tuple-element.33.h1, ...), custom_call_target="tpu_custom_call" | custom-call | tf_op jit(solution)/shard_map/pallas_call | solution.py:336
  128.0 6.2 %collective-permute-start.4 = (f32[1152,128]{1,0:T(8,128)S(1)}, f32[1152,128]{1,0:T(8,128)S(1)}, u32[]{:S(2)}, u32[]{:S(2)}) collective-permute-start(f32[1152,128]{1,0:T(8,128)S(1)} %shard_map.140.own_ref), channel_id=1, source_target_pairs={{0,1},{1,0},{2,3},{3,2},{4,5},{5,4},{6,7},{7,6},{8,9},{9,8},{10,11... | collective-permute-start | bytes 1769480 | tf_op jit(solution)/shard_map/ppermute | solution.py:389
  134.3 0.6 shard_map.141
  134.9 1.0 collective-permute-done.4.other_ref
  135.9 1.5 %shard_map.142 = (f32[368,368]{1,0:T(8,128)}, f32[368,368]{1,0:T(8,128)}) custom-call(f32[1152,128]{1,0:T(8,128)S(1)} %collective-permute-done.4.other_ref, f32[368,368]{1,0:T(8,128)S(1)} %get-tuple-element.40.real_ref, f32[368,368]{1,0:T(8,128)S(1)} %get-tuple-element.41.imag_ref), custom_call_target="tpu_custom_call" | custom-call | tf_op jit(solution)/shard_map/pallas_call | solution.py:336
Async XLA Ops:
  5.0 11.1 %collective-permute-start = (bf16[552,128]{1,0:T(8,128)(2,1)}, bf16[552,128]{1,0:T(8,128)(2,1)S(1)}, u32[]{:S(2)}, u32[]{:S(2)}) collective-permute-start(bf16[552,128]{1,0:T(8,128)(2,1)} %shard_map.131.piece_ref), channel_id=1, source_target_pairs={{0,128},{1,3},{2,130},{3,1},{4,132},{5,7},{6,134},{7,5},{8,136},{9... | collective-permute-start | bytes 423944 | tf_op jit(solution)/shard_map/ppermute | solution.py:380
  13.3 0.9 copy-start.1
  56.8 6.4 %copy-start.2 = (s32[2,1,8]{2,1,0:T(1,128)S(1)}, s32[2,1,8]{2,1,0:T(1,128)}, u32[]{:S(2)}) copy-start(s32[2,1,8]{2,1,0:T(1,128)} %index_ref.3) | copy-start | bytes 196
  56.8 6.4 %collective-permute-start.1 = (bf16[16,552,128]{2,1,0:T(8,128)(2,1)S(1)}, bf16[16,552,128]{2,1,0:T(8,128)(2,1)S(1)}, u32[]{:S(2)}, u32[]{:S(2)}) collective-permute-start(bf16[16,552,128]{2,1,0:T(8,128)(2,1)S(1)} %bitcast.3), channel_id=1, source_target_pairs={{0,1},{1,0},{2,3},{3,2},{4,5},{5,4},{6,7},{7,6},{8,9},{9,8},{10,11... | collective-permute-start | bytes 6782984 | tf_op jit(solution)/shard_map/ppermute | solution.py:389
  63.2 10.1 %copy-start = (bf16[92,736]{1,0:T(8,128)(2,1)S(1)}, bf16[92,736]{1,0:T(8,128)(2,1)}, u32[]{:S(2)}) copy-start(bf16[92,736]{1,0:T(8,128)(2,1)} %dens_ref.1) | copy-start | bytes 406276
  63.2 10.1 %copy-start.3 = (s32[2,1,8]{2,1,0:T(1,128)S(1)}, s32[2,1,8]{2,1,0:T(1,128)}, u32[]{:S(2)}) copy-start(s32[2,1,8]{2,1,0:T(1,128)} %didx_ref.1) | copy-start | bytes 196
  67.9 9.4 %collective-permute-start.2 = (bf16[48,768]{1,0:T(8,128)(2,1)S(1)}, bf16[48,768]{1,0:T(8,128)(2,1)S(1)}, u32[]{:S(2)}, u32[]{:S(2)}) collective-permute-start(bf16[48,768]{1,0:T(8,128)(2,1)S(1)} %get-tuple-element.36.piece_ref), channel_id=1, source_target_pairs={{0,64},{1,65},{2,66},{3,67},{4,68},{5,69},{6,70},{7,71},{8,72},{9,... | collective-permute-start | bytes 221192 | tf_op jit(solution)/shard_map/ppermute | solution.py:380
  75.1 22.4 %copy-start.4 = (s32[2,1,8]{2,1,0:T(1,128)S(1)}, s32[2,1,8]{2,1,0:T(1,128)}, u32[]{:S(2)}) copy-start(s32[2,1,8]{2,1,0:T(1,128)} %index_ref.4) | copy-start | bytes 196
  101.6 22.9 %copy-start.5 = (s32[2,1,8]{2,1,0:T(1,128)S(1)}, s32[2,1,8]{2,1,0:T(1,128)}, u32[]{:S(2)}) copy-start(s32[2,1,8]{2,1,0:T(1,128)} %index_ref.5) | copy-start | bytes 196
  101.6 6.0 %collective-permute-start.3 = (bf16[48,768]{1,0:T(8,128)(2,1)S(1)}, bf16[48,768]{1,0:T(8,128)(2,1)S(1)}, u32[]{:S(2)}, u32[]{:S(2)}) collective-permute-start(bf16[48,768]{1,0:T(8,128)(2,1)S(1)} %get-tuple-element.37.piece_ref), channel_id=1, source_target_pairs={{0,64},{1,65},{2,66},{3,67},{4,68},{5,69},{6,70},{7,71},{8,72},{9,... | collective-permute-start | bytes 221192 | tf_op jit(solution)/shard_map/ppermute | solution.py:380
  128.0 7.8 %collective-permute-start.4 = (f32[1152,128]{1,0:T(8,128)S(1)}, f32[1152,128]{1,0:T(8,128)S(1)}, u32[]{:S(2)}, u32[]{:S(2)}) collective-permute-start(f32[1152,128]{1,0:T(8,128)S(1)} %shard_map.140.own_ref), channel_id=1, source_target_pairs={{0,1},{1,0},{2,3},{3,2},{4,5},{5,4},{6,7},{7,6},{8,9},{9,8},{10,11... | collective-permute-start | bytes 1769480 | tf_op jit(solution)/shard_map/ppermute | solution.py:389

commit v9 on v8

--- a/solution.py
+++ b/solution.py
@@ -80,8 +80,8 @@
         store(wire, (hidx_ref, hcnt_ref))
 
 
-def dense_kernel(didx_ref, dcnt_ref, dens_ref, after_ref, dense_ref):
-    del after_ref
+def dense_kernel(didx_ref, dcnt_ref, fidx_ref, fcnt_ref, dens_ref, total_ref, dense_ref, first_ref):
+    first_ref[...] = keep(all_codes(fidx_ref, fcnt_ref), total_ref[...])
     layer = lax.axis_index("layer")
     dens = dens_ref[...]
     dense_ref[...] = jnp.zeros_like(dense_ref)
@@ -247,17 +247,21 @@
         pipelined(lambda g: unpack_dens(code_ref, g, other_ref, 1, right_refs[g]))
 
     codes = all_codes(index_ref, count_ref)
-    term = keep(codes, total_ref[...])
-    term_ref[...] = term
-    pack(codes, term, rounded_ref, out_ref)
-
-
-def second_kernel(code_ref, index_ref, count_ref, h0, h1, h2, h3, wire_ref, dense_ref, real_ref,
-                  out_ref, r0, r1, r2, r3, rounded_ref):
+    term_ref[...] = total_ref[...]
+    pack(codes, total_ref[...], rounded_ref, out_ref)
+
+
+def second_kernel(code_ref, index_ref, count_ref, h0, h1, h2, h3, wire_ref, term_ref, out_ref, r0, r1,
+                  r2, r3, rounded_ref):
     codes = all_codes(index_ref, count_ref)
-    term = keep(codes, product((h0, h1, h2, h3), code_ref, 1, wire_ref, (r0, r1, r2, r3)))
+    total = product((h0, h1, h2, h3), code_ref, 1, wire_ref, (r0, r1, r2, r3))
+    term_ref[...] = total
+    pack(codes, total, rounded_ref, out_ref)
+
+
+def real_kernel(index_ref, count_ref, total_ref, dense_ref, real_ref):
+    term = keep(all_codes(index_ref, count_ref), total_ref[...])
     real_ref[...] = dense_ref[...] - 0.5 * term
-    pack(codes, term, rounded_ref, out_ref)
 
 
 def third_kernel(code_ref, index_ref, count_ref, h0, h1, h2, h3, wire_ref, first_ref, real_ref,
@@ -426,9 +430,12 @@
         [pltpu.VMEM((BT * ROWS, BT * COLS), F32), rounded] + reading,
         alias={4 + n: n for n in range(8)},
     )
-    ham, (codes, first_term, first_wire) = out[0:4], out[8:]
-    dense_half = call(
-        dense_kernel, [SMEM, SMEM, VMEM, VMEM], (dens_index, dens_count, dens_blocks, codes), half
+    ham, (codes, first_total, first_wire) = out[0:4], out[8:]
+    dense_half, first_term = call(
+        dense_kernel,
+        [SMEM] * 4 + [VMEM] * 2,
+        (dens_index, dens_count, first_index, first_count, dens_blocks, first_total),
+        (half, half),
     )
     pairs = call(
         lay_kernel,
@@ -436,17 +443,20 @@
         (first_wire, to_pair(first_wire, False), dense_half),
         wires,
     )
-    real_half, second_wire = call(
+    second_total, second_wire = call(
         second_kernel,
-        [SMEM] * 3 + [VMEM] * 6,
-        (codes, second_index, second_count, *ham, spread(pairs, False), dense_half),
+        [SMEM] * 3 + [VMEM] * 5,
+        (codes, second_index, second_count, *ham, spread(pairs, False)),
         (half, wire),
         dense_right + [rounded],
     )
+    real_half = call(
+        real_kernel, [SMEM] * 2 + [VMEM] * 2, (second_index, second_count, second_total, dense_half), half
+    )
     pairs = call(
         lay_kernel,
-        [VMEM, VMEM, SMEM],
-        (second_wire, to_pair(second_wire, False), third_count),
+        [VMEM, VMEM, SMEM, VMEM],
+        (second_wire, to_pair(second_wire, False), third_count, real_half),
         wires,
     )
     halves = call(

time: 138 us -> 137 us (level)
    pallas_call x12 -> x13, Pallas kernels: 21.3 us -> 21.9 us  [call(): pl.pallas_call(kernel, out_shape=out_shape, in_specs=in_specs, out_specs=...]
  transfers between devices with their start and end apart: 5 -> 5, of which waited for: 5 -> 5; matrix products, arithmetic and copies ran while one was open for 0% -> 0% of each run, Pallas kernels for 4% -> 5%
where the time goes in v9:
time: 137 us
  blocking collectives  77.5 us (57%)
  starting transfers between devices  24 us (18%)
  Pallas kernels  21.9 us (16%)
  waiting for transfers between devices  8.4 us (6%)
  between operations  4.01 us (3%)
    all_to_all x3, blocking collectives, spread(): tiles = lax.all_to_all(pairs, AXES, 0, 0, axis_index_groups=groups(both))  77.5 us
    pallas_call x13, Pallas kernels, call(): pl.pallas_call(kernel, out_shape=out_shape, in_specs=in_specs, out_specs=...  21.9 us
    ppermute x3, starting transfers between devices, to_pair(): return lax.ppermute(piece, AXES, pair_route(both))  15.7 us
    ppermute x2, starting transfers between devices, swap(): return lax.ppermute(values, 'layer', [(0, 1), (1, 0)])  8.27 us
    ppermute x3, waiting for transfers between devices, to_pair(): return lax.ppermute(piece, AXES, pair_route(both))  6.01 us
  transfers between devices with their start and end apart: 5, of which 5 were waited for; matrix products, arithmetic and copies ran while one was open for 0% of the time, Pallas kernels for 5%

profile of v9, /device:TPU:1, one launch (start us, length us, event | category | flops | bytes accessed | tf_op | source)
XLA Modules:
  0.0 136.8 jit_solution(11582151724040939134)
XLA Ops:
  3.2 1.8 %shard_map.131.piece_ref = bf16[552,128]{1,0:T(8,128)(2,1)} custom-call(s32[2,1,8]{2,1,0:T(1,128)} %hidx_hbm.1, s32[1,1]{1,0:T(1,128)S(6)} %copy.32.hcnt_ref, s32[2,1,8]{2,1,0:T(1,128)} %didx_ref.1, s32[1,1]{1,0:T(1,128)S(6)} %copy.33.dcnt_ref, s32[2,1,8]{2,1,0:T(1,128)} %fidx_ref.1, s32[1,1]{1,0:T(1,128)S(6)} %copy.34.fcnt_ref.count_ref, ...), custom_call_target="tpu_custom_call" | custom-call | tf_op jit(solution)/shard_map/pallas_call | solution.py:340
  5.0 8.3 %collective-permute-start = (bf16[552,128]{1,0:T(8,128)(2,1)}, bf16[552,128]{1,0:T(8,128)(2,1)S(1)}, u32[]{:S(2)}, u32[]{:S(2)}) collective-permute-start(bf16[552,128]{1,0:T(8,128)(2,1)} %shard_map.131.piece_ref), channel_id=1, source_target_pairs={{0,128},{1,3},{2,130},{3,1},{4,132},{5,7},{6,134},{7,5},{8,136},{9... | collective-permute-start | bytes 423944 | tf_op jit(solution)/shard_map/ppermute | solution.py:384
  13.3 0.0 copy-start.1
  13.3 0.9 copy-done.1
  14.2 0.2 shard_map.132.pairs_ref
  14.4 1.7 %collective-permute-done.far_ref = bf16[552,128]{1,0:T(8,128)(2,1)S(1)} collective-permute-done((bf16[552,128]{1,0:T(8,128)(2,1)}, bf16[552,128]{1,0:T(8,128)(2,1)S(1)}, u32[]{:S(2)}, u32[]{:S(2)}) %collective-permute-start) | collective-permute-done | bytes 141344 | tf_op jit(solution)/shard_map/ppermute | solution.py:384
  16.1 0.2 shard_map.133
  16.2 40.6 %all_to_all.15 = bf16[8,2,552,128]{3,2,1,0:T(8,128)(2,1)S(1)} all-to-all(bf16[8,2,552,128]{3,2,1,0:T(8,128)(2,1)S(1)} %shard_map.133), channel_id=1, replica_groups={{0,32,64,96,256,288,320,352},{1,5,9,13,17,21,25,29},{2,34,66,98,258,290..., dimensions={0} | all-to-all | bytes 4521984 | tf_op jit(solution)/shard_map/all_to_all | solution.py:388
  56.8 0.0 copy-start.2
  56.8 2.0 %collective-permute-start.1 = (bf16[16,552,128]{2,1,0:T(8,128)(2,1)S(1)}, bf16[16,552,128]{2,1,0:T(8,128)(2,1)S(1)}, u32[]{:S(2)}, u32[]{:S(2)}) collective-permute-start(bf16[16,552,128]{2,1,0:T(8,128)(2,1)S(1)} %bitcast.3), channel_id=1, source_target_pairs={{0,1},{1,0},{2,3},{3,2},{4,5},{5,4},{6,7},{7,6},{8,9},{9,8},{10,11... | collective-permute-start | bytes 6782984 | tf_op jit(solution)/shard_map/ppermute | solution.py:393
  58.9 2.9 %shard_map.134 = (bf16[5,384,512]{2,1,0:T(8,128)(2,1)S(1)}, bf16[5,384,512]{2,1,0:T(8,128)(2,1)S(1)}, bf16[5,384,512]{2,1,0:T(8,128)(2,1)S(1)}, bf16[5,384,512]{...) custom-call(bf16[16,552,128]{2,1,0:T(8,128)(2,1)S(1)} %bitcast.4), custom_call_target="tpu_custom_call" | custom-call | tf_op jit(solution)/shard_map/pallas_call | solution.py:340
  61.8 1.4 %collective-permute-done.1.other_ref = bf16[16,552,128]{2,1,0:T(8,128)(2,1)S(1)} collective-permute-done((bf16[16,552,128]{2,1,0:T(8,128)(2,1)S(1)}, bf16[16,552,128]{2,1,0:T(8,128)(2,1)S(1)}, u32[]{:S(2)}, u32[]{:S(2)}) %collective-permute-start.1) | collective-permute-done | bytes 2261024 | tf_op jit(solution)/shard_map/ppermute | solution.py:393
  63.2 0.0 copy-done.2
  63.2 0.0 copy-start
  63.2 0.0 copy-start.4
  63.2 4.2 %shard_map.135 = (bf16[5,384,512]{2,1,0:T(8,128)(2,1)S(1)}, bf16[5,384,512]{2,1,0:T(8,128)(2,1)S(1)}, bf16[5,384,512]{2,1,0:T(8,128)(2,1)S(1)}, bf16[5,384,512]{...) custom-call(s32[2,1,8]{2,1,0:T(1,128)S(1)} %copy-done.2, ...), custom_call_target="tpu_custom_call", output_to_operand_aliasing={{0}: (4, {}), {1}: (5, {}), {2}: (6, {}), {3}: (7, {}), {4}... | custom-call | tf_op jit(solution)/shard_map/pallas_call | solution.py:340
  67.4 5.5 %collective-permute-start.2 = (bf16[48,768]{1,0:T(8,128)(2,1)S(1)}, bf16[48,768]{1,0:T(8,128)(2,1)S(1)}, u32[]{:S(2)}, u32[]{:S(2)}) collective-permute-start(bf16[48,768]{1,0:T(8,128)(2,1)S(1)} %get-tuple-element.38.piece_ref), channel_id=1, source_target_pairs={{0,64},{1,65},{2,66},{3,67},{4,68},{5,69},{6,70},{7,71},{8,72},{9,... | collective-permute-start | bytes 221192 | tf_op jit(solution)/shard_map/ppermute | solution.py:384
  73.0 0.0 copy-done
  73.0 0.0 copy-done.4
  73.0 2.1 %shard_map.136 = (f32[384,192]{1,0:T(8,128)S(1)}, f32[384,192]{1,0:T(8,128)S(1)}) custom-call(s32[2,1,8]{2,1,0:T(1,128)S(1)} %copy-done.4, s32[1,1]{1,0:T(1,128)S(6)} %copy.33.dcnt_ref, s32[2,1,8]{2,1,0:T(1,128)S(1)} %copy-done.2, s32[1,1]{1,0:T(1,128)S(6)} %copy.34.fcnt_ref.count_ref, bf16[92,736]{1,0:T(8,128)(2,1)S(1)} %copy-done, ...), custom_call_target="tpu_custom_call" | custom-call | tf_op jit(solution)/shard_map/pallas_call | solution.py:340
  75.1 1.8 %collective-permute-done.2.far_ref = bf16[48,768]{1,0:T(8,128)(2,1)S(1)} collective-permute-done((bf16[48,768]{1,0:T(8,128)(2,1)S(1)}, bf16[48,768]{1,0:T(8,128)(2,1)S(1)}, u32[]{:S(2)}, u32[]{:S(2)}) %collective-permute-start.2) | collective-permute-done | bytes 73760 | tf_op jit(solution)/shard_map/ppermute | solution.py:384
  76.9 0.0 copy-start.3
  76.9 0.1 shard_map.137
  77.0 20.2 %all_to_all.16 = bf16[8,2,48,768]{3,2,1,0:T(8,128)(2,1)S(1)} all-to-all(bf16[8,2,48,768]{3,2,1,0:T(8,128)(2,1)S(1)} %shard_map.137), channel_id=1, replica_groups={{0,32,128,160,256,288,384,416},{1,33,129,161,257,289,385,417},{2,34,130..., dimensions={0} | all-to-all | bytes 2359296 | tf_op jit(solution)/shard_map/all_to_all | solution.py:388
  97.2 0.0 copy-done.3
  97.2 3.8 %shard_map.138 = (f32[384,192]{1,0:T(8,128)S(1)}, bf16[48,768]{1,0:T(8,128)(2,1)S(1)}) custom-call(s32[16,128]{1,0:T(8,128)S(1)} %get-tuple-element.33.code_ref, s32[2,1,8]{2,1,0:T(1,128)S(1)} %copy-done.3, s32[1,1]{1,0:T(1,128)S(6)} %copy.35.scnt_ref.count_ref, bf16[5,384,512]{2,1,0:T(8,128)(2,1)S(1)} %get-tuple-element.34.h0, ...), custom_call_target="tpu_custom_call" | custom-call | tf_op jit(solution)/shard_map/pallas_call | solution.py:340
  101.0 1.9 %collective-permute-start.3 = (bf16[48,768]{1,0:T(8,128)(2,1)S(1)}, bf16[48,768]{1,0:T(8,128)(2,1)S(1)}, u32[]{:S(2)}, u32[]{:S(2)}) collective-permute-start(bf16[48,768]{1,0:T(8,128)(2,1)S(1)} %get-tuple-element.41.piece_ref), channel_id=1, source_target_pairs={{0,64},{1,65},{2,66},{3,67},{4,68},{5,69},{6,70},{7,71},{8,72},{9,... | collective-permute-start | bytes 221192 | tf_op jit(solution)/shard_map/ppermute | solution.py:384
  103.5 0.9 shard_map.139.refs_1_.real_ref
  104.5 0.0 copy-start.5
  104.5 2.5 %collective-permute-done.3.far_ref = bf16[48,768]{1,0:T(8,128)(2,1)S(1)} collective-permute-done((bf16[48,768]{1,0:T(8,128)(2,1)S(1)}, bf16[48,768]{1,0:T(8,128)(2,1)S(1)}, u32[]{:S(2)}, u32[]{:S(2)}) %collective-permute-start.3) | collective-permute-done | bytes 73760 | tf_op jit(solution)/shard_map/ppermute | solution.py:384
  107.0 0.1 shard_map.140
  107.0 16.7 %all_to_all.17 = bf16[8,2,48,768]{3,2,1,0:T(8,128)(2,1)S(1)} all-to-all(bf16[8,2,48,768]{3,2,1,0:T(8,128)(2,1)S(1)} %shard_map.140), channel_id=1, replica_groups={{0,32,128,160,256,288,384,416},{1,33,129,161,257,289,385,417},{2,34,130..., dimensions={0} | all-to-all | bytes 2359296 | tf_op jit(solution)/shard_map/all_to_all | solution.py:388
  123.8 0.0 copy-done.5
  123.8 3.6 %shard_map.141.own_ref = f32[1152,128]{1,0:T(8,128)S(1)} custom-call(s32[16,128]{1,0:T(8,128)S(1)} %get-tuple-element.33.code_ref, s32[2,1,8]{2,1,0:T(1,128)S(1)} %copy-done.5, s32[1,1]{1,0:T(1,128)S(6)} %copy.36.refs_0_.count_ref, bf16[5,384,512]{2,1,0:T(8,128)(2,1)S(1)} %get-tuple-element.34.h0, bf16[5,384,512]{2,1,0:T(8,128)(2,1)S(1)} %get-tuple-element.35.h1, ...), custom_call_target="tpu_custom_call" | custom-call | tf_op jit(solution)/shard_map/pallas_call | solution.py:340
  127.4 6.2 %collective-permute-start.4 = (f32[1152,128]{1,0:T(8,128)S(1)}, f32[1152,128]{1,0:T(8,128)S(1)}, u32[]{:S(2)}, u32[]{:S(2)}) collective-permute-start(f32[1152,128]{1,0:T(8,128)S(1)} %shard_map.141.own_ref), channel_id=1, source_target_pairs={{0,1},{1,0},{2,3},{3,2},{4,5},{5,4},{6,7},{7,6},{8,9},{9,8},{10,11... | collective-permute-start | bytes 1769480 | tf_op jit(solution)/shard_map/ppermute | solution.py:393
  133.6 0.6 shard_map.142
  134.3 1.0 collective-permute-done.4.other_ref
  135.2 1.5 %shard_map.143 = (f32[368,368]{1,0:T(8,128)}, f32[368,368]{1,0:T(8,128)}) custom-call(f32[1152,128]{1,0:T(8,128)S(1)} %collective-permute-done.4.other_ref, f32[368,368]{1,0:T(8,128)S(1)} %get-tuple-element.44.real_ref, f32[368,368]{1,0:T(8,128)S(1)} %get-tuple-element.45.imag_ref), custom_call_target="tpu_custom_call" | custom-call | tf_op jit(solution)/shard_map/pallas_call | solution.py:340
Async XLA Ops:
  5.0 11.1 %collective-permute-start = (bf16[552,128]{1,0:T(8,128)(2,1)}, bf16[552,128]{1,0:T(8,128)(2,1)S(1)}, u32[]{:S(2)}, u32[]{:S(2)}) collective-permute-start(bf16[552,128]{1,0:T(8,128)(2,1)} %shard_map.131.piece_ref), channel_id=1, source_target_pairs={{0,128},{1,3},{2,130},{3,1},{4,132},{5,7},{6,134},{7,5},{8,136},{9... | collective-permute-start | bytes 423944 | tf_op jit(solution)/shard_map/ppermute | solution.py:384
  13.3 0.9 copy-start.1
  56.8 6.4 %copy-start.2 = (s32[2,1,8]{2,1,0:T(1,128)S(1)}, s32[2,1,8]{2,1,0:T(1,128)}, u32[]{:S(2)}) copy-start(s32[2,1,8]{2,1,0:T(1,128)} %fidx_ref.1) | copy-start | bytes 196
  56.8 6.4 %collective-permute-start.1 = (bf16[16,552,128]{2,1,0:T(8,128)(2,1)S(1)}, bf16[16,552,128]{2,1,0:T(8,128)(2,1)S(1)}, u32[]{:S(2)}, u32[]{:S(2)}) collective-permute-start(bf16[16,552,128]{2,1,0:T(8,128)(2,1)S(1)} %bitcast.3), channel_id=1, source_target_pairs={{0,1},{1,0},{2,3},{3,2},{4,5},{5,4},{6,7},{7,6},{8,9},{9,8},{10,11... | collective-permute-start | bytes 6782984 | tf_op jit(solution)/shard_map/ppermute | solution.py:393
  63.2 9.7 %copy-start = (bf16[92,736]{1,0:T(8,128)(2,1)S(1)}, bf16[92,736]{1,0:T(8,128)(2,1)}, u32[]{:S(2)}) copy-start(bf16[92,736]{1,0:T(8,128)(2,1)} %dens_ref.1) | copy-start | bytes 406276
  63.2 9.7 %copy-start.4 = (s32[2,1,8]{2,1,0:T(1,128)S(1)}, s32[2,1,8]{2,1,0:T(1,128)}, u32[]{:S(2)}) copy-start(s32[2,1,8]{2,1,0:T(1,128)} %didx_ref.1) | copy-start | bytes 196
  67.4 9.5 %collective-permute-start.2 = (bf16[48,768]{1,0:T(8,128)(2,1)S(1)}, bf16[48,768]{1,0:T(8,128)(2,1)S(1)}, u32[]{:S(2)}, u32[]{:S(2)}) collective-permute-start(bf16[48,768]{1,0:T(8,128)(2,1)S(1)} %get-tuple-element.38.piece_ref), channel_id=1, source_target_pairs={{0,64},{1,65},{2,66},{3,67},{4,68},{5,69},{6,70},{7,71},{8,72},{9,... | collective-permute-start | bytes 221192 | tf_op jit(solution)/shard_map/ppermute | solution.py:384
  76.9 20.3 %copy-start.3 = (s32[2,1,8]{2,1,0:T(1,128)S(1)}, s32[2,1,8]{2,1,0:T(1,128)}, u32[]{:S(2)}) copy-start(s32[2,1,8]{2,1,0:T(1,128)} %index_ref.6) | copy-start | bytes 196
  101.0 6.0 %collective-permute-start.3 = (bf16[48,768]{1,0:T(8,128)(2,1)S(1)}, bf16[48,768]{1,0:T(8,128)(2,1)S(1)}, u32[]{:S(2)}, u32[]{:S(2)}) collective-permute-start(bf16[48,768]{1,0:T(8,128)(2,1)S(1)} %get-tuple-element.41.piece_ref), channel_id=1, source_target_pairs={{0,64},{1,65},{2,66},{3,67},{4,68},{5,69},{6,70},{7,71},{8,72},{9,... | collective-permute-start | bytes 221192 | tf_op jit(solution)/shard_map/ppermute | solution.py:384
  104.5 19.3 %copy-start.5 = (s32[2,1,8]{2,1,0:T(1,128)S(1)}, s32[2,1,8]{2,1,0:T(1,128)}, u32[]{:S(2)}) copy-start(s32[2,1,8]{2,1,0:T(1,128)} %index_ref.7) | copy-start | bytes 196
  127.4 7.8 %collective-permute-start.4 = (f32[1152,128]{1,0:T(8,128)S(1)}, f32[1152,128]{1,0:T(8,128)S(1)}, u32[]{:S(2)}, u32[]{:S(2)}) collective-permute-start(f32[1152,128]{1,0:T(8,128)S(1)} %shard_map.141.own_ref), channel_id=1, source_target_pairs={{0,1},{1,0},{2,3},{3,2},{4,5},{5,4},{6,7},{7,6},{8,9},{9,8},{10,11... | collective-permute-start | bytes 1769480 | tf_op jit(solution)/shard_map/ppermute | solution.py:393

commit v10 on v9

--- a/solution.py
+++ b/solution.py
@@ -46,13 +46,13 @@
 def prep_kernel(hidx_hbm, hcnt_ref, didx_hbm, dcnt_ref, fidx_hbm, fcnt_ref, sidx_hbm, scnt_ref,
                 ham_hbm, dens_hbm, out_ref, hidx_ref, didx_ref, fidx_ref, sidx_ref, ham_ref,
                 dens_ref, sems):
-    pairs = ((ham_hbm, ham_ref), (dens_hbm, dens_ref), (hidx_hbm, hidx_ref), (didx_hbm, didx_ref),
-             (fidx_hbm, fidx_ref), (sidx_hbm, sidx_ref))
-    copies = [pltpu.make_async_copy(src, dst, sems.at[n]) for n, (src, dst) in enumerate(pairs)]
-    for one in copies:
-        one.start()
-    for one in copies:
-        one.wait()
+    def fetch(*pairs):
+        copies = [pltpu.make_async_copy(src, dst, sems.at[n]) for n, (src, dst) in enumerate(pairs)]
+        for one in copies:
+            one.start()
+        for one in copies:
+            one.wait()
+
     layer = lax.axis_index("layer")
     lane = lax.broadcasted_iota(jnp.int32, (BLK, LANES), 1) - (META - TAIL)
 
@@ -67,6 +67,7 @@
 
     @pl.when(layer == 0)
     def _():
+        fetch((dens_hbm, dens_ref), (didx_hbm, didx_ref), (fidx_hbm, fidx_ref), (sidx_hbm, sidx_ref))
         dens = dens_ref[...]
         pieces = [dot_nt(one_hot((BLK, META), s * BLK, BLK), dens) for s in range(CAP)]
         store(
@@ -76,6 +77,7 @@
 
     @pl.when(layer == 1)
     def _():
+        fetch((ham_hbm, ham_ref), (hidx_hbm, hidx_ref))
         wire = jnp.concatenate([ham_ref[...].astype(F32), jnp.zeros((BLK, WIRE - META), F32)], axis=1)
         store(wire, (hidx_ref, hcnt_ref))
 
@@ -403,7 +405,7 @@
         (ham_index, ham_count, dens_index, dens_count, first_index, first_count, second_index,
          second_count, ham_blocks, dens_blocks),
         shape(WROWS, LANES),
-        [index] * 4 + [packed, packed, pltpu.SemaphoreType.DMA((6,))],
+        [index] * 4 + [packed, packed, pltpu.SemaphoreType.DMA((4,))],
         vmem=62900000,
     )
     half = shape(BT * ROWS, BT * COLS, dtype=F32)

time: 137 us -> 137 us (level)
  no operation moved by 1% of the time
where the time goes in v10:
time: 137 us
  blocking collectives  77.5 us (57%)
  starting transfers between devices  24 us (18%)
  Pallas kernels  21.8 us (16%)
  waiting for transfers between devices  8.4 us (6%)
  between operations  4.01 us (3%)
    all_to_all x3, blocking collectives, spread(): tiles = lax.all_to_all(pairs, AXES, 0, 0, axis_index_groups=groups(both))  77.5 us
    pallas_call x13, Pallas kernels, call(): pl.pallas_call(kernel, out_shape=out_shape, in_specs=in_specs, out_specs=...  21.8 us
    ppermute x3, starting transfers between devices, to_pair(): return lax.ppermute(piece, AXES, pair_route(both))  15.7 us
    ppermute x2, starting transfers between devices, swap(): return lax.ppermute(values, 'layer', [(0, 1), (1, 0)])  8.26 us
    ppermute x3, waiting for transfers between devices, to_pair(): return lax.ppermute(piece, AXES, pair_route(both))  6.01 us
  transfers between devices with their start and end apart: 5, of which 5 were waited for; matrix products, arithmetic and copies ran while one was open for 0% of the time, Pallas kernels for 5%

profile of v10, /device:TPU:1, one launch (start us, length us, event | category | flops | bytes accessed | tf_op | source)
XLA Modules:
  0.0 136.7 jit_solution(5103720193259397287)
XLA Ops:
  3.2 1.7 %shard_map.131.piece_ref = bf16[552,128]{1,0:T(8,128)(2,1)} custom-call(s32[2,1,8]{2,1,0:T(1,128)} %hidx_hbm.1, s32[1,1]{1,0:T(1,128)S(6)} %copy.32.hcnt_ref, s32[2,1,8]{2,1,0:T(1,128)} %didx_ref.1, s32[1,1]{1,0:T(1,128)S(6)} %copy.33.dcnt_ref, s32[2,1,8]{2,1,0:T(1,128)} %fidx_ref.1, s32[1,1]{1,0:T(1,128)S(6)} %copy.34.fcnt_ref.count_ref, ...), custom_call_target="tpu_custom_call" | custom-call | tf_op jit(solution)/shard_map/pallas_call | solution.py:342
  4.9 8.3 %collective-permute-start = (bf16[552,128]{1,0:T(8,128)(2,1)}, bf16[552,128]{1,0:T(8,128)(2,1)S(1)}, u32[]{:S(2)}, u32[]{:S(2)}) collective-permute-start(bf16[552,128]{1,0:T(8,128)(2,1)} %shard_map.131.piece_ref), channel_id=1, source_target_pairs={{0,128},{1,3},{2,130},{3,1},{4,132},{5,7},{6,134},{7,5},{8,136},{9... | collective-permute-start | bytes 423944 | tf_op jit(solution)/shard_map/ppermute | solution.py:386
  13.2 0.0 copy-start.1
  13.2 0.9 copy-done.1
  14.1 0.2 shard_map.132.pairs_ref
  14.3 1.7 %collective-permute-done.far_ref = bf16[552,128]{1,0:T(8,128)(2,1)S(1)} collective-permute-done((bf16[552,128]{1,0:T(8,128)(2,1)}, bf16[552,128]{1,0:T(8,128)(2,1)S(1)}, u32[]{:S(2)}, u32[]{:S(2)}) %collective-permute-start) | collective-permute-done | bytes 141344 | tf_op jit(solution)/shard_map/ppermute | solution.py:386
  16.0 0.2 shard_map.133
  16.1 40.6 %all_to_all.15 = bf16[8,2,552,128]{3,2,1,0:T(8,128)(2,1)S(1)} all-to-all(bf16[8,2,552,128]{3,2,1,0:T(8,128)(2,1)S(1)} %shard_map.133), channel_id=1, replica_groups={{0,32,64,96,256,288,320,352},{1,5,9,13,17,21,25,29},{2,34,66,98,258,290..., dimensions={0} | all-to-all | bytes 4521984 | tf_op jit(solution)/shard_map/all_to_all | solution.py:390
  56.7 0.0 copy-start.2
  56.7 2.0 %collective-permute-start.1 = (bf16[16,552,128]{2,1,0:T(8,128)(2,1)S(1)}, bf16[16,552,128]{2,1,0:T(8,128)(2,1)S(1)}, u32[]{:S(2)}, u32[]{:S(2)}) collective-permute-start(bf16[16,552,128]{2,1,0:T(8,128)(2,1)S(1)} %bitcast.3), channel_id=1, source_target_pairs={{0,1},{1,0},{2,3},{3,2},{4,5},{5,4},{6,7},{7,6},{8,9},{9,8},{10,11... | collective-permute-start | bytes 6782984 | tf_op jit(solution)/shard_map/ppermute | solution.py:395
  58.8 2.9 %shard_map.134 = (bf16[5,384,512]{2,1,0:T(8,128)(2,1)S(1)}, bf16[5,384,512]{2,1,0:T(8,128)(2,1)S(1)}, bf16[5,384,512]{2,1,0:T(8,128)(2,1)S(1)}, bf16[5,384,512]{...) custom-call(bf16[16,552,128]{2,1,0:T(8,128)(2,1)S(1)} %bitcast.4), custom_call_target="tpu_custom_call" | custom-call | tf_op jit(solution)/shard_map/pallas_call | solution.py:342
  61.7 1.4 %collective-permute-done.1.other_ref = bf16[16,552,128]{2,1,0:T(8,128)(2,1)S(1)} collective-permute-done((bf16[16,552,128]{2,1,0:T(8,128)(2,1)S(1)}, bf16[16,552,128]{2,1,0:T(8,128)(2,1)S(1)}, u32[]{:S(2)}, u32[]{:S(2)}) %collective-permute-start.1) | collective-permute-done | bytes 2261024 | tf_op jit(solution)/shard_map/ppermute | solution.py:395
  63.1 0.0 copy-done.2
  63.1 0.0 copy-start
  63.1 0.0 copy-start.4
  63.1 4.2 %shard_map.135 = (bf16[5,384,512]{2,1,0:T(8,128)(2,1)S(1)}, bf16[5,384,512]{2,1,0:T(8,128)(2,1)S(1)}, bf16[5,384,512]{2,1,0:T(8,128)(2,1)S(1)}, bf16[5,384,512]{...) custom-call(s32[2,1,8]{2,1,0:T(1,128)S(1)} %copy-done.2, ...), custom_call_target="tpu_custom_call", output_to_operand_aliasing={{0}: (4, {}), {1}: (5, {}), {2}: (6, {}), {3}: (7, {}), {4}... | custom-call | tf_op jit(solution)/shard_map/pallas_call | solution.py:342
  67.3 5.5 %collective-permute-start.2 = (bf16[48,768]{1,0:T(8,128)(2,1)S(1)}, bf16[48,768]{1,0:T(8,128)(2,1)S(1)}, u32[]{:S(2)}, u32[]{:S(2)}) collective-permute-start(bf16[48,768]{1,0:T(8,128)(2,1)S(1)} %get-tuple-element.38.piece_ref), channel_id=1, source_target_pairs={{0,64},{1,65},{2,66},{3,67},{4,68},{5,69},{6,70},{7,71},{8,72},{9,... | collective-permute-start | bytes 221192 | tf_op jit(solution)/shard_map/ppermute | solution.py:386
  72.9 0.0 copy-done
  72.9 0.0 copy-done.4
  72.9 2.1 %shard_map.136 = (f32[384,192]{1,0:T(8,128)S(1)}, f32[384,192]{1,0:T(8,128)S(1)}) custom-call(s32[2,1,8]{2,1,0:T(1,128)S(1)} %copy-done.4, s32[1,1]{1,0:T(1,128)S(6)} %copy.33.dcnt_ref, s32[2,1,8]{2,1,0:T(1,128)S(1)} %copy-done.2, s32[1,1]{1,0:T(1,128)S(6)} %copy.34.fcnt_ref.count_ref, bf16[92,736]{1,0:T(8,128)(2,1)S(1)} %copy-done, ...), custom_call_target="tpu_custom_call" | custom-call | tf_op jit(solution)/shard_map/pallas_call | solution.py:342
  74.9 1.8 %collective-permute-done.2.far_ref = bf16[48,768]{1,0:T(8,128)(2,1)S(1)} collective-permute-done((bf16[48,768]{1,0:T(8,128)(2,1)S(1)}, bf16[48,768]{1,0:T(8,128)(2,1)S(1)}, u32[]{:S(2)}, u32[]{:S(2)}) %collective-permute-start.2) | collective-permute-done | bytes 73760 | tf_op jit(solution)/shard_map/ppermute | solution.py:386
  76.8 0.0 copy-start.3
  76.8 0.1 shard_map.137
  76.9 20.2 %all_to_all.16 = bf16[8,2,48,768]{3,2,1,0:T(8,128)(2,1)S(1)} all-to-all(bf16[8,2,48,768]{3,2,1,0:T(8,128)(2,1)S(1)} %shard_map.137), channel_id=1, replica_groups={{0,32,128,160,256,288,384,416},{1,33,129,161,257,289,385,417},{2,34,130..., dimensions={0} | all-to-all | bytes 2359296 | tf_op jit(solution)/shard_map/all_to_all | solution.py:390
  97.0 0.0 copy-done.3
  97.0 3.8 %shard_map.138 = (f32[384,192]{1,0:T(8,128)S(1)}, bf16[48,768]{1,0:T(8,128)(2,1)S(1)}) custom-call(s32[16,128]{1,0:T(8,128)S(1)} %get-tuple-element.33.code_ref, s32[2,1,8]{2,1,0:T(1,128)S(1)} %copy-done.3, s32[1,1]{1,0:T(1,128)S(6)} %copy.35.scnt_ref.count_ref, bf16[5,384,512]{2,1,0:T(8,128)(2,1)S(1)} %get-tuple-element.34.h0, ...), custom_call_target="tpu_custom_call" | custom-call | tf_op jit(solution)/shard_map/pallas_call | solution.py:342
  100.8 1.9 %collective-permute-start.3 = (bf16[48,768]{1,0:T(8,128)(2,1)S(1)}, bf16[48,768]{1,0:T(8,128)(2,1)S(1)}, u32[]{:S(2)}, u32[]{:S(2)}) collective-permute-start(bf16[48,768]{1,0:T(8,128)(2,1)S(1)} %get-tuple-element.41.piece_ref), channel_id=1, source_target_pairs={{0,64},{1,65},{2,66},{3,67},{4,68},{5,69},{6,70},{7,71},{8,72},{9,... | collective-permute-start | bytes 221192 | tf_op jit(solution)/shard_map/ppermute | solution.py:386
  103.4 0.9 shard_map.139.refs_1_.real_ref
  104.3 0.0 copy-start.5
  104.4 2.5 %collective-permute-done.3.far_ref = bf16[48,768]{1,0:T(8,128)(2,1)S(1)} collective-permute-done((bf16[48,768]{1,0:T(8,128)(2,1)S(1)}, bf16[48,768]{1,0:T(8,128)(2,1)S(1)}, u32[]{:S(2)}, u32[]{:S(2)}) %collective-permute-start.3) | collective-permute-done | bytes 73760 | tf_op jit(solution)/shard_map/ppermute | solution.py:386
  106.8 0.1 shard_map.140
  106.9 16.8 %all_to_all.17 = bf16[8,2,48,768]{3,2,1,0:T(8,128)(2,1)S(1)} all-to-all(bf16[8,2,48,768]{3,2,1,0:T(8,128)(2,1)S(1)} %shard_map.140), channel_id=1, replica_groups={{0,32,128,160,256,288,384,416},{1,33,129,161,257,289,385,417},{2,34,130..., dimensions={0} | all-to-all | bytes 2359296 | tf_op jit(solution)/shard_map/all_to_all | solution.py:390
  123.7 0.0 copy-done.5
  123.7 3.6 %shard_map.141.own_ref = f32[1152,128]{1,0:T(8,128)S(1)} custom-call(s32[16,128]{1,0:T(8,128)S(1)} %get-tuple-element.33.code_ref, s32[2,1,8]{2,1,0:T(1,128)S(1)} %copy-done.5, s32[1,1]{1,0:T(1,128)S(6)} %copy.36.refs_0_.count_ref, bf16[5,384,512]{2,1,0:T(8,128)(2,1)S(1)} %get-tuple-element.34.h0, bf16[5,384,512]{2,1,0:T(8,128)(2,1)S(1)} %get-tuple-element.35.h1, ...), custom_call_target="tpu_custom_call" | custom-call | tf_op jit(solution)/shard_map/pallas_call | solution.py:342
  127.3 6.2 %collective-permute-start.4 = (f32[1152,128]{1,0:T(8,128)S(1)}, f32[1152,128]{1,0:T(8,128)S(1)}, u32[]{:S(2)}, u32[]{:S(2)}) collective-permute-start(f32[1152,128]{1,0:T(8,128)S(1)} %shard_map.141.own_ref), channel_id=1, source_target_pairs={{0,1},{1,0},{2,3},{3,2},{4,5},{5,4},{6,7},{7,6},{8,9},{9,8},{10,11... | collective-permute-start | bytes 1769480 | tf_op jit(solution)/shard_map/ppermute | solution.py:395
  133.5 0.6 shard_map.142
  134.2 1.0 collective-permute-done.4.other_ref
  135.1 1.5 %shard_map.143 = (f32[368,368]{1,0:T(8,128)}, f32[368,368]{1,0:T(8,128)}) custom-call(f32[1152,128]{1,0:T(8,128)S(1)} %collective-permute-done.4.other_ref, f32[368,368]{1,0:T(8,128)S(1)} %get-tuple-element.44.real_ref, f32[368,368]{1,0:T(8,128)S(1)} %get-tuple-element.45.imag_ref), custom_call_target="tpu_custom_call" | custom-call | tf_op jit(solution)/shard_map/pallas_call | solution.py:342
Async XLA Ops:
  4.9 11.1 %collective-permute-start = (bf16[552,128]{1,0:T(8,128)(2,1)}, bf16[552,128]{1,0:T(8,128)(2,1)S(1)}, u32[]{:S(2)}, u32[]{:S(2)}) collective-permute-start(bf16[552,128]{1,0:T(8,128)(2,1)} %shard_map.131.piece_ref), channel_id=1, source_target_pairs={{0,128},{1,3},{2,130},{3,1},{4,132},{5,7},{6,134},{7,5},{8,136},{9... | collective-permute-start | bytes 423944 | tf_op jit(solution)/shard_map/ppermute | solution.py:386
  13.2 0.9 copy-start.1
  56.7 6.4 %copy-start.2 = (s32[2,1,8]{2,1,0:T(1,128)S(1)}, s32[2,1,8]{2,1,0:T(1,128)}, u32[]{:S(2)}) copy-start(s32[2,1,8]{2,1,0:T(1,128)} %fidx_ref.1) | copy-start | bytes 196
  56.7 6.4 %collective-permute-start.1 = (bf16[16,552,128]{2,1,0:T(8,128)(2,1)S(1)}, bf16[16,552,128]{2,1,0:T(8,128)(2,1)S(1)}, u32[]{:S(2)}, u32[]{:S(2)}) collective-permute-start(bf16[16,552,128]{2,1,0:T(8,128)(2,1)S(1)} %bitcast.3), channel_id=1, source_target_pairs={{0,1},{1,0},{2,3},{3,2},{4,5},{5,4},{6,7},{7,6},{8,9},{9,8},{10,11... | collective-permute-start | bytes 6782984 | tf_op jit(solution)/shard_map/ppermute | solution.py:395
  63.1 9.7 %copy-start = (bf16[92,736]{1,0:T(8,128)(2,1)S(1)}, bf16[92,736]{1,0:T(8,128)(2,1)}, u32[]{:S(2)}) copy-start(bf16[92,736]{1,0:T(8,128)(2,1)} %dens_ref.1) | copy-start | bytes 406276
  63.1 9.7 %copy-start.4 = (s32[2,1,8]{2,1,0:T(1,128)S(1)}, s32[2,1,8]{2,1,0:T(1,128)}, u32[]{:S(2)}) copy-start(s32[2,1,8]{2,1,0:T(1,128)} %didx_ref.1) | copy-start | bytes 196
  67.3 9.5 %collective-permute-start.2 = (bf16[48,768]{1,0:T(8,128)(2,1)S(1)}, bf16[48,768]{1,0:T(8,128)(2,1)S(1)}, u32[]{:S(2)}, u32[]{:S(2)}) collective-permute-start(bf16[48,768]{1,0:T(8,128)(2,1)S(1)} %get-tuple-element.38.piece_ref), channel_id=1, source_target_pairs={{0,64},{1,65},{2,66},{3,67},{4,68},{5,69},{6,70},{7,71},{8,72},{9,... | collective-permute-start | bytes 221192 | tf_op jit(solution)/shard_map/ppermute | solution.py:386
  76.8 20.3 %copy-start.3 = (s32[2,1,8]{2,1,0:T(1,128)S(1)}, s32[2,1,8]{2,1,0:T(1,128)}, u32[]{:S(2)}) copy-start(s32[2,1,8]{2,1,0:T(1,128)} %index_ref.6) | copy-start | bytes 196
  100.8 6.0 %collective-permute-start.3 = (bf16[48,768]{1,0:T(8,128)(2,1)S(1)}, bf16[48,768]{1,0:T(8,128)(2,1)S(1)}, u32[]{:S(2)}, u32[]{:S(2)}) collective-permute-start(bf16[48,768]{1,0:T(8,128)(2,1)S(1)} %get-tuple-element.41.piece_ref), channel_id=1, source_target_pairs={{0,64},{1,65},{2,66},{3,67},{4,68},{5,69},{6,70},{7,71},{8,72},{9,... | collective-permute-start | bytes 221192 | tf_op jit(solution)/shard_map/ppermute | solution.py:386
  104.3 19.4 %copy-start.5 = (s32[2,1,8]{2,1,0:T(1,128)S(1)}, s32[2,1,8]{2,1,0:T(1,128)}, u32[]{:S(2)}) copy-start(s32[2,1,8]{2,1,0:T(1,128)} %index_ref.7) | copy-start | bytes 196
  127.3 7.8 %collective-permute-start.4 = (f32[1152,128]{1,0:T(8,128)S(1)}, f32[1152,128]{1,0:T(8,128)S(1)}, u32[]{:S(2)}, u32[]{:S(2)}) collective-permute-start(f32[1152,128]{1,0:T(8,128)S(1)} %shard_map.141.own_ref), channel_id=1, source_target_pairs={{0,1},{1,0},{2,3},{3,2},{4,5},{5,4},{6,7},{7,6},{8,9},{9,8},{10,11... | collective-permute-start | bytes 1769480 | tf_op jit(solution)/shard_map/ppermute | solution.py:395
